TPU v7x, 256 devices: a whole 4x4x8 slice. The times are simulated.
256 devices in a mesh: dp: 8 (over z), tok: 2 (over core), expert: 16 (over y, x).
Axes of the slice: x: 4, y: 4, z: 8, core: 2. Of those that a mesh axis runs over, the one named last changes fastest.
Arguments:
- tokens: bfloat16 [256, 256, 1280], P(('dp', 'tok', 'expert')), may hold values from -6 to 6
- router: bfloat16 [1280, 32], replicated, may hold values from -13.975425 to 13.975425
- expert_in: bfloat16 [32, 1280, 5120], P(('tok', 'expert'), None, 'dp'), may hold values from -0.15625 to 0.15625
- expert_out: bfloat16 [32, 5120, 1280], P(('tok', 'expert'), 'dp'), may hold values from -0.078125 to 0.078125
- grad_out: bfloat16 [256, 256, 1280], P(('dp', 'tok', 'expert')), may hold values from -6 to 6
Outputs:
- grad_tokens: bfloat16 [256, 256, 1280], P(('dp', 'tok', 'expert'))
- grad_router: float32 [1280, 32], replicated
- grad_expert_in: bfloat16 [32, 1280, 5120], P(('tok', 'expert'), None, 'dp')
- grad_expert_out: bfloat16 [32, 5120, 1280], P(('tok', 'expert'), 'dp')
All inputs are finite; a program needn't handle non-finite values.
Results may differ from a plain program's by a relative error of at most 0.0085.
Values may be sent and summed in bfloat16 or wider, within the bound.
No kernel may reach another device: no remote copies, remote signals or barrier semaphores. Data moves between devices by JAX's collectives and lax.ppermute only.
A program may use at most 64 MiB of HBM per device.

v0:
```python
import jax
import jax.numpy as jnp
from jax import lax
from jax.sharding import PartitionSpec as P

ITERS = 4


GELU_SCALE = 0.7978845608028654
GELU_CUBIC = 0.044715


def gelu_pair(hidden_pre):
    inner_arg = GELU_SCALE * (hidden_pre + GELU_CUBIC * hidden_pre * hidden_pre * hidden_pre)
    tanh_val = jnp.tanh(inner_arg)
    activated = 0.5 * hidden_pre * (1.0 + tanh_val)
    derivative = 0.5 * (1.0 + tanh_val) + 0.5 * hidden_pre * (
        1.0 - tanh_val * tanh_val
    ) * GELU_SCALE * (1.0 + 3.0 * GELU_CUBIC * hidden_pre * hidden_pre)
    return (activated, derivative)


def forward_iterates(router_scores):
    iterate = router_scores
    stored_residuals = []
    for sweep_index in range(ITERS):
        line_divisor_factor = iterate - jax.nn.logsumexp(iterate, axis=2, keepdims=True)
        column_divisor = line_divisor_factor - jax.nn.logsumexp(
            line_divisor_factor, axis=1, keepdims=True
        )
        stored_residuals.append((line_divisor_factor, column_divisor))
        iterate = column_divisor
    return stored_residuals


def backward_sequence(gradient, stored_residuals):
    for line_divisor_factor, column_divisor in reversed(stored_residuals):
        gradient = gradient - jnp.exp(column_divisor) * jnp.sum(gradient, axis=1, keepdims=True)
        gradient = gradient - jnp.exp(line_divisor_factor) * jnp.sum(
            gradient, axis=2, keepdims=True
        )
    return gradient


def body(tokens, router, expert_in, expert_out, grad_out):
    images, seq_len, model_width = tokens.shape
    tok_count = lax.axis_size("tok")
    expert_count = lax.axis_size("expert")
    owners = tok_count * expert_count
    router_scores = jnp.einsum("btd,ds->bts", tokens, router, preferred_element_type=jnp.float32)
    combine = jax.nn.softmax(router_scores, axis=2)
    combine_rounded = combine.astype(jnp.bfloat16)
    stored_residuals = forward_iterates(router_scores)
    assignment_matrix = jnp.exp(stored_residuals[-1][1])
    dispatch_rounded = assignment_matrix.astype(jnp.bfloat16)
    slot_part = jnp.einsum(
        "bts,btd->sbd", dispatch_rounded, tokens, preferred_element_type=jnp.float32
    ).astype(jnp.bfloat16)
    grad_part = jnp.einsum(
        "bts,btd->sbd", combine_rounded, grad_out, preferred_element_type=jnp.float32
    ).astype(jnp.bfloat16)
    moved_in, moved_grad = (
        lax.all_to_all(slot_part, ("tok", "expert"), split_axis=0, concat_axis=0, tiled=True),
        lax.all_to_all(grad_part, ("tok", "expert"), split_axis=0, concat_axis=0, tiled=True),
    )
    rows_in = moved_in.reshape(owners * images, model_width)
    rows_grad = moved_grad.reshape(owners * images, model_width)
    all_in, all_grad = (
        lax.all_gather(rows_in, "dp", axis=0, tiled=True),
        lax.all_gather(rows_grad, "dp", axis=0, tiled=True),
    )
    weight_in = expert_in[0]
    weight_out = expert_out[0]
    hidden_pre = jnp.dot(all_in, weight_in, preferred_element_type=jnp.float32)
    activated, derivative = gelu_pair(hidden_pre)
    hidden_act = activated.astype(jnp.bfloat16)
    grad_act = lax.dot_general(
        all_grad, weight_out, (((1,), (1,)), ((), ())), preferred_element_type=jnp.float32
    )
    grad_pre = (grad_act * derivative).astype(jnp.bfloat16)
    grad_win = lax.dot_general(
        all_in, grad_pre, (((0,), (0,)), ((), ())), preferred_element_type=jnp.float32
    ).astype(jnp.bfloat16)[None]
    out_weight_gradient = lax.dot_general(
        hidden_act, all_grad, (((0,), (0,)), ((), ())), preferred_element_type=jnp.float32
    ).astype(jnp.bfloat16)[None]
    forward_rows = jnp.dot(hidden_act, weight_out, preferred_element_type=jnp.float32)
    backward_rows = lax.dot_general(
        grad_pre, weight_in, (((1,), (1,)), ((), ())), preferred_element_type=jnp.float32
    )
    summed = lax.psum_scatter(
        jnp.concatenate([forward_rows, backward_rows], axis=1),
        "dp",
        scatter_dimension=0,
        tiled=True,
    )
    slot_out = summed[:, :model_width].astype(jnp.bfloat16)
    bucket_cotangent = summed[:, model_width:].astype(jnp.bfloat16)
    back_out, back_grad = (
        lax.all_to_all(
            slot_out.reshape(owners, images, model_width),
            ("tok", "expert"),
            split_axis=0,
            concat_axis=0,
            tiled=True,
        ),
        lax.all_to_all(
            bucket_cotangent.reshape(owners, images, model_width),
            ("tok", "expert"),
            split_axis=0,
            concat_axis=0,
            tiled=True,
        ),
    )
    grad_comb = jnp.einsum("btd,sbd->bts", grad_out, back_out, preferred_element_type=jnp.float32)
    logit_cotangent = combine * (grad_comb - jnp.sum(combine * grad_comb, axis=2, keepdims=True))
    doubly_stochastic_adjoint = (
        jnp.einsum("btd,sbd->bts", tokens, back_grad, preferred_element_type=jnp.float32)
        * assignment_matrix
    )
    doubly_stochastic_adjoint = backward_sequence(doubly_stochastic_adjoint, stored_residuals)
    accumulated_cotangent = (logit_cotangent + doubly_stochastic_adjoint).astype(jnp.bfloat16)
    grad_tokens = (
        jnp.einsum("bts,sbd->btd", dispatch_rounded, back_grad, preferred_element_type=jnp.float32)
        + jnp.einsum(
            "bts,ds->btd", accumulated_cotangent, router, preferred_element_type=jnp.float32
        )
    ).astype(jnp.bfloat16)
    router_part = jnp.einsum(
        "btd,bts->ds", tokens, accumulated_cotangent, preferred_element_type=jnp.float32
    )
    grad_router = lax.psum(router_part, ("dp", "tok", "expert"))
    return (grad_tokens, grad_router, grad_win, out_weight_gradient)


def solution(mesh):
    return jax.shard_map(
        body,
        mesh=mesh,
        in_specs=(
            P(("dp", "tok", "expert"), None, None),
            P(),
            P(("tok", "expert"), None, "dp"),
            P(("tok", "expert"), "dp", None),
            P(("dp", "tok", "expert"), None, None),
        ),
        out_specs=(
            P(("dp", "tok", "expert"), None, None),
            P(),
            P(("tok", "expert"), None, "dp"),
            P(("tok", "expert"), "dp", None),
        ),
        check_vma=False,
    )
```

profile of v0, /device:TPU:1, one launch (start us, length us, event | category | flops | bytes accessed | tf_op | source)
XLA Modules:
  0.0 423.9 jit_solution(1599589056745215849)
XLA Ops:
  7.2 1.6 fusion.61
  8.8 0.1 subtract_reduce_fusion.3
  9.0 0.2 exponential_reduce_fusion.6
  9.2 0.1 fusion.56
  9.3 0.1 fusion.45
  9.4 0.2 subtract_reduce_fusion.2
  9.6 0.2 exponential_reduce_fusion.4
  9.8 0.1 fusion.60
  9.9 0.1 subtract_reduce_fusion.1
  10.1 0.2 exponential_reduce_fusion.2
  10.3 0.1 fusion.57
  10.4 0.1 exponential_reduce_fusion.1
  10.5 0.2 subtract_reduce_fusion
  10.7 0.2 exponential_reduce_fusion
  10.9 1.4 fusion.4
  12.3 0.5 broadcast.187
  12.8 0.6 reduce.52
  13.5 0.7 reshape.437
  14.1 8.6 %all-to-all-start = ((bf16[32,2,640]{2,1,0:T(2,128)(2,1)}), bf16[32,2,640]{2,1,0:T(2,128)(2,1)}, u32[]{:S(2)}, u32[]{:S(2)}) async-start(bf16[32,2,640]{2,1,0:T(2,128)(2,1)} %reshape.437), calls=%async_computation | async-start | bytes 163840 | tf_op jit(solution)/shard_map/all_to_all | solution.py:63
  22.8 0.2 fusion.5
  23.0 0.8 reduce.53
  23.8 0.7 reshape.439
  24.4 5.5 %all-to-all-done = bf16[32,2,640]{2,1,0:T(2,128)(2,1)} async-done(((bf16[32,2,640]{2,1,0:T(2,128)(2,1)}), bf16[32,2,640]{2,1,0:T(2,128)(2,1)}, u32[]{:S(2)}, u32[]{:S(2)}) %all-to-all-start) | async-done | bytes 81952 | tf_op jit(solution)/shard_map/all_to_all | solution.py:63
  30.0 4.8 %all-to-all-start.1 = ((bf16[32,2,640]{2,1,0:T(2,128)(2,1)}), bf16[32,2,640]{2,1,0:T(2,128)(2,1)}, u32[]{:S(2)}, u32[]{:S(2)}) async-start(bf16[32,2,640]{2,1,0:T(2,128)(2,1)} %reshape.439), calls=%async_computation.1 | async-start | bytes 163840 | tf_op jit(solution)/shard_map/all_to_all | solution.py:64
  34.8 0.0 reduce-scatter.2.cloned.1.call-start
  34.9 1.0 reshape.438
  35.8 25.4 %all-gather = bf16[256,1,1280]{2,0,1:T(8,128)(2,1)} all-gather(bf16[32,1,1280]{2,0,1:T(8,128)(2,1)S(1)} %copy.14), channel_id=2, replica_groups=mesh['dp'=8,'tok'=2,'expert'=16] {'dp'}, dimensions={0}, use_global_device_ids=true | all-gather | bytes 737280 | tf_op jit(solution)/shard_map/all_gather | solution.py:69
  61.2 1.0 reshape.440
  62.2 20.4 %all-gather.1 = bf16[256,1,1280]{2,0,1:T(8,128)(2,1)S(1)} all-gather(bf16[32,1,1280]{2,0,1:T(8,128)(2,1)S(1)} %copy.16), channel_id=3, replica_groups=mesh['dp'=8,'tok'=2,'expert'=16] {'dp'}, dimensions={0}, use_global_device_ids=true | all-gather | bytes 737280 | tf_op jit(solution)/shard_map/all_gather | solution.py:70
  82.6 2.0 fusion.12
  84.6 0.8 fusion.8
  85.4 0.8 fusion.17
  86.3 0.7 copy-done.9
  87.0 0.7 fusion.10
  87.7 1.8 pad_maximum_fusion
  89.5 1.1 copy-done.5
  90.6 3.1 fusion.1
  93.7 46.2 %reduce-scatter.2.cloned.1.call-done = f32[32,2560]{1,0:T(8,128)} async-done(((f32[256,2560]{1,0:T(8,128)}), f32[32,2560]{1,0:T(8,128)}) %reduce-scatter.2.cloned.1.call-update) | async-done | bytes 327696 | tf_op jit(solution)/shard_map/reduce_scatter | solution.py:91
  139.9 1.0 convert.4
  140.9 0.6 reduce.54
  141.5 0.7 reshape.441
  142.2 11.6 %all-to-all-start.2 = ((bf16[32,2,640]{2,1,0:T(2,128)(2,1)}), bf16[32,2,640]{2,1,0:T(2,128)(2,1)S(1)}, u32[]{:S(2)}, u32[]{:S(2)}) async-start(bf16[32,2,640]{2,1,0:T(2,128)(2,1)} %reshape.441), calls=%async_computation.3 | async-start | bytes 163840 | tf_op jit(solution)/shard_map/all_to_all | solution.py:107
  153.8 1.9 fusion
  155.7 0.6 reduce.55
  156.3 0.7 reshape.443
  157.0 3.9 all-to-all-done.2
  160.9 4.2 all-to-all-start.3
  165.1 0.1 reshape.442
  165.2 0.4 fusion.62
  165.7 1.5 fusion.40
  167.2 0.1 fusion.55
  167.3 0.2 fusion.46
  167.5 0.1 fusion.59
  167.6 0.1 fusion.47
  167.7 0.1 fusion.58
  167.8 0.2 fusion.48
  168.0 4.2 all-to-all-done.3
  172.2 0.1 reshape.444
  172.3 0.4 multiply_reduce_fusion
  172.7 0.1 add_convert_fusion
  172.8 0.9 convolution_bitcast_fusion
  173.7 2.5 fusion.3
  176.2 239.2 %all-reduce.2.cloned.1.call-done = f32[1280,32]{0,1:T(8,128)} async-done(((f32[1280,32]{0,1:T(8,128)}), f32[1280,32]{0,1:T(8,128)}) %all-reduce.2.cloned.1.call-update) | async-done | bytes 163856 | tf_op jit(solution)/shard_map/psum | solution.py:132
  415.4 1.6 copy.42
  (47 shorter events, 0.4 us)
Async XLA Ops:
  7.2 77.4 %copy-start = (bf16[1,640,1280]{2,1,0:T(8,128)(2,1)S(1)}, bf16[1,640,1280]{2,1,0:T(8,128)(2,1)}, u32[]{:S(2)}) copy-start(bf16[1,640,1280]{2,1,0:T(8,128)(2,1)} %param.8) | copy-start | bytes 4915204
  7.2 15.6 %copy-start.6 = (bf16[1,256,1280]{2,1,0:T(8,128)(2,1)S(1)}, bf16[1,256,1280]{2,1,0:T(8,128)(2,1)}, u32[]{:S(2)}) copy-start(bf16[1,256,1280]{2,1,0:T(8,128)(2,1)} %param.9) | copy-start | bytes 1966084
  14.1 15.9 %all-to-all-start = ((bf16[32,2,640]{2,1,0:T(2,128)(2,1)}), bf16[32,2,640]{2,1,0:T(2,128)(2,1)}, u32[]{:S(2)}, u32[]{:S(2)}) async-start(bf16[32,2,640]{2,1,0:T(2,128)(2,1)} %reshape.437), calls=%async_computation | async-start | bytes 163840 | tf_op jit(solution)/shard_map/all_to_all | solution.py:63
  23.0 59.6 %copy-start.2 = (bf16[1,1280,640]{2,1,0:T(8,128)(2,1)S(1)}, bf16[1,1280,640]{2,1,0:T(8,128)(2,1)}, u32[]{:S(2)}) copy-start(bf16[1,1280,640]{2,1,0:T(8,128)(2,1)} %param.7) | copy-start | bytes 4915204
  30.0 31.2 %all-to-all-start.1 = ((bf16[32,2,640]{2,1,0:T(2,128)(2,1)}), bf16[32,2,640]{2,1,0:T(2,128)(2,1)}, u32[]{:S(2)}, u32[]{:S(2)}) async-start(bf16[32,2,640]{2,1,0:T(2,128)(2,1)} %reshape.439), calls=%async_computation.1 | async-start | bytes 163840 | tf_op jit(solution)/shard_map/all_to_all | solution.py:64
  34.8 105.0 %reduce-scatter.2.cloned.1.call-start = ((), (), s32[]{:S(2)}) async-start(), calls=%async_computation.5 | async-start | bytes 2949120 | tf_op jit(solution)/shard_map/reduce_scatter | solution.py:91
  82.6 2.8 copy-start.8
  84.6 0.8 copy-start.4
  86.3 0.7 copy-start.9
  89.5 1.1 copy-start.5
  90.6 63.2 %copy-start.3 = (bf16[256,1,1280]{2,0,1:T(8,128)(2,1)S(1)}, bf16[256,1,1280]{2,0,1:T(8,128)(2,1)}, u32[]{:S(2)}) copy-start(bf16[256,1,1280]{2,0,1:T(8,128)(2,1)} %all-gather) | copy-start | bytes 1966084
  90.6 63.2 %copy-start.10 = (bf16[256,640]{1,0:T(8,128)(2,1)S(1)}, bf16[256,640]{1,0:T(8,128)(2,1)}, u32[]{:S(2)}) copy-start(bf16[256,640]{1,0:T(8,128)(2,1)} %copy-done.9) | copy-start | bytes 983044
  142.2 18.7 %all-to-all-start.2 = ((bf16[32,2,640]{2,1,0:T(2,128)(2,1)}), bf16[32,2,640]{2,1,0:T(2,128)(2,1)S(1)}, u32[]{:S(2)}, u32[]{:S(2)}) async-start(bf16[32,2,640]{2,1,0:T(2,128)(2,1)} %reshape.441), calls=%async_computation.3 | async-start | bytes 163840 | tf_op jit(solution)/shard_map/all_to_all | solution.py:107
  153.8 11.5 %copy-start.1 = (bf16[1,256,1280]{2,1,0:T(8,128)(2,1)S(1)}, bf16[1,256,1280]{2,1,0:T(8,128)(2,1)}, u32[]{:S(2)}) copy-start(bf16[1,256,1280]{2,1,0:T(8,128)(2,1)} %param.5) | copy-start | bytes 1966084
  160.9 11.3 %all-to-all-start.3 = ((bf16[32,2,640]{2,1,0:T(2,128)(2,1)}), bf16[32,2,640]{2,1,0:T(2,128)(2,1)S(1)}, u32[]{:S(2)}, u32[]{:S(2)}) async-start(bf16[32,2,640]{2,1,0:T(2,128)(2,1)} %reshape.443), calls=%async_computation.4 | async-start | bytes 163840 | tf_op jit(solution)/shard_map/all_to_all | solution.py:100
  165.1 7.2 %copy-start.7 = (bf16[1,256,1280]{2,1,0:T(8,128)(2,1)S(1)}, bf16[1,256,1280]{2,1,0:T(8,128)(2,1)}, u32[]{:S(2)}) copy-start(bf16[1,256,1280]{2,1,0:T(8,128)(2,1)} %param.9) | copy-start | bytes 1966084
  165.1 250.3 %all-reduce.2.cloned.1.call-start = ((), (), s32[]{:S(2)}) async-start(), calls=%async_computation.6 | async-start | bytes 327680 | tf_op jit(solution)/shard_map/psum | solution.py:132
  167.2 6.5 %copy-start.11 = (bf16[1280,32]{0,1:T(8,128)(2,1)S(1)}, bf16[1280,32]{0,1:T(8,128)(2,1)}, u32[]{:S(2)}) copy-start(bf16[1280,32]{0,1:T(8,128)(2,1)} %param.6) | copy-start | bytes 245764
Sparse Core Ops, SparseCore 0:
  89.6 50.1 reduce-scatter.1
  173.8 241.5 all-reduce.1
where the time goes:
time: 425 us; the launch traced here: 424 us
  waiting for transfers between devices  299 us (70%)
  blocking collectives  45.8 us (11%)
  starting transfers between devices  29.3 us (7%)
  matrix products  18.2 us (4%)
  between operations  14.4 us (3%)
  local copies, waits for them, and re-layouts  8.71 us (2%)
  other arithmetic  8.41 us (2%)
    psum x1, waiting for transfers between devices, body(): grad_router = lax.psum(router_part, ('dp', 'tok', 'expert'))  239 us
    reduce_scatter x1, waiting for transfers between devices, body(): lax.psum_scatter(jnp.concatenate([forward_rows, backward_rows], axis=1),...  46.2 us
    all_gather x1, blocking collectives, body(): lax.all_gather(rows_in, 'dp', axis=0, tiled=True)  25.4 us
    all_gather x1, blocking collectives, body(): lax.all_gather(rows_grad, 'dp', axis=0, tiled=True)  20.4 us
    all_to_all x1, starting transfers between devices, body(): lax.all_to_all(bucket_cotangent.reshape(owners, images, model_width), ('t...  11.6 us
    all_to_all x1, starting transfers between devices, body(): lax.all_to_all(slot_part, ('tok', 'expert'), split_axis=0, concat_axis=0,...  8.64 us
  transfers between devices with their start and end apart: 6, of which 5 were waited for; matrix products, arithmetic and copies ran while one was open for 3% of the time, Pallas kernels for 0%

commit v1 on v0

v1 whole, which is shorter than its diff:
```python
import jax
import jax.numpy as jnp
from jax import lax
from jax.sharding import PartitionSpec as P

ITERS = 4


GELU_SCALE = 0.7978845608028654
GELU_CUBIC = 0.044715


def gelu_pair(hidden_pre):
    inner_arg = GELU_SCALE * (hidden_pre + GELU_CUBIC * hidden_pre * hidden_pre * hidden_pre)
    tanh_val = jnp.tanh(inner_arg)
    activated = 0.5 * hidden_pre * (1.0 + tanh_val)
    derivative = 0.5 * (1.0 + tanh_val) + 0.5 * hidden_pre * (
        1.0 - tanh_val * tanh_val
    ) * GELU_SCALE * (1.0 + 3.0 * GELU_CUBIC * hidden_pre * hidden_pre)
    return (activated, derivative)


def forward_iterates(router_scores):
    iterate = router_scores
    stored_residuals = []
    for sweep_index in range(ITERS):
        line_divisor_factor = iterate - jax.nn.logsumexp(iterate, axis=1, keepdims=True)
        column_divisor = line_divisor_factor - jax.nn.logsumexp(
            line_divisor_factor, axis=0, keepdims=True
        )
        stored_residuals.append((line_divisor_factor, column_divisor))
        iterate = column_divisor
    return stored_residuals


def backward_sequence(gradient, stored_residuals):
    for line_divisor_factor, column_divisor in reversed(stored_residuals):
        gradient = gradient - jnp.exp(column_divisor) * jnp.sum(gradient, axis=0, keepdims=True)
        gradient = gradient - jnp.exp(line_divisor_factor) * jnp.sum(
            gradient, axis=1, keepdims=True
        )
    return gradient


def shift(value, step):
    size = lax.axis_size("dp")
    return lax.ppermute(value, "dp", [(i, (i + step) % size) for i in range(size)])


def ring_gather(rows):
    half = rows.shape[1] // 2
    blocks = [rows]
    behind = ahead = rows
    for _ in range(3):
        behind, ahead = shift(behind, 1), shift(ahead, -1)
        blocks += [behind, ahead]
    far = jnp.concatenate([shift(behind[:, :half], 1), shift(ahead[:, half:], -1)], axis=1)
    return jnp.concatenate(blocks + [far], axis=0)


def ring_reduce(partial, rows):
    half = partial.shape[1] // 2
    block = [partial[i * rows : (i + 1) * rows] for i in range(8)]
    own, far = block[0], block[7]
    down_path, up_path = [block[5], block[3], block[1]], [block[6], block[4], block[2]]
    narrow = jnp.bfloat16
    wide = jnp.float32
    from_above = shift(far[:, :half].astype(narrow), -1).astype(wide)
    from_below = shift(far[:, half:].astype(narrow), 1).astype(wide)
    down = jnp.concatenate([from_above + down_path[0][:, :half], down_path[0][:, half:]], axis=1)
    up = jnp.concatenate([up_path[0][:, :half], from_below + up_path[0][:, half:]], axis=1)
    for step in range(3):
        down = shift(down.astype(narrow), -1).astype(wide)
        up = shift(up.astype(narrow), 1).astype(wide)
        if step < 2:
            down, up = down + down_path[step + 1], up + up_path[step + 1]
    return own + down + up


def swap(value):
    return lax.all_to_all(value, ("tok", "expert"), split_axis=0, concat_axis=0, tiled=True)


def sum_everywhere(part):
    slots = part.shape[0]
    mine = jnp.sum(swap(part), axis=0, keepdims=True)
    seen = [mine] + [shift(mine, step) for step in range(1, 8)]
    while len(seen) > 1:
        middle = len(seen) // 2
        seen = [seen[i] + seen[i + middle] for i in range(middle)]
    return swap(jnp.broadcast_to(seen[0], (slots, part.shape[1])))


def body(tokens, router, expert_in, expert_out, grad_out):
    patches, image_grad = tokens[0], grad_out[0]
    model_width = patches.shape[1]
    router_scores = jnp.dot(patches, router, preferred_element_type=jnp.float32)
    combine = jax.nn.softmax(router_scores, axis=1)
    combine_rounded = combine.astype(jnp.bfloat16)
    stored_residuals = forward_iterates(router_scores)
    assignment_matrix = jnp.exp(stored_residuals[-1][1])
    dispatch_rounded = assignment_matrix.astype(jnp.bfloat16)
    slot_part = jnp.dot(dispatch_rounded.T, patches, preferred_element_type=jnp.float32).astype(
        jnp.bfloat16
    )
    grad_part = jnp.dot(combine_rounded.T, image_grad, preferred_element_type=jnp.float32).astype(
        jnp.bfloat16
    )
    rows = swap(jnp.concatenate([slot_part, grad_part], axis=1))
    gathered = ring_gather(rows)
    all_in, all_grad = gathered[:, :model_width], gathered[:, model_width:]
    weight_in = expert_in[0]
    weight_out = expert_out[0]
    hidden_pre = jnp.dot(all_in, weight_in, preferred_element_type=jnp.float32)
    activated, derivative = gelu_pair(hidden_pre)
    hidden_act = activated.astype(jnp.bfloat16)
    grad_act = lax.dot_general(
        all_grad, weight_out, (((1,), (1,)), ((), ())), preferred_element_type=jnp.float32
    )
    grad_pre = (grad_act * derivative).astype(jnp.bfloat16)
    forward_rows = jnp.dot(hidden_act, weight_out, preferred_element_type=jnp.float32)
    backward_rows = lax.dot_general(
        grad_pre, weight_in, (((1,), (1,)), ((), ())), preferred_element_type=jnp.float32
    )
    summed = ring_reduce(
        jnp.concatenate([forward_rows, backward_rows], axis=1), rows.shape[0]
    ).astype(jnp.bfloat16)
    grad_win = lax.dot_general(
        all_in, grad_pre, (((0,), (0,)), ((), ())), preferred_element_type=jnp.float32
    ).astype(jnp.bfloat16)[None]
    out_weight_gradient = lax.dot_general(
        hidden_act, all_grad, (((0,), (0,)), ((), ())), preferred_element_type=jnp.float32
    ).astype(jnp.bfloat16)[None]
    back = swap(summed)
    back_out, back_grad = back[:, :model_width], back[:, model_width:]
    grad_comb = lax.dot_general(
        image_grad, back_out, (((1,), (1,)), ((), ())), preferred_element_type=jnp.float32
    )
    logit_cotangent = combine * (grad_comb - jnp.sum(combine * grad_comb, axis=1, keepdims=True))
    doubly_stochastic_adjoint = (
        lax.dot_general(
            patches, back_grad, (((1,), (1,)), ((), ())), preferred_element_type=jnp.float32
        )
        * assignment_matrix
    )
    doubly_stochastic_adjoint = backward_sequence(doubly_stochastic_adjoint, stored_residuals)
    accumulated_cotangent = (logit_cotangent + doubly_stochastic_adjoint).astype(jnp.bfloat16)
    router_part = lax.dot_general(
        accumulated_cotangent, patches, (((0,), (0,)), ((), ())), preferred_element_type=jnp.float32
    )
    grad_router = sum_everywhere(router_part).T
    grad_tokens = (
        jnp.dot(dispatch_rounded, back_grad, preferred_element_type=jnp.float32)
        + lax.dot_general(
            accumulated_cotangent, router, (((1,), (1,)), ((), ())), preferred_element_type=jnp.float32
        )
    ).astype(jnp.bfloat16)[None]
    return (grad_tokens, grad_router, grad_win, out_weight_gradient)


def solution(mesh):
    return jax.shard_map(
        body,
        mesh=mesh,
        in_specs=(
            P(("dp", "tok", "expert"), None, None),
            P(),
            P(("tok", "expert"), None, "dp"),
            P(("tok", "expert"), "dp", None),
            P(("dp", "tok", "expert"), None, None),
        ),
        out_specs=(
            P(("dp", "tok", "expert"), None, None),
            P(),
            P(("tok", "expert"), None, "dp"),
            P(("tok", "expert"), "dp", None),
        ),
        check_vma=False,
    )
```

time: 425 us -> 154 us (0.36)
  waiting for transfers between devices: 299 us -> 41.7 us
  starting transfers between devices: 29.3 us -> 48 us
  between operations: 14.4 us -> 1.11 us
  blocking collectives: 45.8 us -> 38 us
  local copies, waits for them, and re-layouts: 8.71 us -> 3.7 us
    psum x1 -> x0, waiting for transfers between devices: 239 us -> none  [body(): grad_router = lax.psum(router_part, ('dp', 'tok', 'expert'))]
    reduce_scatter x1 -> x0, waiting for transfers between devices: 46.2 us -> none  [body(): lax.psum_scatter(jnp.concatenate([forward_rows, backward_rows], axis=1),...]
    all_gather x2 -> x0, blocking collectives: 45.8 us -> none  [the longest x1 25.4 us: body(): lax.all_gather(rows_in, 'dp', axis=0, tiled=True)]
    all_to_all x0 -> x2, blocking collectives: none -> 38 us  [swap(): lax.all_to_all(value, ('tok', 'expert'), split_axis=0, concat_axis=0, til...]
    ppermute x0 -> x23, starting transfers between devices: none -> 36.8 us  [shift(): lax.ppermute(value, 'dp', [(i, (i + step) % size) for i in range(size)])]
    ppermute x0 -> x23, waiting for transfers between devices: none -> 31.9 us  [shift(): lax.ppermute(value, 'dp', [(i, (i + step) % size) for i in range(size)])]
    all_to_all x4 -> x2, starting transfers between devices: 29.2 us -> 11.2 us  [swap(): lax.all_to_all(value, ('tok', 'expert'), split_axis=0, concat_axis=0, til...]
    unnamed x33 -> x31, local copies, waits for them, and re-layouts: 8.12 us -> 1.55 us
  transfers between devices with their start and end apart: 6 -> 25, of which waited for: 5 -> 14; matrix products, arithmetic and copies ran while one was open for 3% -> 7% of each run, Pallas kernels for 0% -> 0%
where the time goes in v1:
time: 154 us
  starting transfers between devices  48 us (31%)
  waiting for transfers between devices  41.7 us (27%)
  blocking collectives  38 us (25%)
  matrix products  16.3 us (11%)
  other arithmetic  4.75 us (3%)
  local copies, waits for them, and re-layouts  3.7 us (2%)
    all_to_all x2, blocking collectives, swap(): lax.all_to_all(value, ('tok', 'expert'), split_axis=0, concat_axis=0, til...  38 us
    ppermute x23, starting transfers between devices, shift(): lax.ppermute(value, 'dp', [(i, (i + step) % size) for i in range(size)])  36.8 us
    ppermute x23, waiting for transfers between devices, shift(): lax.ppermute(value, 'dp', [(i, (i + step) % size) for i in range(size)])  31.9 us
    all_to_all x2, starting transfers between devices, swap(): lax.all_to_all(value, ('tok', 'expert'), split_axis=0, concat_axis=0, til...  11.2 us
    all_to_all x2, waiting for transfers between devices, swap(): lax.all_to_all(value, ('tok', 'expert'), split_axis=0, concat_axis=0, til...  9.84 us
    dot_general x1, matrix products, body(): lax.dot_general(hidden_act, all_grad, (((0,), (0,)), ((), ())), preferred...  3.24 us
  transfers between devices with their start and end apart: 25, of which 14 were waited for; matrix products, arithmetic and copies ran while one was open for 7% of the time, Pallas kernels for 0%

profile of v1, /device:TPU:1, one launch (start us, length us, event | category | flops | bytes accessed | tf_op | source)
XLA Modules:
  0.0 153.6 jit_solution(7148602931655643007)
XLA Ops:
  0.7 1.6 %fusion.68 = (f32[256]{0:T(256)S(1)}, f32[256,32]{0,1:T(8,128)S(1)}) fusion(bf16[1280,32]{0,1:T(8,128)(2,1)} %param.6, bf16[1,256,1280]{2,1,0:T(8,128)(2,1)} %param.5), kind=kOutput, calls=%fused_computation.136 | convolution fusion | flops 20979456 | bytes 771072 | tf_op jit(solution)/shard_map/dot_general | solution.py:97
  2.4 0.2 exponential_reduce_fusion.6
  2.9 0.2 subtract_reduce_fusion.2
  3.1 0.2 exponential_reduce_fusion.4
  3.5 0.2 exponential_reduce_fusion.2
  4.0 0.2 subtract_reduce_fusion
  4.2 0.2 exponential_reduce_fusion
  4.4 0.3 convolution_convert_fusion.3
  4.7 0.2 convolution_convert_fusion.2
  4.9 0.5 broadcast.144
  5.4 0.7 reduce.3
  6.2 16.2 %all_to_all.42 = bf16[32,2,1280]{2,1,0:T(2,128)(2,1)S(1)} all-to-all(bf16[32,2,1280]{2,1,0:T(2,128)(2,1)S(1)} %reshape.160), channel_id=1, replica_groups=mesh['dp'=8,'tok'=2,'expert'=16] {'tok','expert'}, dimensions={0} | all-to-all | bytes 327680 | tf_op jit(solution)/shard_map/all_to_all | solution.py:81
  22.5 1.7 %collective-permute-start = (bf16[32,2560]{1,0:T(8,128)(2,1)S(1)}, bf16[32,2560]{1,0:T(8,128)(2,1)S(1)}, u32[]{:S(2)}, u32[]{:S(2)}) collective-permute-start(bf16[32,2560]{1,0:T(8,128)(2,1)S(1)} %get-tuple-element.13), channel_id=1, source_target_pairs={{0,32},{32,64},{64,96},{96,128},{128,160},{160,192},{192,224},{224... | collective-permute-start | bytes 491528 | tf_op jit(solution)/shard_map/ppermute | solution.py:47
  24.3 4.0 %collective-permute-start.1 = (bf16[32,2560]{1,0:T(8,128)(2,1)S(1)}, bf16[32,2560]{1,0:T(8,128)(2,1)S(1)}, u32[]{:S(2)}, u32[]{:S(2)}) collective-permute-start(bf16[32,2560]{1,0:T(8,128)(2,1)S(1)} %get-tuple-element.13), channel_id=1, source_target_pairs={{0,224},{32,0},{64,32},{96,64},{128,96},{160,128},{192,160},{224,1... | collective-permute-start | bytes 491528 | tf_op jit(solution)/shard_map/ppermute | solution.py:47
  28.3 4.0 %collective-permute-done = bf16[32,2560]{1,0:T(8,128)(2,1)S(1)} collective-permute-done((bf16[32,2560]{1,0:T(8,128)(2,1)S(1)}, bf16[32,2560]{1,0:T(8,128)(2,1)S(1)}, u32[]{:S(2)}, u32[]{:S(2)}) %collective-permute-start) | collective-permute-done | bytes 163872 | tf_op jit(solution)/shard_map/ppermute | solution.py:47
  32.3 2.7 %collective-permute-start.3 = (bf16[32,2560]{1,0:T(8,128)(2,1)S(1)}, bf16[32,2560]{1,0:T(8,128)(2,1)S(1)}, u32[]{:S(2)}, u32[]{:S(2)}) collective-permute-start(bf16[32,2560]{1,0:T(8,128)(2,1)S(1)} %collective-permute-done.1), channel_id=1, source_target_pairs={{0,224},{32,0},{64,32},{96,64},{128,96},{160,128},{192,160},{224,1... | collective-permute-start | bytes 491528 | tf_op jit(solution)/shard_map/ppermute | solution.py:47
  35.0 3.0 %collective-permute-done.2 = bf16[32,2560]{1,0:T(8,128)(2,1)S(1)} collective-permute-done((bf16[32,2560]{1,0:T(8,128)(2,1)S(1)}, bf16[32,2560]{1,0:T(8,128)(2,1)S(1)}, u32[]{:S(2)}, u32[]{:S(2)}) %collective-permute-start.2) | collective-permute-done | bytes 163872 | tf_op jit(solution)/shard_map/ppermute | solution.py:47
  38.1 2.7 %collective-permute-start.5 = (bf16[32,2560]{1,0:T(8,128)(2,1)S(1)}, bf16[32,2560]{1,0:T(8,128)(2,1)S(1)}, u32[]{:S(2)}, u32[]{:S(2)}) collective-permute-start(bf16[32,2560]{1,0:T(8,128)(2,1)S(1)} %collective-permute-done.3), channel_id=1, source_target_pairs={{0,224},{32,0},{64,32},{96,64},{128,96},{160,128},{192,160},{224,1... | collective-permute-start | bytes 491528 | tf_op jit(solution)/shard_map/ppermute | solution.py:47
  40.9 2.2 %collective-permute-done.5 = bf16[32,2560]{1,0:T(8,128)(2,1)S(1)} collective-permute-done((bf16[32,2560]{1,0:T(8,128)(2,1)S(1)}, bf16[32,2560]{1,0:T(8,128)(2,1)S(1)}, u32[]{:S(2)}, u32[]{:S(2)}) %collective-permute-start.5) | collective-permute-done | bytes 163872 | tf_op jit(solution)/shard_map/ppermute | solution.py:47
  43.1 3.1 %collective-permute-start.7 = (bf16[32,1280]{1,0:T(8,128)(2,1)S(1)}, bf16[32,1280]{1,0:T(8,128)(2,1)S(1)}, u32[]{:S(2)}, u32[]{:S(2)}) collective-permute-start(bf16[32,1280]{1,0:T(8,128)(2,1)S(1)} %slice.88), channel_id=1, source_target_pairs={{0,224},{32,0},{64,32},{96,64},{128,96},{160,128},{192,160},{224,1... | collective-permute-start | bytes 245768 | tf_op jit(solution)/shard_map/ppermute | solution.py:47
  46.4 1.3 collective-permute-done.7
  47.7 3.1 %collective-permute-done.6 = bf16[32,1280]{1,0:T(8,128)(2,1)S(1)} collective-permute-done((bf16[32,1280]{1,0:T(8,128)(2,1)S(1)}, bf16[32,1280]{1,0:T(8,128)(2,1)S(1)}, u32[]{:S(2)}, u32[]{:S(2)}) %collective-permute-start.6) | collective-permute-done | bytes 81952 | tf_op jit(solution)/shard_map/ppermute | solution.py:47
  50.9 0.7 fusion.10
  51.5 0.4 copy-done.5
  51.9 0.8 fusion.15
  52.8 0.8 fusion.70
  53.5 0.7 fusion.69
  54.4 1.5 collective-permute-start.12
  55.9 1.7 %collective-permute-done.8 = bf16[32,1280]{1,0:T(8,128)(2,1)S(1)} collective-permute-done((bf16[32,1280]{1,0:T(8,128)(2,1)S(1)}, bf16[32,1280]{1,0:T(8,128)(2,1)S(1)}, u32[]{:S(2)}, u32[]{:S(2)}) %collective-permute-start.8) | collective-permute-done | bytes 81952 | tf_op jit(solution)/shard_map/ppermute | solution.py:47
  57.7 1.5 collective-permute-start.9
  59.2 0.3 collective-permute-start.13
  59.5 2.8 %collective-permute-done.9 = bf16[32,2560]{1,0:T(8,128)(2,1)S(1)} collective-permute-done((bf16[32,2560]{1,0:T(8,128)(2,1)S(1)}, bf16[32,2560]{1,0:T(8,128)(2,1)S(1)}, u32[]{:S(2)}, u32[]{:S(2)}) %collective-permute-start.9) | collective-permute-done | bytes 163872 | tf_op jit(solution)/shard_map/ppermute | solution.py:47
  62.4 3.2 %collective-permute-start.10 = (bf16[32,2560]{1,0:T(8,128)(2,1)S(1)}, bf16[32,2560]{1,0:T(8,128)(2,1)S(1)}, u32[]{:S(2)}, u32[]{:S(2)}) collective-permute-start(bf16[32,2560]{1,0:T(8,128)(2,1)S(1)} %fusion.39), channel_id=1, source_target_pairs={{0,224},{32,0},{64,32},{96,64},{128,96},{160,128},{192,160},{224,1... | collective-permute-start | bytes 491528 | tf_op jit(solution)/shard_map/ppermute | solution.py:47
  65.6 3.3 %collective-permute-done.10 = bf16[32,2560]{1,0:T(8,128)(2,1)S(1)} collective-permute-done((bf16[32,2560]{1,0:T(8,128)(2,1)S(1)}, bf16[32,2560]{1,0:T(8,128)(2,1)S(1)}, u32[]{:S(2)}, u32[]{:S(2)}) %collective-permute-start.10) | collective-permute-done | bytes 163872 | tf_op jit(solution)/shard_map/ppermute | solution.py:47
  69.1 3.5 %collective-permute-start.11 = (bf16[32,2560]{1,0:T(8,128)(2,1)S(1)}, bf16[32,2560]{1,0:T(8,128)(2,1)S(1)}, u32[]{:S(2)}, u32[]{:S(2)}) collective-permute-start(bf16[32,2560]{1,0:T(8,128)(2,1)S(1)} %get-tuple-element.16), channel_id=1, source_target_pairs={{0,224},{32,0},{64,32},{96,64},{128,96},{160,128},{192,160},{224,1... | collective-permute-start | bytes 491528 | tf_op jit(solution)/shard_map/ppermute | solution.py:47
  72.5 2.6 %collective-permute-done.14 = bf16[32,2560]{1,0:T(8,128)(2,1)S(1)} collective-permute-done((bf16[32,2560]{1,0:T(8,128)(2,1)S(1)}, bf16[32,2560]{1,0:T(8,128)(2,1)S(1)}, u32[]{:S(2)}, u32[]{:S(2)}) %collective-permute-start.14) | collective-permute-done | bytes 163872 | tf_op jit(solution)/shard_map/ppermute | solution.py:47
  75.3 0.2 collective-permute-done.11
  75.5 5.1 %collective-permute-done.15 = bf16[32,2560]{1,0:T(8,128)(2,1)S(1)} collective-permute-done((bf16[32,2560]{1,0:T(8,128)(2,1)S(1)}, bf16[32,2560]{1,0:T(8,128)(2,1)S(1)}, u32[]{:S(2)}, u32[]{:S(2)}) %collective-permute-start.15) | collective-permute-done | bytes 163872 | tf_op jit(solution)/shard_map/ppermute | solution.py:47
  80.7 0.7 reduce.4
  81.5 21.8 %all_to_all.43 = bf16[32,2,1280]{2,1,0:T(2,128)(2,1)S(1)} all-to-all(bf16[32,2,1280]{2,1,0:T(2,128)(2,1)S(1)} %reshape.162), channel_id=1, replica_groups=mesh['dp'=8,'tok'=2,'expert'=16] {'tok','expert'}, dimensions={0} | all-to-all | bytes 327680 | tf_op jit(solution)/shard_map/all_to_all | solution.py:81
  103.5 0.4 fusion.71
  104.0 0.2 fusion.51
  104.5 0.2 fusion.53
  104.7 0.4 multiply_reduce_fusion
  105.2 0.2 convolution_bitcast_fusion
  105.4 0.8 copy.14
  106.3 4.2 %all-to-all-start.2 = ((f32[32,1,1280]{2,1,0:T(1,128)}), f32[32,1,1280]{2,1,0:T(1,128)S(1)}, u32[]{:S(2)}, u32[]{:S(2)}) async-start(f32[32,1,1280]{2,1,0:T(1,128)} %copy.14), calls=%async_computation.2 | async-start | bytes 327680 | tf_op jit(solution)/shard_map/all_to_all | solution.py:81
  110.5 3.2 %fusion.1 = bf16[1,640,1280]{2,1,0:T(8,128)(2,1)} fusion(bf16[256,2560]{1,0:T(8,128)(2,1)} %copy-done.5, f32[256,640]{1,0:T(8,128)} %copy-done.4), kind=kOutput, calls=%fused_computation.3 | convolution fusion | flops 421724160 | bytes 2949120 | tf_op jit(solution)/shard_map/dot_general | solution.py:131
  113.7 4.5 %all-to-all-done.2 = f32[32,1,1280]{2,1,0:T(1,128)S(1)} async-done(((f32[32,1,1280]{2,1,0:T(1,128)}), f32[32,1,1280]{2,1,0:T(1,128)S(1)}, u32[]{:S(2)}, u32[]{:S(2)}) %all-to-all-start.2) | async-done | bytes 163872 | tf_op jit(solution)/shard_map/all_to_all | solution.py:81
  118.4 0.7 collective-permute-start.21
  119.1 1.4 collective-permute-start.22
  120.5 3.0 %fusion = bf16[1,1280,640]{2,1,0:T(8,128)(2,1)} fusion(bf16[256,640]{1,0:T(8,128)(2,1)S(1)} %copy-done.7, bf16[256,2560]{1,0:T(8,128)(2,1)} %copy-done.5), kind=kOutput, calls=%fused_computation.2 | convolution fusion | flops 420249600 | bytes 2621440 | tf_op jit(solution)/shard_map/dot_general | solution.py:128
  123.4 0.8 collective-permute-start.19
  124.2 3.1 %collective-permute-start.20 = (f32[1,1280]{1,0:T(1,128)S(1)}, f32[1,1280]{1,0:T(1,128)S(1)}, u32[]{:S(2)}, u32[]{:S(2)}) collective-permute-start(f32[1,1280]{1,0:T(1,128)S(1)} %broadcast_in_dim.11), channel_id=1, source_target_pairs={{0,160},{32,192},{64,224},{96,0},{128,32},{160,64},{192,96},{224,1... | collective-permute-start | bytes 15368 | tf_op jit(solution)/shard_map/ppermute | solution.py:47
  127.4 0.8 collective-permute-start.17
  128.2 2.8 %collective-permute-start.18 = (f32[1,1280]{1,0:T(1,128)S(1)}, f32[1,1280]{1,0:T(1,128)S(1)}, u32[]{:S(2)}, u32[]{:S(2)}) collective-permute-start(f32[1,1280]{1,0:T(1,128)S(1)} %broadcast_in_dim.11), channel_id=1, source_target_pairs={{0,192},{32,224},{64,0},{96,32},{128,64},{160,96},{192,128},{224,1... | collective-permute-start | bytes 15368 | tf_op jit(solution)/shard_map/ppermute | solution.py:47
  131.0 2.5 %collective-permute-start.16 = (f32[1,1280]{1,0:T(1,128)S(1)}, f32[1,1280]{1,0:T(1,128)S(1)}, u32[]{:S(2)}, u32[]{:S(2)}) collective-permute-start(f32[1,1280]{1,0:T(1,128)S(1)} %broadcast_in_dim.11), channel_id=1, source_target_pairs={{0,128},{32,160},{64,192},{96,224},{128,0},{160,32},{192,64},{224,... | collective-permute-start | bytes 15368 | tf_op jit(solution)/shard_map/ppermute | solution.py:47
  133.5 1.5 fusion.47
  135.0 2.3 %collective-permute-done.16 = f32[1,1280]{1,0:T(1,128)S(1)} collective-permute-done((f32[1,1280]{1,0:T(1,128)S(1)}, f32[1,1280]{1,0:T(1,128)S(1)}, u32[]{:S(2)}, u32[]{:S(2)}) %collective-permute-start.16) | collective-permute-done | bytes 5152 | tf_op jit(solution)/shard_map/ppermute | solution.py:47
  137.4 0.8 broadcast_in_dim.12
  138.1 7.0 %all-to-all-start.3 = ((f32[32,1,1280]{2,1,0:T(1,128)}), f32[32,1,1280]{2,1,0:T(1,128)S(1)}, u32[]{:S(2)}, u32[]{:S(2)}) async-start(f32[32,1,1280]{2,1,0:T(1,128)} %broadcast_in_dim.12), calls=%async_computation.3 | async-start | bytes 327680 | tf_op jit(solution)/shard_map/all_to_all | solution.py:81
  145.2 2.5 %fusion.3 = bf16[1,256,1280]{2,1,0:T(8,128)(2,1)} fusion(f32[256,1280]{1,0:T(8,128)} %fusion.47, bf16[256,32]{0,1:T(8,128)(2,1)S(1)} %add_convert_fusion, bf16[1280,32]{0,1:T(8,128)(2,1)S(1)} %copy-done.8), kind=kOutput, calls=%fused_computation.6 | convolution fusion | flops 21626880 | bytes 2064384 | tf_op jit(solution)/shard_map/dot_general | solution.py:154
  147.7 5.3 %all-to-all-done.3 = f32[32,1,1280]{2,1,0:T(1,128)S(1)} async-done(((f32[32,1,1280]{2,1,0:T(1,128)}), f32[32,1,1280]{2,1,0:T(1,128)S(1)}, u32[]{:S(2)}, u32[]{:S(2)}) %all-to-all-start.3) | async-done | bytes 163872 | tf_op jit(solution)/shard_map/all_to_all | solution.py:81
  153.0 0.7 copy.22
  (93 shorter events, 2.8 us)
Async XLA Ops:
  0.6 51.3 %copy-start = (bf16[1,640,1280]{2,1,0:T(8,128)(2,1)S(1)}, bf16[1,640,1280]{2,1,0:T(8,128)(2,1)}, u32[]{:S(2)}) copy-start(bf16[1,640,1280]{2,1,0:T(8,128)(2,1)} %param.8) | copy-start | bytes 4915204
  0.6 3.7 %copy-start.1 = (bf16[1,256,1280]{2,1,0:T(8,128)(2,1)S(1)}, bf16[1,256,1280]{2,1,0:T(8,128)(2,1)}, u32[]{:S(2)}) copy-start(bf16[1,256,1280]{2,1,0:T(8,128)(2,1)} %param.5) | copy-start | bytes 1966084
  0.7 4.0 %copy-start.3 = (bf16[1,256,1280]{2,1,0:T(8,128)(2,1)S(1)}, bf16[1,256,1280]{2,1,0:T(8,128)(2,1)}, u32[]{:S(2)}) copy-start(bf16[1,256,1280]{2,1,0:T(8,128)(2,1)} %param.9) | copy-start | bytes 1966084
  22.5 9.7 %collective-permute-start = (bf16[32,2560]{1,0:T(8,128)(2,1)S(1)}, bf16[32,2560]{1,0:T(8,128)(2,1)S(1)}, u32[]{:S(2)}, u32[]{:S(2)}) collective-permute-start(bf16[32,2560]{1,0:T(8,128)(2,1)S(1)} %get-tuple-element.13), channel_id=1, source_target_pairs={{0,32},{32,64},{64,96},{96,128},{128,160},{160,192},{192,224},{224... | collective-permute-start | bytes 491528 | tf_op jit(solution)/shard_map/ppermute | solution.py:47
  24.3 8.0 %collective-permute-start.1 = (bf16[32,2560]{1,0:T(8,128)(2,1)S(1)}, bf16[32,2560]{1,0:T(8,128)(2,1)S(1)}, u32[]{:S(2)}, u32[]{:S(2)}) collective-permute-start(bf16[32,2560]{1,0:T(8,128)(2,1)S(1)} %get-tuple-element.13), channel_id=1, source_target_pairs={{0,224},{32,0},{64,32},{96,64},{128,96},{160,128},{192,160},{224,1... | collective-permute-start | bytes 491528 | tf_op jit(solution)/shard_map/ppermute | solution.py:47
  32.3 5.8 %collective-permute-start.2 = (bf16[32,2560]{1,0:T(8,128)(2,1)S(1)}, bf16[32,2560]{1,0:T(8,128)(2,1)S(1)}, u32[]{:S(2)}, u32[]{:S(2)}) collective-permute-start(bf16[32,2560]{1,0:T(8,128)(2,1)S(1)} %collective-permute-done), channel_id=1, source_target_pairs={{0,32},{32,64},{64,96},{96,128},{128,160},{160,192},{192,224},{224... | collective-permute-start | bytes 491528 | tf_op jit(solution)/shard_map/ppermute | solution.py:47
  32.3 18.6 %copy-start.2 = (bf16[1,1280,640]{2,1,0:T(8,128)(2,1)S(1)}, bf16[1,1280,640]{2,1,0:T(8,128)(2,1)}, u32[]{:S(2)}) copy-start(bf16[1,1280,640]{2,1,0:T(8,128)(2,1)} %param.7) | copy-start | bytes 4915204
  32.3 5.8 %collective-permute-start.3 = (bf16[32,2560]{1,0:T(8,128)(2,1)S(1)}, bf16[32,2560]{1,0:T(8,128)(2,1)S(1)}, u32[]{:S(2)}, u32[]{:S(2)}) collective-permute-start(bf16[32,2560]{1,0:T(8,128)(2,1)S(1)} %collective-permute-done.1), channel_id=1, source_target_pairs={{0,224},{32,0},{64,32},{96,64},{128,96},{160,128},{192,160},{224,1... | collective-permute-start | bytes 491528 | tf_op jit(solution)/shard_map/ppermute | solution.py:47
  38.1 8.2 %collective-permute-start.4 = (bf16[32,2560]{1,0:T(8,128)(2,1)S(1)}, bf16[32,2560]{1,0:T(8,128)(2,1)S(1)}, u32[]{:S(2)}, u32[]{:S(2)}) collective-permute-start(bf16[32,2560]{1,0:T(8,128)(2,1)S(1)} %collective-permute-done.2), channel_id=1, source_target_pairs={{0,32},{32,64},{64,96},{96,128},{128,160},{160,192},{192,224},{224... | collective-permute-start | bytes 491528 | tf_op jit(solution)/shard_map/ppermute | solution.py:47
  38.1 5.0 %collective-permute-start.5 = (bf16[32,2560]{1,0:T(8,128)(2,1)S(1)}, bf16[32,2560]{1,0:T(8,128)(2,1)S(1)}, u32[]{:S(2)}, u32[]{:S(2)}) collective-permute-start(bf16[32,2560]{1,0:T(8,128)(2,1)S(1)} %collective-permute-done.3), channel_id=1, source_target_pairs={{0,224},{32,0},{64,32},{96,64},{128,96},{160,128},{192,160},{224,1... | collective-permute-start | bytes 491528 | tf_op jit(solution)/shard_map/ppermute | solution.py:47
  43.1 4.6 %collective-permute-start.7 = (bf16[32,1280]{1,0:T(8,128)(2,1)S(1)}, bf16[32,1280]{1,0:T(8,128)(2,1)S(1)}, u32[]{:S(2)}, u32[]{:S(2)}) collective-permute-start(bf16[32,1280]{1,0:T(8,128)(2,1)S(1)} %slice.88), channel_id=1, source_target_pairs={{0,224},{32,0},{64,32},{96,64},{128,96},{160,128},{192,160},{224,1... | collective-permute-start | bytes 245768 | tf_op jit(solution)/shard_map/ppermute | solution.py:47
  46.2 4.6 %collective-permute-start.6 = (bf16[32,1280]{1,0:T(8,128)(2,1)S(1)}, bf16[32,1280]{1,0:T(8,128)(2,1)S(1)}, u32[]{:S(2)}, u32[]{:S(2)}) collective-permute-start(bf16[32,1280]{1,0:T(8,128)(2,1)S(1)} %slice.87), channel_id=1, source_target_pairs={{0,32},{32,64},{64,96},{96,128},{128,160},{160,192},{192,224},{224... | collective-permute-start | bytes 245768 | tf_op jit(solution)/shard_map/ppermute | solution.py:47
  50.8 1.1 copy-start.5
  51.9 0.8 copy-start.4
  52.7 0.8 copy-start.6
  54.3 3.4 %collective-permute-start.8 = (bf16[32,1280]{1,0:T(8,128)(2,1)S(1)}, bf16[32,1280]{1,0:T(8,128)(2,1)S(1)}, u32[]{:S(2)}, u32[]{:S(2)}) collective-permute-start(bf16[32,1280]{1,0:T(8,128)(2,1)S(1)} %get-tuple-element.18), channel_id=1, source_target_pairs={{0,224},{32,0},{64,32},{96,64},{128,96},{160,128},{192,160},{224,1... | collective-permute-start | bytes 245768 | tf_op jit(solution)/shard_map/ppermute | solution.py:47
  54.4 4.8 %collective-permute-start.12 = (bf16[32,1280]{1,0:T(8,128)(2,1)S(1)}, bf16[32,1280]{1,0:T(8,128)(2,1)S(1)}, u32[]{:S(2)}, u32[]{:S(2)}) collective-permute-start(bf16[32,1280]{1,0:T(8,128)(2,1)S(1)} %get-tuple-element.21), channel_id=1, source_target_pairs={{0,32},{32,64},{64,96},{96,128},{128,160},{160,192},{192,224},{224... | collective-permute-start | bytes 245768 | tf_op jit(solution)/shard_map/ppermute | solution.py:47
  57.7 4.6 %collective-permute-start.9 = (bf16[32,2560]{1,0:T(8,128)(2,1)S(1)}, bf16[32,2560]{1,0:T(8,128)(2,1)S(1)}, u32[]{:S(2)}, u32[]{:S(2)}) collective-permute-start(bf16[32,2560]{1,0:T(8,128)(2,1)S(1)} %pad_maximum_fusion.1), channel_id=1, source_target_pairs={{0,224},{32,0},{64,32},{96,64},{128,96},{160,128},{192,160},{224,1... | collective-permute-start | bytes 491528 | tf_op jit(solution)/shard_map/ppermute | solution.py:47
  59.2 6.3 %collective-permute-start.13 = (bf16[32,2560]{1,0:T(8,128)(2,1)S(1)}, bf16[32,2560]{1,0:T(8,128)(2,1)S(1)}, u32[]{:S(2)}, u32[]{:S(2)}) collective-permute-start(bf16[32,2560]{1,0:T(8,128)(2,1)S(1)} %pad_maximum_fusion.2), channel_id=1, source_target_pairs={{0,32},{32,64},{64,96},{96,128},{128,160},{160,192},{192,224},{224... | collective-permute-start | bytes 491528 | tf_op jit(solution)/shard_map/ppermute | solution.py:47
  62.4 6.5 %collective-permute-start.10 = (bf16[32,2560]{1,0:T(8,128)(2,1)S(1)}, bf16[32,2560]{1,0:T(8,128)(2,1)S(1)}, u32[]{:S(2)}, u32[]{:S(2)}) collective-permute-start(bf16[32,2560]{1,0:T(8,128)(2,1)S(1)} %fusion.39), channel_id=1, source_target_pairs={{0,224},{32,0},{64,32},{96,64},{128,96},{160,128},{192,160},{224,1... | collective-permute-start | bytes 491528 | tf_op jit(solution)/shard_map/ppermute | solution.py:47
  69.0 6.2 %collective-permute-start.14 = (bf16[32,2560]{1,0:T(8,128)(2,1)S(1)}, bf16[32,2560]{1,0:T(8,128)(2,1)S(1)}, u32[]{:S(2)}, u32[]{:S(2)}) collective-permute-start(bf16[32,2560]{1,0:T(8,128)(2,1)S(1)} %get-tuple-element.17), channel_id=1, source_target_pairs={{0,32},{32,64},{64,96},{96,128},{128,160},{160,192},{192,224},{224... | collective-permute-start | bytes 491528 | tf_op jit(solution)/shard_map/ppermute | solution.py:47
  69.1 6.5 %collective-permute-start.11 = (bf16[32,2560]{1,0:T(8,128)(2,1)S(1)}, bf16[32,2560]{1,0:T(8,128)(2,1)S(1)}, u32[]{:S(2)}, u32[]{:S(2)}) collective-permute-start(bf16[32,2560]{1,0:T(8,128)(2,1)S(1)} %get-tuple-element.16), channel_id=1, source_target_pairs={{0,224},{32,0},{64,32},{96,64},{128,96},{160,128},{192,160},{224,1... | collective-permute-start | bytes 491528 | tf_op jit(solution)/shard_map/ppermute | solution.py:47
  75.2 5.5 %collective-permute-start.15 = (bf16[32,2560]{1,0:T(8,128)(2,1)S(1)}, bf16[32,2560]{1,0:T(8,128)(2,1)S(1)}, u32[]{:S(2)}, u32[]{:S(2)}) collective-permute-start(bf16[32,2560]{1,0:T(8,128)(2,1)S(1)} %fusion.36), channel_id=1, source_target_pairs={{0,32},{32,64},{64,96},{96,128},{128,160},{160,192},{192,224},{224... | collective-permute-start | bytes 491528 | tf_op jit(solution)/shard_map/ppermute | solution.py:47
  106.3 12.0 %all-to-all-start.2 = ((f32[32,1,1280]{2,1,0:T(1,128)}), f32[32,1,1280]{2,1,0:T(1,128)S(1)}, u32[]{:S(2)}, u32[]{:S(2)}) async-start(f32[32,1,1280]{2,1,0:T(1,128)} %copy.14), calls=%async_computation.2 | async-start | bytes 327680 | tf_op jit(solution)/shard_map/all_to_all | solution.py:81
  110.5 10.0 %copy-start.7 = (bf16[256,640]{1,0:T(8,128)(2,1)S(1)}, bf16[256,640]{1,0:T(8,128)(2,1)}, u32[]{:S(2)}) copy-start(bf16[256,640]{1,0:T(8,128)(2,1)} %copy-done.6) | copy-start | bytes 983044
  118.4 9.8 %collective-permute-start.21 = (f32[1,1280]{1,0:T(1,128)S(1)}, f32[1,1280]{1,0:T(1,128)S(1)}, u32[]{:S(2)}, u32[]{:S(2)}) collective-permute-start(f32[1,1280]{1,0:T(1,128)S(1)} %broadcast_in_dim.11), channel_id=1, source_target_pairs={{0,96},{32,128},{64,160},{96,192},{128,224},{160,0},{192,32},{224,... | collective-permute-start | bytes 15368 | tf_op jit(solution)/shard_map/ppermute | solution.py:47
  119.1 11.9 %collective-permute-start.22 = (f32[1,1280]{1,0:T(1,128)S(1)}, f32[1,1280]{1,0:T(1,128)S(1)}, u32[]{:S(2)}, u32[]{:S(2)}) collective-permute-start(f32[1,1280]{1,0:T(1,128)S(1)} %broadcast_in_dim.11), channel_id=1, source_target_pairs={{0,224},{32,0},{64,32},{96,64},{128,96},{160,128},{192,160},{224,1... | collective-permute-start | bytes 15368 | tf_op jit(solution)/shard_map/ppermute | solution.py:47
  123.4 21.7 %copy-start.8 = (bf16[1280,32]{0,1:T(8,128)(2,1)S(1)}, bf16[1280,32]{0,1:T(8,128)(2,1)}, u32[]{:S(2)}) copy-start(bf16[1280,32]{0,1:T(8,128)(2,1)} %param.6) | copy-start | bytes 245764
  123.4 11.5 %collective-permute-start.19 = (f32[1,1280]{1,0:T(1,128)S(1)}, f32[1,1280]{1,0:T(1,128)S(1)}, u32[]{:S(2)}, u32[]{:S(2)}) collective-permute-start(f32[1,1280]{1,0:T(1,128)S(1)} %broadcast_in_dim.11), channel_id=1, source_target_pairs={{0,32},{32,64},{64,96},{96,128},{128,160},{160,192},{192,224},{224... | collective-permute-start | bytes 15368 | tf_op jit(solution)/shard_map/ppermute | solution.py:47
  124.2 10.7 %collective-permute-start.20 = (f32[1,1280]{1,0:T(1,128)S(1)}, f32[1,1280]{1,0:T(1,128)S(1)}, u32[]{:S(2)}, u32[]{:S(2)}) collective-permute-start(f32[1,1280]{1,0:T(1,128)S(1)} %broadcast_in_dim.11), channel_id=1, source_target_pairs={{0,160},{32,192},{64,224},{96,0},{128,32},{160,64},{192,96},{224,1... | collective-permute-start | bytes 15368 | tf_op jit(solution)/shard_map/ppermute | solution.py:47
  127.4 7.6 %collective-permute-start.17 = (f32[1,1280]{1,0:T(1,128)S(1)}, f32[1,1280]{1,0:T(1,128)S(1)}, u32[]{:S(2)}, u32[]{:S(2)}) collective-permute-start(f32[1,1280]{1,0:T(1,128)S(1)} %broadcast_in_dim.11), channel_id=1, source_target_pairs={{0,64},{32,96},{64,128},{96,160},{128,192},{160,224},{192,0},{224,... | collective-permute-start | bytes 15368 | tf_op jit(solution)/shard_map/ppermute | solution.py:47
  128.2 6.8 %collective-permute-start.18 = (f32[1,1280]{1,0:T(1,128)S(1)}, f32[1,1280]{1,0:T(1,128)S(1)}, u32[]{:S(2)}, u32[]{:S(2)}) collective-permute-start(f32[1,1280]{1,0:T(1,128)S(1)} %broadcast_in_dim.11), channel_id=1, source_target_pairs={{0,192},{32,224},{64,0},{96,32},{128,64},{160,96},{192,128},{224,1... | collective-permute-start | bytes 15368 | tf_op jit(solution)/shard_map/ppermute | solution.py:47
  131.0 6.4 %collective-permute-start.16 = (f32[1,1280]{1,0:T(1,128)S(1)}, f32[1,1280]{1,0:T(1,128)S(1)}, u32[]{:S(2)}, u32[]{:S(2)}) collective-permute-start(f32[1,1280]{1,0:T(1,128)S(1)} %broadcast_in_dim.11), channel_id=1, source_target_pairs={{0,128},{32,160},{64,192},{96,224},{128,0},{160,32},{192,64},{224,... | collective-permute-start | bytes 15368 | tf_op jit(solution)/shard_map/ppermute | solution.py:47
  138.1 14.8 %all-to-all-start.3 = ((f32[32,1,1280]{2,1,0:T(1,128)}), f32[32,1,1280]{2,1,0:T(1,128)S(1)}, u32[]{:S(2)}, u32[]{:S(2)}) async-start(f32[32,1,1280]{2,1,0:T(1,128)} %broadcast_in_dim.12), calls=%async_computation.3 | async-start | bytes 327680 | tf_op jit(solution)/shard_map/all_to_all | solution.py:81

commit v2 on v1

--- a/solution.py
+++ b/solution.py
@@ -47,34 +47,31 @@
     return lax.ppermute(value, "dp", [(i, (i + step) % size) for i in range(size)])
 
 
-def ring_gather(rows):
+def gather_blocks(rows):
     half = rows.shape[1] // 2
-    blocks = [rows]
-    behind = ahead = rows
-    for _ in range(3):
-        behind, ahead = shift(behind, 1), shift(ahead, -1)
-        blocks += [behind, ahead]
-    far = jnp.concatenate([shift(behind[:, :half], 1), shift(ahead[:, half:], -1)], axis=1)
-    return jnp.concatenate(blocks + [far], axis=0)
+    behind_two, ahead_two = shift(rows, 2), shift(rows, -2)
+    behind_one, ahead_one = shift(rows, 1), shift(rows, -1)
+    behind_three, ahead_three = shift(behind_two, 1), shift(ahead_two, -1)
+    away = jnp.concatenate(
+        [shift(behind_two[:, :half], 2), shift(ahead_two[:, half:], -2)], axis=1
+    )
+    return jnp.concatenate(
+        [rows, behind_one, ahead_one, behind_two, ahead_two, behind_three, ahead_three, away], axis=0
+    )
 
 
-def ring_reduce(partial, rows):
+def reduce_blocks(partial, rows):
     half = partial.shape[1] // 2
     block = [partial[i * rows : (i + 1) * rows] for i in range(8)]
-    own, far = block[0], block[7]
-    down_path, up_path = [block[5], block[3], block[1]], [block[6], block[4], block[2]]
-    narrow = jnp.bfloat16
-    wide = jnp.float32
-    from_above = shift(far[:, :half].astype(narrow), -1).astype(wide)
-    from_below = shift(far[:, half:].astype(narrow), 1).astype(wide)
-    down = jnp.concatenate([from_above + down_path[0][:, :half], down_path[0][:, half:]], axis=1)
-    up = jnp.concatenate([up_path[0][:, :half], from_below + up_path[0][:, half:]], axis=1)
-    for step in range(3):
-        down = shift(down.astype(narrow), -1).astype(wide)
-        up = shift(up.astype(narrow), 1).astype(wide)
-        if step < 2:
-            down, up = down + down_path[step + 1], up + up_path[step + 1]
-    return own + down + up
+    own, behind_one, ahead_one, behind_two, ahead_two, behind_three, ahead_three, away = block
+    send = lambda value, step: shift(value.astype(jnp.bfloat16), step).astype(jnp.float32)
+    down, up = send(behind_three, -1), send(ahead_three, 1)
+    away_down, away_up = send(away[:, :half], -2), send(away[:, half:], 2)
+    near = send(behind_one, -1) + send(ahead_one, 1)
+    down, up = down + behind_two, up + ahead_two
+    down = jnp.concatenate([down[:, :half] + away_down, down[:, half:]], axis=1)
+    up = jnp.concatenate([up[:, :half], up[:, half:] + away_up], axis=1)
+    return own + near + (send(down, -2) + send(up, 2))
 
 
 def swap(value):
@@ -82,13 +79,11 @@
 
 
 def sum_everywhere(part):
-    slots = part.shape[0]
+    slots, width = part.shape
     mine = jnp.sum(swap(part), axis=0, keepdims=True)
-    seen = [mine] + [shift(mine, step) for step in range(1, 8)]
-    while len(seen) > 1:
-        middle = len(seen) // 2
-        seen = [seen[i] + seen[i + middle] for i in range(middle)]
-    return swap(jnp.broadcast_to(seen[0], (slots, part.shape[1])))
+    copies = jnp.broadcast_to(mine, (lax.axis_size("dp"), width))
+    seen = lax.all_to_all(copies, "dp", split_axis=0, concat_axis=0, tiled=True)
+    return swap(jnp.broadcast_to(jnp.sum(seen, axis=0, keepdims=True), (slots, width)))
 
 
 def body(tokens, router, expert_in, expert_out, grad_out):
@@ -107,7 +102,7 @@
         jnp.bfloat16
     )
     rows = swap(jnp.concatenate([slot_part, grad_part], axis=1))
-    gathered = ring_gather(rows)
+    gathered = gather_blocks(rows)
     all_in, all_grad = gathered[:, :model_width], gathered[:, model_width:]
     weight_in = expert_in[0]
     weight_out = expert_out[0]
@@ -122,7 +117,7 @@
     backward_rows = lax.dot_general(
         grad_pre, weight_in, (((1,), (1,)), ((), ())), preferred_element_type=jnp.float32
     )
-    summed = ring_reduce(
+    summed = reduce_blocks(
         jnp.concatenate([forward_rows, backward_rows], axis=1), rows.shape[0]
     ).astype(jnp.bfloat16)
     grad_win = lax.dot_general(

time: 154 us -> 135 us (0.88)
  blocking collectives: 38 us -> 16.2 us
  waiting for transfers between devices: 41.7 us -> 37.2 us
  local copies, waits for them, and re-layouts: 3.7 us -> 6.42 us
  starting transfers between devices: 48 us -> 50.4 us
  other arithmetic: 4.75 us -> 6.44 us
    all_to_all x2 -> x1, blocking collectives: 38 us -> 16.2 us  [swap(): lax.all_to_all(value, ('tok', 'expert'), split_axis=0, concat_axis=0, til...]
    ppermute x23 -> x16, waiting for transfers between devices: 31.9 us -> 17 us  [shift(): lax.ppermute(value, 'dp', [(i, (i + step) % size) for i in range(size)])]
    ppermute x23 -> x16, starting transfers between devices: 36.8 us -> 26.8 us  [shift(): lax.ppermute(value, 'dp', [(i, (i + step) % size) for i in range(size)])]
    all_to_all x2 -> x3, starting transfers between devices: 11.2 us -> 18.4 us  [swap(): lax.all_to_all(value, ('tok', 'expert'), split_axis=0, concat_axis=0, til...]
    all_to_all x0 -> x1, waiting for transfers between devices: none -> 5.47 us  [sum_everywhere(): seen = lax.all_to_all(copies, 'dp', split_axis=0, concat_axis=0, tiled=True)]
    all_to_all x0 -> x1, starting transfers between devices: none -> 5.23 us  [sum_everywhere(): seen = lax.all_to_all(copies, 'dp', split_axis=0, concat_axis=0, tiled=True)]
    all_to_all x2 -> x3, waiting for transfers between devices: 9.84 us -> 14.7 us  [swap(): lax.all_to_all(value, ('tok', 'expert'), split_axis=0, concat_axis=0, til...]
    unnamed x31 -> x27, local copies, waits for them, and re-layouts: 1.55 us -> 3.57 us
  transfers between devices with their start and end apart: 25 -> 20, of which waited for: 14 -> 11; matrix products, arithmetic and copies ran while one was open for 7% -> 8% of each run, Pallas kernels for 0% -> 0%
where the time goes in v2:
time: 135 us; the launch traced here: 134 us
  starting transfers between devices  50.4 us (37%)
  waiting for transfers between devices  37.2 us (28%)
  matrix products  16.3 us (12%)
  blocking collectives  16.2 us (12%)
  other arithmetic  6.44 us (5%)
  local copies, waits for them, and re-layouts  6.42 us (5%)
    ppermute x16, starting transfers between devices, shift(): lax.ppermute(value, 'dp', [(i, (i + step) % size) for i in range(size)])  26.8 us
    all_to_all x3, starting transfers between devices, swap(): lax.all_to_all(value, ('tok', 'expert'), split_axis=0, concat_axis=0, til...  18.4 us
    ppermute x16, waiting for transfers between devices, shift(): lax.ppermute(value, 'dp', [(i, (i + step) % size) for i in range(size)])  17 us
    all_to_all x1, blocking collectives, swap(): lax.all_to_all(value, ('tok', 'expert'), split_axis=0, concat_axis=0, til...  16.2 us
    all_to_all x3, waiting for transfers between devices, swap(): lax.all_to_all(value, ('tok', 'expert'), split_axis=0, concat_axis=0, til...  14.7 us
    all_to_all x1, waiting for transfers between devices, sum_everywhere(): seen = lax.all_to_all(copies, 'dp', split_axis=0, concat_axis=0, tiled=True)  5.47 us
    all_to_all x1, starting transfers between devices, sum_everywhere(): seen = lax.all_to_all(copies, 'dp', split_axis=0, concat_axis=0, tiled=True)  5.23 us
    unnamed x27, local copies, waits for them, and re-layouts  3.57 us
  transfers between devices with their start and end apart: 20, of which 11 were waited for; matrix products, arithmetic and copies ran while one was open for 8% of the time, Pallas kernels for 0%

profile of v2, /device:TPU:1, one launch (start us, length us, event | category | flops | bytes accessed | tf_op | source)
XLA Modules:
  0.0 134.1 jit_solution(13339438961363662150)
XLA Ops:
  0.7 1.6 %fusion.69 = (f32[256]{0:T(256)S(1)}, f32[256,32]{0,1:T(8,128)S(1)}) fusion(bf16[1280,32]{0,1:T(8,128)(2,1)} %param.6, bf16[1,256,1280]{2,1,0:T(8,128)(2,1)} %param.5), kind=kOutput, calls=%fused_computation.142 | convolution fusion | flops 20979456 | bytes 771072 | tf_op jit(solution)/shard_map/dot_general | solution.py:92
  2.3 0.1 subtract_reduce_fusion.3
  2.4 0.2 exponential_reduce_fusion.6
  2.9 0.2 subtract_reduce_fusion.2
  3.1 0.2 exponential_reduce_fusion.4
  3.4 0.1 subtract_reduce_fusion.1
  3.5 0.2 exponential_reduce_fusion.2
  4.0 0.2 subtract_reduce_fusion
  4.2 0.2 exponential_reduce_fusion
  4.4 0.3 convolution_convert_fusion.3
  4.7 0.2 convolution_convert_fusion.2
  4.9 0.5 broadcast.139
  5.4 0.7 reduce.2
  6.2 16.2 %all_to_all.48 = bf16[32,2,1280]{2,1,0:T(2,128)(2,1)S(1)} all-to-all(bf16[32,2,1280]{2,1,0:T(2,128)(2,1)S(1)} %reshape.165), channel_id=1, replica_groups=mesh['dp'=8,'tok'=2,'expert'=16] {'tok','expert'}, dimensions={0} | all-to-all | bytes 327680 | tf_op jit(solution)/shard_map/all_to_all | solution.py:78
  22.4 0.1 reshape.166
  22.6 6.1 %collective-permute-start.3 = (bf16[32,2560]{1,0:T(8,128)(2,1)S(1)}, bf16[32,2560]{1,0:T(8,128)(2,1)S(1)}, u32[]{:S(2)}, u32[]{:S(2)}) collective-permute-start(bf16[32,2560]{1,0:T(8,128)(2,1)S(1)} %get-tuple-element.13), channel_id=1, source_target_pairs={{0,192},{32,224},{64,0},{96,32},{128,64},{160,96},{192,128},{224,1... | collective-permute-start | bytes 491528 | tf_op jit(solution)/shard_map/ppermute | solution.py:47
  28.7 0.7 collective-permute-start
  29.4 2.4 %collective-permute-start.1 = (bf16[32,2560]{1,0:T(8,128)(2,1)S(1)}, bf16[32,2560]{1,0:T(8,128)(2,1)S(1)}, u32[]{:S(2)}, u32[]{:S(2)}) collective-permute-start(bf16[32,2560]{1,0:T(8,128)(2,1)S(1)} %get-tuple-element.13), channel_id=1, source_target_pairs={{0,224},{32,0},{64,32},{96,64},{128,96},{160,128},{192,160},{224,1... | collective-permute-start | bytes 491528 | tf_op jit(solution)/shard_map/ppermute | solution.py:47
  31.8 3.3 %collective-permute-done.3 = bf16[32,2560]{1,0:T(8,128)(2,1)S(1)} collective-permute-done((bf16[32,2560]{1,0:T(8,128)(2,1)S(1)}, bf16[32,2560]{1,0:T(8,128)(2,1)S(1)}, u32[]{:S(2)}, u32[]{:S(2)}) %collective-permute-start.3) | collective-permute-done | bytes 163872 | tf_op jit(solution)/shard_map/ppermute | solution.py:47
  35.1 4.8 %collective-permute-start.7 = (bf16[32,1280]{1,0:T(8,128)(2,1)S(1)}, bf16[32,1280]{1,0:T(8,128)(2,1)S(1)}, u32[]{:S(2)}, u32[]{:S(2)}) collective-permute-start(bf16[32,1280]{1,0:T(8,128)(2,1)S(1)} %slice.90), channel_id=1, source_target_pairs={{0,192},{32,224},{64,0},{96,32},{128,64},{160,96},{192,128},{224,1... | collective-permute-start | bytes 245768 | tf_op jit(solution)/shard_map/ppermute | solution.py:47
  40.1 2.9 %collective-permute-done = bf16[32,2560]{1,0:T(8,128)(2,1)S(1)} collective-permute-done((bf16[32,2560]{1,0:T(8,128)(2,1)S(1)}, bf16[32,2560]{1,0:T(8,128)(2,1)S(1)}, u32[]{:S(2)}, u32[]{:S(2)}) %collective-permute-start) | collective-permute-done | bytes 163872 | tf_op jit(solution)/shard_map/ppermute | solution.py:47
  43.1 4.4 %collective-permute-done.4 = bf16[32,2560]{1,0:T(8,128)(2,1)S(1)} collective-permute-done((bf16[32,2560]{1,0:T(8,128)(2,1)S(1)}, bf16[32,2560]{1,0:T(8,128)(2,1)S(1)}, u32[]{:S(2)}, u32[]{:S(2)}) %collective-permute-start.4) | collective-permute-done | bytes 163872 | tf_op jit(solution)/shard_map/ppermute | solution.py:47
  47.5 0.2 collective-permute-done.5
  47.7 0.7 fusion.11
  48.5 0.8 fusion.7
  49.3 0.8 fusion.16
  50.1 0.7 fusion.9
  50.8 0.1 fusion.2
  51.0 2.5 %collective-permute-start.10 = (bf16[32,2560]{1,0:T(8,128)(2,1)S(1)}, bf16[32,2560]{1,0:T(8,128)(2,1)S(1)}, u32[]{:S(2)}, u32[]{:S(2)}) collective-permute-start(bf16[32,2560]{1,0:T(8,128)(2,1)S(1)} %get-tuple-element.20), channel_id=1, source_target_pairs={{0,224},{32,0},{64,32},{96,64},{128,96},{160,128},{192,160},{224,1... | collective-permute-start | bytes 491528 | tf_op jit(solution)/shard_map/ppermute | solution.py:47
  53.7 3.6 %collective-permute-start.11 = (bf16[32,1280]{1,0:T(8,128)(2,1)S(1)}, bf16[32,1280]{1,0:T(8,128)(2,1)S(1)}, u32[]{:S(2)}, u32[]{:S(2)}) collective-permute-start(bf16[32,1280]{1,0:T(8,128)(2,1)S(1)} %slice.170), channel_id=1, source_target_pairs={{0,192},{32,224},{64,0},{96,32},{128,64},{160,96},{192,128},{224,1... | collective-permute-start | bytes 245768 | tf_op jit(solution)/shard_map/ppermute | solution.py:47
  57.2 0.4 collective-permute-start.9
  57.6 2.3 %collective-permute-start.8 = (bf16[32,2560]{1,0:T(8,128)(2,1)S(1)}, bf16[32,2560]{1,0:T(8,128)(2,1)S(1)}, u32[]{:S(2)}, u32[]{:S(2)}) collective-permute-start(bf16[32,2560]{1,0:T(8,128)(2,1)S(1)} %get-tuple-element.18), channel_id=1, source_target_pairs={{0,224},{32,0},{64,32},{96,64},{128,96},{160,128},{192,160},{224,1... | collective-permute-start | bytes 491528 | tf_op jit(solution)/shard_map/ppermute | solution.py:47
  60.0 0.5 collective-permute-done.14
  60.7 3.6 %collective-permute-start.12 = (bf16[32,2560]{1,0:T(8,128)(2,1)S(1)}, bf16[32,2560]{1,0:T(8,128)(2,1)S(1)}, u32[]{:S(2)}, u32[]{:S(2)}) collective-permute-start(bf16[32,2560]{1,0:T(8,128)(2,1)S(1)} %pad_maximum_fusion.1), channel_id=1, source_target_pairs={{0,192},{32,224},{64,0},{96,32},{128,64},{160,96},{192,128},{224,1... | collective-permute-start | bytes 491528 | tf_op jit(solution)/shard_map/ppermute | solution.py:47
  64.3 1.9 %collective-permute-done.9 = bf16[32,2560]{1,0:T(8,128)(2,1)S(1)} collective-permute-done((bf16[32,2560]{1,0:T(8,128)(2,1)S(1)}, bf16[32,2560]{1,0:T(8,128)(2,1)S(1)}, u32[]{:S(2)}, u32[]{:S(2)}) %collective-permute-start.9) | collective-permute-done | bytes 163872 | tf_op jit(solution)/shard_map/ppermute | solution.py:47
  66.2 3.9 %collective-permute-done.15 = bf16[32,2560]{1,0:T(8,128)(2,1)S(1)} collective-permute-done((bf16[32,2560]{1,0:T(8,128)(2,1)S(1)}, bf16[32,2560]{1,0:T(8,128)(2,1)S(1)}, u32[]{:S(2)}, u32[]{:S(2)}) %collective-permute-start.15) | collective-permute-done | bytes 163872 | tf_op jit(solution)/shard_map/ppermute | solution.py:47
  70.1 0.8 fusion.46
  70.9 1.6 %reduce.3 = bf16[32,2560]{1,0:T(8,128)(2,1)S(1)} reduce(bf16[32,1,2560]{2,0,1:T(8,128)(2,1)} %fusion.46, bf16[]{:T(256)} %broadcast.139), dimensions={1}, to_apply=%copy.19.reduce_sub_computation | reduce | bytes 327682 | tf_op jit(solution)/shard_map/all_to_all | solution.py:78
  72.5 0.7 reshape.167
  73.2 8.6 %all-to-all-start.1 = ((bf16[32,2,1280]{2,1,0:T(2,128)(2,1)}), bf16[32,2,1280]{2,1,0:T(2,128)(2,1)S(1)}, u32[]{:S(2)}, u32[]{:S(2)}) async-start(bf16[32,2,1280]{2,1,0:T(2,128)(2,1)} %reshape.167), calls=%async_computation.1 | async-start | bytes 327680 | tf_op jit(solution)/shard_map/all_to_all | solution.py:78
  81.8 3.2 %fusion.1 = bf16[1,640,1280]{2,1,0:T(8,128)(2,1)} fusion(bf16[256,2560]{1,0:T(8,128)(2,1)} %copy-done.5, f32[256,640]{1,0:T(8,128)} %copy-done.4), kind=kOutput, calls=%fused_computation.10 | convolution fusion | flops 421724160 | bytes 2949120 | tf_op jit(solution)/shard_map/dot_general | solution.py:126
  85.0 4.6 %all-to-all-done.1 = bf16[32,2,1280]{2,1,0:T(2,128)(2,1)S(1)} async-done(((bf16[32,2,1280]{2,1,0:T(2,128)(2,1)}), bf16[32,2,1280]{2,1,0:T(2,128)(2,1)S(1)}, u32[]{:S(2)}, u32[]{:S(2)}) %all-to-all-start.1) | async-done | bytes 163872 | tf_op jit(solution)/shard_map/all_to_all | solution.py:78
  89.6 0.8 reshape.168
  90.4 1.0 copy.31
  91.4 0.4 fusion.70
  92.0 0.2 fusion.53
  92.3 0.1 fusion.54
  92.5 0.2 fusion.55
  92.7 0.4 multiply_reduce_fusion
  93.2 0.2 convolution_bitcast_fusion
  93.4 0.8 copy.20
  94.3 4.2 %all-to-all-start.2 = ((f32[32,1,1280]{2,1,0:T(1,128)}), f32[32,1,1280]{2,1,0:T(1,128)S(1)}, u32[]{:S(2)}, u32[]{:S(2)}) async-start(f32[32,1,1280]{2,1,0:T(1,128)} %copy.20), calls=%async_computation.2 | async-start | bytes 327680 | tf_op jit(solution)/shard_map/all_to_all | solution.py:78
  98.5 3.0 %fusion = bf16[1,1280,640]{2,1,0:T(8,128)(2,1)} fusion(bf16[256,640]{1,0:T(8,128)(2,1)S(1)} %fusion.16, bf16[256,2560]{1,0:T(8,128)(2,1)} %copy-done.5), kind=kOutput, calls=%fused_computation.9 | convolution fusion | flops 420249600 | bytes 2621440 | tf_op jit(solution)/shard_map/dot_general | solution.py:123
  101.4 4.8 %all-to-all-done.2 = f32[32,1,1280]{2,1,0:T(1,128)S(1)} async-done(((f32[32,1,1280]{2,1,0:T(1,128)}), f32[32,1,1280]{2,1,0:T(1,128)S(1)}, u32[]{:S(2)}, u32[]{:S(2)}) %all-to-all-start.2) | async-done | bytes 163872 | tf_op jit(solution)/shard_map/all_to_all | solution.py:78
  106.3 0.1 reduce_sum.198
  106.4 0.6 broadcast_in_dim.11
  107.0 5.2 %all-to-all-start.3 = ((f32[8,1,1280]{2,1,0:T(1,128)}), f32[8,1,1280]{2,1,0:T(1,128)S(1)}, u32[]{:S(2)}, u32[]{:S(2)}) async-start(f32[8,1,1280]{2,1,0:T(1,128)} %broadcast_in_dim.11), calls=%async_computation.3 | async-start | bytes 81920 | tf_op jit(solution)/shard_map/all_to_all | solution.py:85
  112.2 1.5 %fusion.49 = f32[256,1280]{1,0:T(8,128)} fusion(bf16[32,2560]{1,0:T(8,128)(2,1)S(1)} %bitcast.71, f32[32]{0:T(128)S(1)} %log_add_fusion.4, f32[256]{0:T(256)S(1)} %log_add_fusion, f32[256,32]{0,1:T(8,128)S(1)} %get-tuple-element.15, f32[32]{0:T(128)S(1)} %log_add_fusion.5, f32[256]{0:T(256)S(1)} %log_add_fusion.1), kind=kOutput, calls=%fused_computation.76 | convolution fusion | flops 21012480 | bytes 1428480 | tf_op jit(solution)/shard_map/dot_general | solution.py:148
  113.7 5.5 %all-to-all-done.3 = f32[8,1,1280]{2,1,0:T(1,128)S(1)} async-done(((f32[8,1,1280]{2,1,0:T(1,128)}), f32[8,1,1280]{2,1,0:T(1,128)S(1)}, u32[]{:S(2)}, u32[]{:S(2)}) %all-to-all-start.3) | async-done | bytes 40992 | tf_op jit(solution)/shard_map/all_to_all | solution.py:85
  119.2 0.8 broadcast_in_dim.12
  120.0 5.6 %all-to-all-start.4 = ((f32[32,1,1280]{2,1,0:T(1,128)}), f32[32,1,1280]{2,1,0:T(1,128)S(1)}, u32[]{:S(2)}, u32[]{:S(2)}) async-start(f32[32,1,1280]{2,1,0:T(1,128)} %broadcast_in_dim.12), calls=%async_computation.4 | async-start | bytes 327680 | tf_op jit(solution)/shard_map/all_to_all | solution.py:78
  125.6 2.5 %fusion.4 = bf16[1,256,1280]{2,1,0:T(8,128)(2,1)} fusion(f32[256,1280]{1,0:T(8,128)} %fusion.49, bf16[256,32]{0,1:T(8,128)(2,1)S(1)} %add_convert_fusion, bf16[1280,32]{0,1:T(8,128)(2,1)S(1)} %copy-done.6), kind=kOutput, calls=%fused_computation.14 | convolution fusion | flops 21626880 | bytes 2064384 | tf_op jit(solution)/shard_map/dot_general | solution.py:149
  128.2 5.3 %all-to-all-done.4 = f32[32,1,1280]{2,1,0:T(1,128)S(1)} async-done(((f32[32,1,1280]{2,1,0:T(1,128)}), f32[32,1,1280]{2,1,0:T(1,128)S(1)}, u32[]{:S(2)}, u32[]{:S(2)}) %all-to-all-start.4) | async-done | bytes 163872 | tf_op jit(solution)/shard_map/all_to_all | solution.py:78
  133.4 0.7 copy.30
  (80 shorter events, 2.0 us)
Async XLA Ops:
  0.6 47.8 %copy-start = (bf16[1,640,1280]{2,1,0:T(8,128)(2,1)S(1)}, bf16[1,640,1280]{2,1,0:T(8,128)(2,1)}, u32[]{:S(2)}) copy-start(bf16[1,640,1280]{2,1,0:T(8,128)(2,1)} %param.8) | copy-start | bytes 4915204
  0.6 3.7 %copy-start.1 = (bf16[1,256,1280]{2,1,0:T(8,128)(2,1)S(1)}, bf16[1,256,1280]{2,1,0:T(8,128)(2,1)}, u32[]{:S(2)}) copy-start(bf16[1,256,1280]{2,1,0:T(8,128)(2,1)} %param.5) | copy-start | bytes 1966084
  0.7 4.0 %copy-start.3 = (bf16[1,256,1280]{2,1,0:T(8,128)(2,1)S(1)}, bf16[1,256,1280]{2,1,0:T(8,128)(2,1)}, u32[]{:S(2)}) copy-start(bf16[1,256,1280]{2,1,0:T(8,128)(2,1)} %param.9) | copy-start | bytes 1966084
  22.5 25.2 %copy-start.2 = (bf16[1,1280,640]{2,1,0:T(8,128)(2,1)S(1)}, bf16[1,1280,640]{2,1,0:T(8,128)(2,1)}, u32[]{:S(2)}) copy-start(bf16[1,1280,640]{2,1,0:T(8,128)(2,1)} %param.7) | copy-start | bytes 4915204
  22.6 12.5 %collective-permute-start.3 = (bf16[32,2560]{1,0:T(8,128)(2,1)S(1)}, bf16[32,2560]{1,0:T(8,128)(2,1)S(1)}, u32[]{:S(2)}, u32[]{:S(2)}) collective-permute-start(bf16[32,2560]{1,0:T(8,128)(2,1)S(1)} %get-tuple-element.13), channel_id=1, source_target_pairs={{0,192},{32,224},{64,0},{96,32},{128,64},{160,96},{192,128},{224,1... | collective-permute-start | bytes 491528 | tf_op jit(solution)/shard_map/ppermute | solution.py:47
  28.7 11.2 %collective-permute-start.2 = (bf16[32,2560]{1,0:T(8,128)(2,1)S(1)}, bf16[32,2560]{1,0:T(8,128)(2,1)S(1)}, u32[]{:S(2)}, u32[]{:S(2)}) collective-permute-start(bf16[32,2560]{1,0:T(8,128)(2,1)S(1)} %get-tuple-element.13), channel_id=1, source_target_pairs={{0,64},{32,96},{64,128},{96,160},{128,192},{160,224},{192,0},{224,... | collective-permute-start | bytes 491528 | tf_op jit(solution)/shard_map/ppermute | solution.py:47
  28.7 14.3 %collective-permute-start = (bf16[32,2560]{1,0:T(8,128)(2,1)S(1)}, bf16[32,2560]{1,0:T(8,128)(2,1)S(1)}, u32[]{:S(2)}, u32[]{:S(2)}) collective-permute-start(bf16[32,2560]{1,0:T(8,128)(2,1)S(1)} %get-tuple-element.13), channel_id=1, source_target_pairs={{0,32},{32,64},{64,96},{96,128},{128,160},{160,192},{192,224},{224... | collective-permute-start | bytes 491528 | tf_op jit(solution)/shard_map/ppermute | solution.py:47
  29.4 13.6 %collective-permute-start.1 = (bf16[32,2560]{1,0:T(8,128)(2,1)S(1)}, bf16[32,2560]{1,0:T(8,128)(2,1)S(1)}, u32[]{:S(2)}, u32[]{:S(2)}) collective-permute-start(bf16[32,2560]{1,0:T(8,128)(2,1)S(1)} %get-tuple-element.13), channel_id=1, source_target_pairs={{0,224},{32,0},{64,32},{96,64},{128,96},{160,128},{192,160},{224,1... | collective-permute-start | bytes 491528 | tf_op jit(solution)/shard_map/ppermute | solution.py:47
  35.1 12.6 %collective-permute-start.7 = (bf16[32,1280]{1,0:T(8,128)(2,1)S(1)}, bf16[32,1280]{1,0:T(8,128)(2,1)S(1)}, u32[]{:S(2)}, u32[]{:S(2)}) collective-permute-start(bf16[32,1280]{1,0:T(8,128)(2,1)S(1)} %slice.90), channel_id=1, source_target_pairs={{0,192},{32,224},{64,0},{96,32},{128,64},{160,96},{192,128},{224,1... | collective-permute-start | bytes 245768 | tf_op jit(solution)/shard_map/ppermute | solution.py:47
  39.9 7.8 %collective-permute-start.6 = (bf16[32,1280]{1,0:T(8,128)(2,1)S(1)}, bf16[32,1280]{1,0:T(8,128)(2,1)S(1)}, u32[]{:S(2)}, u32[]{:S(2)}) collective-permute-start(bf16[32,1280]{1,0:T(8,128)(2,1)S(1)} %slice.89), channel_id=1, source_target_pairs={{0,64},{32,96},{64,128},{96,160},{128,192},{160,224},{192,0},{224,... | collective-permute-start | bytes 245768 | tf_op jit(solution)/shard_map/ppermute | solution.py:47
  40.0 7.5 %collective-permute-start.4 = (bf16[32,2560]{1,0:T(8,128)(2,1)S(1)}, bf16[32,2560]{1,0:T(8,128)(2,1)S(1)}, u32[]{:S(2)}, u32[]{:S(2)}) collective-permute-start(bf16[32,2560]{1,0:T(8,128)(2,1)S(1)} %collective-permute-done.2), channel_id=1, source_target_pairs={{0,32},{32,64},{64,96},{96,128},{128,160},{160,192},{192,224},{224... | collective-permute-start | bytes 491528 | tf_op jit(solution)/shard_map/ppermute | solution.py:47
  43.0 4.7 %collective-permute-start.5 = (bf16[32,2560]{1,0:T(8,128)(2,1)S(1)}, bf16[32,2560]{1,0:T(8,128)(2,1)S(1)}, u32[]{:S(2)}, u32[]{:S(2)}) collective-permute-start(bf16[32,2560]{1,0:T(8,128)(2,1)S(1)} %collective-permute-done.3), channel_id=1, source_target_pairs={{0,224},{32,0},{64,32},{96,64},{128,96},{160,128},{192,160},{224,1... | collective-permute-start | bytes 491528 | tf_op jit(solution)/shard_map/ppermute | solution.py:47
  47.7 1.5 %copy-start.5 = (bf16[256,2560]{1,0:T(8,128)(2,1)}, bf16[256,2560]{1,0:T(8,128)(2,1)S(1)}, u32[]{:S(2)}) copy-start(bf16[256,2560]{1,0:T(8,128)(2,1)S(1)} %maximum_dynamic-update-slice_fusion) | copy-start | bytes 3932164
  48.4 0.8 copy-start.4
  51.0 6.6 %collective-permute-start.10 = (bf16[32,2560]{1,0:T(8,128)(2,1)S(1)}, bf16[32,2560]{1,0:T(8,128)(2,1)S(1)}, u32[]{:S(2)}, u32[]{:S(2)}) collective-permute-start(bf16[32,2560]{1,0:T(8,128)(2,1)S(1)} %get-tuple-element.20), channel_id=1, source_target_pairs={{0,224},{32,0},{64,32},{96,64},{128,96},{160,128},{192,160},{224,1... | collective-permute-start | bytes 491528 | tf_op jit(solution)/shard_map/ppermute | solution.py:47
  53.5 6.4 %collective-permute-start.13 = (bf16[32,2560]{1,0:T(8,128)(2,1)S(1)}, bf16[32,2560]{1,0:T(8,128)(2,1)S(1)}, u32[]{:S(2)}, u32[]{:S(2)}) collective-permute-start(bf16[32,2560]{1,0:T(8,128)(2,1)S(1)} %get-tuple-element.19), channel_id=1, source_target_pairs={{0,32},{32,64},{64,96},{96,128},{128,160},{160,192},{192,224},{224... | collective-permute-start | bytes 491528 | tf_op jit(solution)/shard_map/ppermute | solution.py:47
  53.6 6.9 %collective-permute-start.14 = (bf16[32,1280]{1,0:T(8,128)(2,1)S(1)}, bf16[32,1280]{1,0:T(8,128)(2,1)S(1)}, u32[]{:S(2)}, u32[]{:S(2)}) collective-permute-start(bf16[32,1280]{1,0:T(8,128)(2,1)S(1)} %slice.167), channel_id=1, source_target_pairs={{0,64},{32,96},{64,128},{96,160},{128,192},{160,224},{192,0},{224,... | collective-permute-start | bytes 245768 | tf_op jit(solution)/shard_map/ppermute | solution.py:47
  53.7 7.0 %collective-permute-start.11 = (bf16[32,1280]{1,0:T(8,128)(2,1)S(1)}, bf16[32,1280]{1,0:T(8,128)(2,1)S(1)}, u32[]{:S(2)}, u32[]{:S(2)}) collective-permute-start(bf16[32,1280]{1,0:T(8,128)(2,1)S(1)} %slice.170), channel_id=1, source_target_pairs={{0,192},{32,224},{64,0},{96,32},{128,64},{160,96},{192,128},{224,1... | collective-permute-start | bytes 245768 | tf_op jit(solution)/shard_map/ppermute | solution.py:47
  57.2 9.0 %collective-permute-start.9 = (bf16[32,2560]{1,0:T(8,128)(2,1)S(1)}, bf16[32,2560]{1,0:T(8,128)(2,1)S(1)}, u32[]{:S(2)}, u32[]{:S(2)}) collective-permute-start(bf16[32,2560]{1,0:T(8,128)(2,1)S(1)} %get-tuple-element.21), channel_id=1, source_target_pairs={{0,32},{32,64},{64,96},{96,128},{128,160},{160,192},{192,224},{224... | collective-permute-start | bytes 491528 | tf_op jit(solution)/shard_map/ppermute | solution.py:47
  57.6 8.6 %collective-permute-start.8 = (bf16[32,2560]{1,0:T(8,128)(2,1)S(1)}, bf16[32,2560]{1,0:T(8,128)(2,1)S(1)}, u32[]{:S(2)}, u32[]{:S(2)}) collective-permute-start(bf16[32,2560]{1,0:T(8,128)(2,1)S(1)} %get-tuple-element.18), channel_id=1, source_target_pairs={{0,224},{32,0},{64,32},{96,64},{128,96},{160,128},{192,160},{224,1... | collective-permute-start | bytes 491528 | tf_op jit(solution)/shard_map/ppermute | solution.py:47
  60.5 9.6 %collective-permute-start.15 = (bf16[32,2560]{1,0:T(8,128)(2,1)S(1)}, bf16[32,2560]{1,0:T(8,128)(2,1)S(1)}, u32[]{:S(2)}, u32[]{:S(2)}) collective-permute-start(bf16[32,2560]{1,0:T(8,128)(2,1)S(1)} %pad_maximum_fusion.2), channel_id=1, source_target_pairs={{0,64},{32,96},{64,128},{96,160},{128,192},{160,224},{192,0},{224,... | collective-permute-start | bytes 491528 | tf_op jit(solution)/shard_map/ppermute | solution.py:47
  60.7 9.4 %collective-permute-start.12 = (bf16[32,2560]{1,0:T(8,128)(2,1)S(1)}, bf16[32,2560]{1,0:T(8,128)(2,1)S(1)}, u32[]{:S(2)}, u32[]{:S(2)}) collective-permute-start(bf16[32,2560]{1,0:T(8,128)(2,1)S(1)} %pad_maximum_fusion.1), channel_id=1, source_target_pairs={{0,192},{32,224},{64,0},{96,32},{128,64},{160,96},{192,128},{224,1... | collective-permute-start | bytes 491528 | tf_op jit(solution)/shard_map/ppermute | solution.py:47
  73.2 16.4 %all-to-all-start.1 = ((bf16[32,2,1280]{2,1,0:T(2,128)(2,1)}), bf16[32,2,1280]{2,1,0:T(2,128)(2,1)S(1)}, u32[]{:S(2)}, u32[]{:S(2)}) async-start(bf16[32,2,1280]{2,1,0:T(2,128)(2,1)} %reshape.167), calls=%async_computation.1 | async-start | bytes 327680 | tf_op jit(solution)/shard_map/all_to_all | solution.py:78
  94.3 12.0 %all-to-all-start.2 = ((f32[32,1,1280]{2,1,0:T(1,128)}), f32[32,1,1280]{2,1,0:T(1,128)S(1)}, u32[]{:S(2)}, u32[]{:S(2)}) async-start(f32[32,1,1280]{2,1,0:T(1,128)} %copy.20), calls=%async_computation.2 | async-start | bytes 327680 | tf_op jit(solution)/shard_map/all_to_all | solution.py:78
  101.4 24.2 %copy-start.6 = (bf16[1280,32]{0,1:T(8,128)(2,1)S(1)}, bf16[1280,32]{0,1:T(8,128)(2,1)}, u32[]{:S(2)}) copy-start(bf16[1280,32]{0,1:T(8,128)(2,1)} %param.6) | copy-start | bytes 245764
  107.0 12.2 %all-to-all-start.3 = ((f32[8,1,1280]{2,1,0:T(1,128)}), f32[8,1,1280]{2,1,0:T(1,128)S(1)}, u32[]{:S(2)}, u32[]{:S(2)}) async-start(f32[8,1,1280]{2,1,0:T(1,128)} %broadcast_in_dim.11), calls=%async_computation.3 | async-start | bytes 81920 | tf_op jit(solution)/shard_map/all_to_all | solution.py:85
  120.0 13.4 %all-to-all-start.4 = ((f32[32,1,1280]{2,1,0:T(1,128)}), f32[32,1,1280]{2,1,0:T(1,128)S(1)}, u32[]{:S(2)}, u32[]{:S(2)}) async-start(f32[32,1,1280]{2,1,0:T(1,128)} %broadcast_in_dim.12), calls=%async_computation.4 | async-start | bytes 327680 | tf_op jit(solution)/shard_map/all_to_all | solution.py:78

commit v3 on v2

--- a/solution.py
+++ b/solution.py
@@ -47,33 +47,6 @@
     return lax.ppermute(value, "dp", [(i, (i + step) % size) for i in range(size)])
 
 
-def gather_blocks(rows):
-    half = rows.shape[1] // 2
-    behind_two, ahead_two = shift(rows, 2), shift(rows, -2)
-    behind_one, ahead_one = shift(rows, 1), shift(rows, -1)
-    behind_three, ahead_three = shift(behind_two, 1), shift(ahead_two, -1)
-    away = jnp.concatenate(
-        [shift(behind_two[:, :half], 2), shift(ahead_two[:, half:], -2)], axis=1
-    )
-    return jnp.concatenate(
-        [rows, behind_one, ahead_one, behind_two, ahead_two, behind_three, ahead_three, away], axis=0
-    )
-
-
-def reduce_blocks(partial, rows):
-    half = partial.shape[1] // 2
-    block = [partial[i * rows : (i + 1) * rows] for i in range(8)]
-    own, behind_one, ahead_one, behind_two, ahead_two, behind_three, ahead_three, away = block
-    send = lambda value, step: shift(value.astype(jnp.bfloat16), step).astype(jnp.float32)
-    down, up = send(behind_three, -1), send(ahead_three, 1)
-    away_down, away_up = send(away[:, :half], -2), send(away[:, half:], 2)
-    near = send(behind_one, -1) + send(ahead_one, 1)
-    down, up = down + behind_two, up + ahead_two
-    down = jnp.concatenate([down[:, :half] + away_down, down[:, half:]], axis=1)
-    up = jnp.concatenate([up[:, :half], up[:, half:] + away_up], axis=1)
-    return own + near + (send(down, -2) + send(up, 2))
-
-
 def swap(value):
     return lax.all_to_all(value, ("tok", "expert"), split_axis=0, concat_axis=0, tiled=True)
 
@@ -84,6 +57,28 @@
     copies = jnp.broadcast_to(mine, (lax.axis_size("dp"), width))
     seen = lax.all_to_all(copies, "dp", split_axis=0, concat_axis=0, tiled=True)
     return swap(jnp.broadcast_to(jnp.sum(seen, axis=0, keepdims=True), (slots, width)))
+
+
+def paired_swap(first, second):
+    moved = swap(jnp.stack([first, second], axis=1))
+    return jnp.concatenate([moved[:, 0], moved[:, 1]], axis=1)
+
+
+def expert_rows(rows, weight_in, weight_out):
+    width = weight_in.shape[0]
+    row_in, row_grad = rows[:, :width], rows[:, width:]
+    hidden_pre = jnp.dot(row_in, weight_in, preferred_element_type=jnp.float32)
+    activated, derivative = gelu_pair(hidden_pre)
+    hidden_act = activated.astype(jnp.bfloat16)
+    grad_act = lax.dot_general(
+        row_grad, weight_out, (((1,), (1,)), ((), ())), preferred_element_type=jnp.float32
+    )
+    grad_pre = (grad_act * derivative).astype(jnp.bfloat16)
+    forward_rows = jnp.dot(hidden_act, weight_out, preferred_element_type=jnp.float32)
+    backward_rows = lax.dot_general(
+        grad_pre, weight_in, (((1,), (1,)), ((), ())), preferred_element_type=jnp.float32
+    )
+    return hidden_act, grad_pre, forward_rows, backward_rows
 
 
 def body(tokens, router, expert_in, expert_out, grad_out):
@@ -101,33 +96,56 @@
     grad_part = jnp.dot(combine_rounded.T, image_grad, preferred_element_type=jnp.float32).astype(
         jnp.bfloat16
     )
-    rows = swap(jnp.concatenate([slot_part, grad_part], axis=1))
-    gathered = gather_blocks(rows)
-    all_in, all_grad = gathered[:, :model_width], gathered[:, model_width:]
+    rows = paired_swap(slot_part, grad_part)
     weight_in = expert_in[0]
     weight_out = expert_out[0]
-    hidden_pre = jnp.dot(all_in, weight_in, preferred_element_type=jnp.float32)
-    activated, derivative = gelu_pair(hidden_pre)
-    hidden_act = activated.astype(jnp.bfloat16)
-    grad_act = lax.dot_general(
-        all_grad, weight_out, (((1,), (1,)), ((), ())), preferred_element_type=jnp.float32
+    count, half = rows.shape[0], model_width
+
+    behind_two, ahead_two = shift(rows, 2), shift(rows, -2)
+    behind_one, ahead_one = shift(rows, 1), shift(rows, -1)
+    behind_three, ahead_three = shift(behind_two, 1), shift(ahead_two, -1)
+    away = jnp.concatenate(
+        [shift(behind_two[:, :half], 2), shift(ahead_two[:, half:], -2)], axis=1
     )
-    grad_pre = (grad_act * derivative).astype(jnp.bfloat16)
-    forward_rows = jnp.dot(hidden_act, weight_out, preferred_element_type=jnp.float32)
-    backward_rows = lax.dot_general(
-        grad_pre, weight_in, (((1,), (1,)), ((), ())), preferred_element_type=jnp.float32
+    near_rows = jnp.concatenate([rows, behind_one, ahead_one, behind_two, ahead_two], axis=0)
+    far_rows = jnp.concatenate([behind_three, ahead_three, away], axis=0)
+    near_act, near_pre, near_forward, near_backward = expert_rows(near_rows, weight_in, weight_out)
+
+    def block(forward_rows, backward_rows, place):
+        piece = slice(place * count, (place + 1) * count)
+        return jnp.concatenate([forward_rows[piece], backward_rows[piece]], axis=1)
+
+    send = lambda value, step: shift(value.astype(jnp.bfloat16), step).astype(jnp.float32)
+    own = block(near_forward, near_backward, 0)
+    to_behind, to_ahead, far_rows = lax.optimization_barrier(
+        (
+            block(near_forward, near_backward, 1).astype(jnp.bfloat16),
+            block(near_forward, near_backward, 2).astype(jnp.bfloat16),
+            far_rows,
+        )
     )
-    summed = reduce_blocks(
-        jnp.concatenate([forward_rows, backward_rows], axis=1), rows.shape[0]
-    ).astype(jnp.bfloat16)
+    near = send(to_behind, -1) + send(to_ahead, 1)
+    far_act, far_pre, far_forward, far_backward = expert_rows(far_rows, weight_in, weight_out)
+    down = send(block(far_forward, far_backward, 0), -1)
+    up = send(block(far_forward, far_backward, 1), 1)
+    away_down, away_up = send(far_forward[2 * count :], -2), send(far_backward[2 * count :], 2)
+    down = down + block(near_forward, near_backward, 3)
+    up = up + block(near_forward, near_backward, 4)
+    down = jnp.concatenate([down[:, :half] + away_down, down[:, half:]], axis=1)
+    up = jnp.concatenate([up[:, :half], up[:, half:] + away_up], axis=1)
+    summed = (own + near + (send(down, -2) + send(up, 2))).astype(jnp.bfloat16)
+
+    all_rows = jnp.concatenate([near_rows, far_rows], axis=0)
+    grad_pre = jnp.concatenate([near_pre, far_pre], axis=0)
+    hidden_act = jnp.concatenate([near_act, far_act], axis=0)
     grad_win = lax.dot_general(
-        all_in, grad_pre, (((0,), (0,)), ((), ())), preferred_element_type=jnp.float32
+        all_rows[:, :half], grad_pre, (((0,), (0,)), ((), ())), preferred_element_type=jnp.float32
     ).astype(jnp.bfloat16)[None]
     out_weight_gradient = lax.dot_general(
-        hidden_act, all_grad, (((0,), (0,)), ((), ())), preferred_element_type=jnp.float32
+        hidden_act, all_rows[:, half:], (((0,), (0,)), ((), ())), preferred_element_type=jnp.float32
     ).astype(jnp.bfloat16)[None]
-    back = swap(summed)
-    back_out, back_grad = back[:, :model_width], back[:, model_width:]
+    back = paired_swap(summed[:, :half], summed[:, half:])
+    back_out, back_grad = back[:, :half], back[:, half:]
     grad_comb = lax.dot_general(
         image_grad, back_out, (((1,), (1,)), ((), ())), preferred_element_type=jnp.float32
     )

time: 135 us -> 149 us (1.10)
  starting transfers between devices: 50.4 us -> 58.4 us
  waiting for transfers between devices: 37.2 us -> 42.4 us
  local copies, waits for them, and re-layouts: 6.42 us -> 9.05 us
  other arithmetic: 6.44 us -> 4.75 us
    all_to_all x3, starting transfers between devices: 18.4 us -> 22.2 us  [swap(): lax.all_to_all(value, ('tok', 'expert'), split_axis=0, concat_axis=0, til...]
    all_to_all x4 -> x0, other arithmetic: 3.09 us -> none  [swap(): lax.all_to_all(value, ('tok', 'expert'), split_axis=0, concat_axis=0, til...]
    ppermute x16, waiting for transfers between devices: 17 us -> 19.7 us  [shift(): lax.ppermute(value, 'dp', [(i, (i + step) % size) for i in range(size)])]
    all_to_all x1, starting transfers between devices: 5.23 us -> 7.38 us  [sum_everywhere(): seen = lax.all_to_all(copies, 'dp', split_axis=0, concat_axis=0, tiled=True)]
    ppermute x16, starting transfers between devices: 26.8 us -> 28.8 us  [shift(): lax.ppermute(value, 'dp', [(i, (i + step) % size) for i in range(size)])]
    dot_general x6 -> x10, matrix products: 9.15 us -> 10.4 us  [the longest x1 3.11 us: body(): lax.dot_general(all_rows[:, :half], grad_pre, (((0,), (0,)), ((), ())), p...]
    unnamed x27 -> x25, local copies, waits for them, and re-layouts: 3.57 us -> 4.33 us
  transfers between devices with their start and end apart: 20 -> 20, of which waited for: 11 -> 12; matrix products, arithmetic and copies ran while one was open for 8% -> 11% of each run, Pallas kernels for 0% -> 0%
where the time goes in v3:
time: 149 us; the launch traced here: 148 us
  starting transfers between devices  58.4 us (39%)
  waiting for transfers between devices  42.4 us (28%)
  matrix products  16.3 us (11%)
  blocking collectives  16.2 us (11%)
  local copies, waits for them, and re-layouts  9.05 us (6%)
  other arithmetic  4.75 us (3%)
    ppermute x16, starting transfers between devices, shift(): lax.ppermute(value, 'dp', [(i, (i + step) % size) for i in range(size)])  28.8 us
    all_to_all x3, starting transfers between devices, swap(): lax.all_to_all(value, ('tok', 'expert'), split_axis=0, concat_axis=0, til...  22.2 us
    ppermute x16, waiting for transfers between devices, shift(): lax.ppermute(value, 'dp', [(i, (i + step) % size) for i in range(size)])  19.7 us
    all_to_all x1, blocking collectives, swap(): lax.all_to_all(value, ('tok', 'expert'), split_axis=0, concat_axis=0, til...  16.2 us
    all_to_all x3, waiting for transfers between devices, swap(): lax.all_to_all(value, ('tok', 'expert'), split_axis=0, concat_axis=0, til...  16.2 us
    all_to_all x1, starting transfers between devices, sum_everywhere(): seen = lax.all_to_all(copies, 'dp', split_axis=0, concat_axis=0, tiled=True)  7.38 us
    all_to_all x1, waiting for transfers between devices, sum_everywhere(): seen = lax.all_to_all(copies, 'dp', split_axis=0, concat_axis=0, tiled=True)  6.52 us
    unnamed x25, local copies, waits for them, and re-layouts  4.33 us
  transfers between devices with their start and end apart: 20, of which 12 were waited for; matrix products, arithmetic and copies ran while one was open for 11% of the time, Pallas kernels for 0%

profile of v3, /device:TPU:1, one launch (start us, length us, event | category | flops | bytes accessed | tf_op | source)
XLA Modules:
  0.0 148.2 jit_solution(18049580773502965165)
XLA Ops:
  0.7 1.6 %fusion.94 = (f32[256]{0:T(256)S(1)}, f32[256,32]{0,1:T(8,128)S(1)}) fusion(bf16[1280,32]{0,1:T(8,128)(2,1)} %param.6, bf16[1,256,1280]{2,1,0:T(8,128)(2,1)} %param.5), kind=kOutput, calls=%fused_computation.176 | convolution fusion | flops 20979456 | bytes 771072 | tf_op jit(solution)/shard_map/dot_general | solution.py:87
  4.4 1.4 fusion.4
  5.7 0.2 fusion.5
  6.2 16.2 %all_to_all.34 = bf16[32,2,1280]{2,1,0:T(2,128)(2,1)S(1)} all-to-all(bf16[32,2,1280]{2,1,0:T(2,128)(2,1)S(1)} %copy.27), channel_id=1, replica_groups=mesh['dp'=8,'tok'=2,'expert'=16] {'tok','expert'}, dimensions={0} | all-to-all | bytes 327680 | tf_op jit(solution)/shard_map/all_to_all | solution.py:51
  22.4 0.2 fusion.93
  22.6 0.7 constant_dynamic-update-slice_fusion.10
  23.3 3.0 %collective-permute-start.2 = (bf16[32,2560]{1,0:T(8,128)(2,1)S(1)}, bf16[32,2560]{1,0:T(8,128)(2,1)S(1)}, u32[]{:S(2)}, u32[]{:S(2)}) collective-permute-start(bf16[32,2560]{1,0:T(8,128)(2,1)S(1)} %get-tuple-element.46), channel_id=1, source_target_pairs={{0,64},{32,96},{64,128},{96,160},{128,192},{160,224},{192,0},{224,... | collective-permute-start | bytes 491528 | tf_op jit(solution)/shard_map/ppermute | solution.py:47
  26.3 3.0 %collective-permute-start.3 = (bf16[32,2560]{1,0:T(8,128)(2,1)S(1)}, bf16[32,2560]{1,0:T(8,128)(2,1)S(1)}, u32[]{:S(2)}, u32[]{:S(2)}) collective-permute-start(bf16[32,2560]{1,0:T(8,128)(2,1)S(1)} %get-tuple-element.46), channel_id=1, source_target_pairs={{0,192},{32,224},{64,0},{96,32},{128,64},{160,96},{192,128},{224,1... | collective-permute-start | bytes 491528 | tf_op jit(solution)/shard_map/ppermute | solution.py:47
  29.4 0.7 collective-permute-start
  30.1 1.9 %collective-permute-start.1 = (bf16[32,2560]{1,0:T(8,128)(2,1)S(1)}, bf16[32,2560]{1,0:T(8,128)(2,1)S(1)}, u32[]{:S(2)}, u32[]{:S(2)}) collective-permute-start(bf16[32,2560]{1,0:T(8,128)(2,1)S(1)} %get-tuple-element.46), channel_id=1, source_target_pairs={{0,224},{32,0},{64,32},{96,64},{128,96},{160,128},{192,160},{224,1... | collective-permute-start | bytes 491528 | tf_op jit(solution)/shard_map/ppermute | solution.py:47
  32.0 2.0 %collective-permute-done.2 = bf16[32,2560]{1,0:T(8,128)(2,1)S(1)} collective-permute-done((bf16[32,2560]{1,0:T(8,128)(2,1)S(1)}, bf16[32,2560]{1,0:T(8,128)(2,1)S(1)}, u32[]{:S(2)}, u32[]{:S(2)}) %collective-permute-start.2) | collective-permute-done | bytes 163872 | tf_op jit(solution)/shard_map/ppermute | solution.py:47
  34.0 3.6 %collective-permute-start.6 = (bf16[32,1280]{1,0:T(8,128)(2,1)S(1)}, bf16[32,1280]{1,0:T(8,128)(2,1)S(1)}, u32[]{:S(2)}, u32[]{:S(2)}) collective-permute-start(bf16[32,1280]{1,0:T(8,128)(2,1)S(1)} %slice.158), channel_id=1, source_target_pairs={{0,64},{32,96},{64,128},{96,160},{128,192},{160,224},{192,0},{224,... | collective-permute-start | bytes 245768 | tf_op jit(solution)/shard_map/ppermute | solution.py:47
  37.6 0.7 collective-permute-done.3
  38.2 2.2 %collective-permute-start.7 = (bf16[32,1280]{1,0:T(8,128)(2,1)S(1)}, bf16[32,1280]{1,0:T(8,128)(2,1)S(1)}, u32[]{:S(2)}, u32[]{:S(2)}) collective-permute-start(bf16[32,1280]{1,0:T(8,128)(2,1)S(1)} %slice.159), channel_id=1, source_target_pairs={{0,192},{32,224},{64,0},{96,32},{128,64},{160,96},{192,128},{224,1... | collective-permute-start | bytes 245768 | tf_op jit(solution)/shard_map/ppermute | solution.py:47
  40.5 0.7 constant_dynamic-update-slice_fusion.9
  41.3 0.7 constant_dynamic-update-slice_fusion.8
  42.0 0.7 constant_dynamic-update-slice_fusion.7
  42.7 0.7 constant_dynamic-update-slice_fusion.6
  43.4 0.5 multiply_convert_fusion
  43.9 0.9 copy-done.2
  44.8 0.7 fusion.23
  45.5 0.6 fusion.95
  46.2 0.5 fusion.96
  46.8 0.9 collective-permute-start.4
  47.8 1.8 %collective-permute-start.5 = (bf16[32,2560]{1,0:T(8,128)(2,1)S(1)}, bf16[32,2560]{1,0:T(8,128)(2,1)S(1)}, u32[]{:S(2)}, u32[]{:S(2)}) collective-permute-start(bf16[32,2560]{1,0:T(8,128)(2,1)S(1)} %collective-permute-done.3), channel_id=1, source_target_pairs={{0,224},{32,0},{64,32},{96,64},{128,96},{160,128},{192,160},{224,1... | collective-permute-start | bytes 491528 | tf_op jit(solution)/shard_map/ppermute | solution.py:47
  49.6 2.7 %collective-permute-done.4 = bf16[32,2560]{1,0:T(8,128)(2,1)S(1)} collective-permute-done((bf16[32,2560]{1,0:T(8,128)(2,1)S(1)}, bf16[32,2560]{1,0:T(8,128)(2,1)S(1)}, u32[]{:S(2)}, u32[]{:S(2)}) %collective-permute-start.4) | collective-permute-done | bytes 163872 | tf_op jit(solution)/shard_map/ppermute | solution.py:47
  52.3 2.7 %collective-permute-start.8 = (bf16[32,2560]{1,0:T(8,128)(2,1)S(1)}, bf16[32,2560]{1,0:T(8,128)(2,1)S(1)}, u32[]{:S(2)}, u32[]{:S(2)}) collective-permute-start(bf16[32,2560]{1,0:T(8,128)(2,1)S(1)} %pad_maximum_fusion.2), channel_id=1, source_target_pairs={{0,224},{32,0},{64,32},{96,64},{128,96},{160,128},{192,160},{224,1... | collective-permute-start | bytes 491528 | tf_op jit(solution)/shard_map/ppermute | solution.py:47
  55.1 0.4 multiply_convert_fusion.1
  55.5 0.6 fusion.29
  56.2 0.6 convolution_convert_fusion.2
  56.8 2.8 %collective-permute-start.14 = (bf16[32,1280]{1,0:T(8,128)(2,1)S(1)}, bf16[32,1280]{1,0:T(8,128)(2,1)S(1)}, u32[]{:S(2)}, u32[]{:S(2)}) collective-permute-start(bf16[32,1280]{1,0:T(8,128)(2,1)S(1)} %get-tuple-element.34), channel_id=1, source_target_pairs={{0,64},{32,96},{64,128},{96,160},{128,192},{160,224},{192,0},{224,... | collective-permute-start | bytes 245768 | tf_op jit(solution)/shard_map/ppermute | solution.py:47
  59.6 0.4 convolution_convert_fusion.3
  60.1 0.9 collective-permute-start.11
  61.0 1.5 %collective-permute-start.10 = (bf16[32,2560]{1,0:T(8,128)(2,1)S(1)}, bf16[32,2560]{1,0:T(8,128)(2,1)S(1)}, u32[]{:S(2)}, u32[]{:S(2)}) collective-permute-start(bf16[32,2560]{1,0:T(8,128)(2,1)S(1)} %pad_maximum_fusion.4), channel_id=1, source_target_pairs={{0,224},{32,0},{64,32},{96,64},{128,96},{160,128},{192,160},{224,1... | collective-permute-start | bytes 491528 | tf_op jit(solution)/shard_map/ppermute | solution.py:47
  62.5 4.4 %collective-permute-done.10 = bf16[32,2560]{1,0:T(8,128)(2,1)S(1)} collective-permute-done((bf16[32,2560]{1,0:T(8,128)(2,1)S(1)}, bf16[32,2560]{1,0:T(8,128)(2,1)S(1)}, u32[]{:S(2)}, u32[]{:S(2)}) %collective-permute-start.10) | collective-permute-done | bytes 163872 | tf_op jit(solution)/shard_map/ppermute | solution.py:47
  67.0 1.0 collective-permute-start.13
  68.0 4.3 %collective-permute-done.13 = bf16[32,2560]{1,0:T(8,128)(2,1)S(1)} collective-permute-done((bf16[32,2560]{1,0:T(8,128)(2,1)S(1)}, bf16[32,2560]{1,0:T(8,128)(2,1)S(1)}, u32[]{:S(2)}, u32[]{:S(2)}) %collective-permute-start.13) | collective-permute-done | bytes 163872 | tf_op jit(solution)/shard_map/ppermute | solution.py:47
  72.4 0.6 collective-permute-start.12
  73.0 2.0 %collective-permute-start.15 = (bf16[32,2560]{1,0:T(8,128)(2,1)S(1)}, bf16[32,2560]{1,0:T(8,128)(2,1)S(1)}, u32[]{:S(2)}, u32[]{:S(2)}) collective-permute-start(bf16[32,2560]{1,0:T(8,128)(2,1)S(1)} %pad_maximum_fusion.7), channel_id=1, source_target_pairs={{0,64},{32,96},{64,128},{96,160},{128,192},{160,224},{192,0},{224,... | collective-permute-start | bytes 491528 | tf_op jit(solution)/shard_map/ppermute | solution.py:47
  75.0 0.8 constant_dynamic-update-slice_fusion.5
  75.8 3.5 %collective-permute-done.12 = bf16[32,2560]{1,0:T(8,128)(2,1)S(1)} collective-permute-done((bf16[32,2560]{1,0:T(8,128)(2,1)S(1)}, bf16[32,2560]{1,0:T(8,128)(2,1)S(1)}, u32[]{:S(2)}, u32[]{:S(2)}) %collective-permute-start.12) | collective-permute-done | bytes 163872 | tf_op jit(solution)/shard_map/ppermute | solution.py:47
  79.3 2.0 %collective-permute-done.15 = bf16[32,2560]{1,0:T(8,128)(2,1)S(1)} collective-permute-done((bf16[32,2560]{1,0:T(8,128)(2,1)S(1)}, bf16[32,2560]{1,0:T(8,128)(2,1)S(1)}, u32[]{:S(2)}, u32[]{:S(2)}) %collective-permute-start.15) | collective-permute-done | bytes 163872 | tf_op jit(solution)/shard_map/ppermute | solution.py:47
  81.4 0.8 copy.30
  82.3 12.3 %all-to-all-start.1 = ((bf16[32,2,1280]{2,1,0:T(2,128)(2,1)}), bf16[32,2,1280]{2,1,0:T(2,128)(2,1)S(1)}, u32[]{:S(2)}, u32[]{:S(2)}) async-start(bf16[32,2,1280]{2,1,0:T(2,128)(2,1)} %copy.30), calls=%async_computation.1 | async-start | bytes 327680 | tf_op jit(solution)/shard_map/all_to_all | solution.py:51
  94.6 3.1 %fusion = bf16[1,1280,640]{2,1,0:T(8,128)(2,1)} fusion(bf16[256,2560]{1,0:T(8,128)(2,1)} %constant_dynamic-update-slice_fusion.5, bf16[96,640]{1,0:T(8,128)(2,1)} %copy-done.7, bf16[160,640]{1,0:T(8,128)(2,1)} %copy-done.4), kind=kOutput, calls=%fused_computation.2 | convolution fusion | flops 420904960 | bytes 2621440 | tf_op jit(solution)/shard_map/dot_general | solution.py:141
  97.7 4.7 %all-to-all-done.1 = bf16[32,2,1280]{2,1,0:T(2,128)(2,1)S(1)} async-done(((bf16[32,2,1280]{2,1,0:T(2,128)(2,1)}), bf16[32,2,1280]{2,1,0:T(2,128)(2,1)S(1)}, u32[]{:S(2)}, u32[]{:S(2)}) %all-to-all-start.1) | async-done | bytes 163872 | tf_op jit(solution)/shard_map/all_to_all | solution.py:51
  102.4 0.2 fusion.92
  102.6 0.4 fusion.97
  103.9 0.4 multiply_reduce_fusion
  104.3 0.7 add_convert_fusion
  105.0 0.2 convolution_bitcast_fusion
  105.2 0.8 copy.33
  106.1 4.3 %all-to-all-start.2 = ((f32[32,1,1280]{2,1,0:T(1,128)}), f32[32,1,1280]{2,1,0:T(1,128)S(1)}, u32[]{:S(2)}, u32[]{:S(2)}) async-start(f32[32,1,1280]{2,1,0:T(1,128)} %copy.33), calls=%async_computation.2 | async-start | bytes 327680 | tf_op jit(solution)/shard_map/all_to_all | solution.py:51
  110.4 2.9 %fusion.1 = bf16[1,640,1280]{2,1,0:T(8,128)(2,1)} fusion(bf16[256,2560]{1,0:T(8,128)(2,1)} %constant_dynamic-update-slice_fusion.5, bf16[96,640]{1,0:T(8,128)(2,1)S(1)} %get-tuple-element.61, bf16[160,640]{1,0:T(8,128)(2,1)S(1)} %get-tuple-element.55), kind=kOutput, calls=%fused_computation.3 | convolution fusion | flops 420904960 | bytes 2621440 | tf_op jit(solution)/shard_map/dot_general | solution.py:144
  113.3 4.9 %all-to-all-done.2 = f32[32,1,1280]{2,1,0:T(1,128)S(1)} async-done(((f32[32,1,1280]{2,1,0:T(1,128)}), f32[32,1,1280]{2,1,0:T(1,128)S(1)}, u32[]{:S(2)}, u32[]{:S(2)}) %all-to-all-start.2) | async-done | bytes 163872 | tf_op jit(solution)/shard_map/all_to_all | solution.py:51
  118.3 0.6 broadcast_in_dim.11
  119.0 7.4 %all-to-all-start.3 = ((f32[8,1,1280]{2,1,0:T(1,128)}), f32[8,1,1280]{2,1,0:T(1,128)S(1)}, u32[]{:S(2)}, u32[]{:S(2)}) async-start(f32[8,1,1280]{2,1,0:T(1,128)} %broadcast_in_dim.11), calls=%async_computation.3 | async-start | bytes 81920 | tf_op jit(solution)/shard_map/all_to_all | solution.py:58
  126.3 0.4 fusion.66
  126.8 6.5 %all-to-all-done.3 = f32[8,1,1280]{2,1,0:T(1,128)S(1)} async-done(((f32[8,1,1280]{2,1,0:T(1,128)}), f32[8,1,1280]{2,1,0:T(1,128)S(1)}, u32[]{:S(2)}, u32[]{:S(2)}) %all-to-all-start.3) | async-done | bytes 40992 | tf_op jit(solution)/shard_map/all_to_all | solution.py:58
  133.3 0.8 broadcast_in_dim.12
  134.1 5.6 %all-to-all-start.4 = ((f32[32,1,1280]{2,1,0:T(1,128)}), f32[32,1,1280]{2,1,0:T(1,128)S(1)}, u32[]{:S(2)}, u32[]{:S(2)}) async-start(f32[32,1,1280]{2,1,0:T(1,128)} %broadcast_in_dim.12), calls=%async_computation.4 | async-start | bytes 327680 | tf_op jit(solution)/shard_map/all_to_all | solution.py:51
  139.7 1.2 fusion.3
  140.9 6.6 %all-to-all-done.4 = f32[32,1,1280]{2,1,0:T(1,128)S(1)} async-done(((f32[32,1,1280]{2,1,0:T(1,128)}), f32[32,1,1280]{2,1,0:T(1,128)S(1)}, u32[]{:S(2)}, u32[]{:S(2)}) %all-to-all-start.4) | async-done | bytes 163872 | tf_op jit(solution)/shard_map/all_to_all | solution.py:51
  147.5 0.7 copy.53
  (95 shorter events, 4.0 us)
Async XLA Ops:
  0.6 42.7 %copy-start = (bf16[1,1280,640]{2,1,0:T(8,128)(2,1)S(1)}, bf16[1,1280,640]{2,1,0:T(8,128)(2,1)}, u32[]{:S(2)}) copy-start(bf16[1,1280,640]{2,1,0:T(8,128)(2,1)} %param.7) | copy-start | bytes 4915204
  0.6 5.1 %copy-start.3 = (bf16[1,256,1280]{2,1,0:T(8,128)(2,1)S(1)}, bf16[1,256,1280]{2,1,0:T(8,128)(2,1)}, u32[]{:S(2)}) copy-start(bf16[1,256,1280]{2,1,0:T(8,128)(2,1)} %param.9) | copy-start | bytes 1966084
  3.2 100.7 %copy-start.9 = (f32[256]{0:T(256)}, f32[256]{0:T(256)S(1)}, u32[]{:S(2)}) copy-start(f32[256]{0:T(256)S(1)} %get-tuple-element.13) | copy-start | bytes 3076
  23.3 10.7 %collective-permute-start.2 = (bf16[32,2560]{1,0:T(8,128)(2,1)S(1)}, bf16[32,2560]{1,0:T(8,128)(2,1)S(1)}, u32[]{:S(2)}, u32[]{:S(2)}) collective-permute-start(bf16[32,2560]{1,0:T(8,128)(2,1)S(1)} %get-tuple-element.46), channel_id=1, source_target_pairs={{0,64},{32,96},{64,128},{96,160},{128,192},{160,224},{192,0},{224,... | collective-permute-start | bytes 491528 | tf_op jit(solution)/shard_map/ppermute | solution.py:47
  26.3 11.9 %collective-permute-start.3 = (bf16[32,2560]{1,0:T(8,128)(2,1)S(1)}, bf16[32,2560]{1,0:T(8,128)(2,1)S(1)}, u32[]{:S(2)}, u32[]{:S(2)}) collective-permute-start(bf16[32,2560]{1,0:T(8,128)(2,1)S(1)} %get-tuple-element.46), channel_id=1, source_target_pairs={{0,192},{32,224},{64,0},{96,32},{128,64},{160,96},{192,128},{224,1... | collective-permute-start | bytes 491528 | tf_op jit(solution)/shard_map/ppermute | solution.py:47
  29.4 11.1 %collective-permute-start = (bf16[32,2560]{1,0:T(8,128)(2,1)S(1)}, bf16[32,2560]{1,0:T(8,128)(2,1)S(1)}, u32[]{:S(2)}, u32[]{:S(2)}) collective-permute-start(bf16[32,2560]{1,0:T(8,128)(2,1)S(1)} %get-tuple-element.46), channel_id=1, source_target_pairs={{0,32},{32,64},{64,96},{96,128},{128,160},{160,192},{192,224},{224... | collective-permute-start | bytes 491528 | tf_op jit(solution)/shard_map/ppermute | solution.py:47
  30.1 11.2 %collective-permute-start.1 = (bf16[32,2560]{1,0:T(8,128)(2,1)S(1)}, bf16[32,2560]{1,0:T(8,128)(2,1)S(1)}, u32[]{:S(2)}, u32[]{:S(2)}) collective-permute-start(bf16[32,2560]{1,0:T(8,128)(2,1)S(1)} %get-tuple-element.46), channel_id=1, source_target_pairs={{0,224},{32,0},{64,32},{96,64},{128,96},{160,128},{192,160},{224,1... | collective-permute-start | bytes 491528 | tf_op jit(solution)/shard_map/ppermute | solution.py:47
  34.0 15.6 %collective-permute-start.6 = (bf16[32,1280]{1,0:T(8,128)(2,1)S(1)}, bf16[32,1280]{1,0:T(8,128)(2,1)S(1)}, u32[]{:S(2)}, u32[]{:S(2)}) collective-permute-start(bf16[32,1280]{1,0:T(8,128)(2,1)S(1)} %slice.158), channel_id=1, source_target_pairs={{0,64},{32,96},{64,128},{96,160},{128,192},{160,224},{192,0},{224,... | collective-permute-start | bytes 245768 | tf_op jit(solution)/shard_map/ppermute | solution.py:47
  38.2 11.4 %collective-permute-start.7 = (bf16[32,1280]{1,0:T(8,128)(2,1)S(1)}, bf16[32,1280]{1,0:T(8,128)(2,1)S(1)}, u32[]{:S(2)}, u32[]{:S(2)}) collective-permute-start(bf16[32,1280]{1,0:T(8,128)(2,1)S(1)} %slice.159), channel_id=1, source_target_pairs={{0,192},{32,224},{64,0},{96,32},{128,64},{160,96},{192,128},{224,1... | collective-permute-start | bytes 245768 | tf_op jit(solution)/shard_map/ppermute | solution.py:47
  43.4 1.4 copy-start.2
  45.5 6.8 %copy-start.4 = (bf16[160,640]{1,0:T(8,128)(2,1)}, bf16[160,640]{1,0:T(8,128)(2,1)S(1)}, u32[]{:S(2)}) copy-start(bf16[160,640]{1,0:T(8,128)(2,1)S(1)} %fusion.23) | copy-start | bytes 614404
  46.8 5.5 %collective-permute-start.4 = (bf16[32,2560]{1,0:T(8,128)(2,1)S(1)}, bf16[32,2560]{1,0:T(8,128)(2,1)S(1)}, u32[]{:S(2)}, u32[]{:S(2)}) collective-permute-start(bf16[32,2560]{1,0:T(8,128)(2,1)S(1)} %collective-permute-done.2), channel_id=1, source_target_pairs={{0,32},{32,64},{64,96},{96,128},{128,160},{160,192},{192,224},{224... | collective-permute-start | bytes 491528 | tf_op jit(solution)/shard_map/ppermute | solution.py:47
  47.8 4.5 %collective-permute-start.5 = (bf16[32,2560]{1,0:T(8,128)(2,1)S(1)}, bf16[32,2560]{1,0:T(8,128)(2,1)S(1)}, u32[]{:S(2)}, u32[]{:S(2)}) collective-permute-start(bf16[32,2560]{1,0:T(8,128)(2,1)S(1)} %collective-permute-done.3), channel_id=1, source_target_pairs={{0,224},{32,0},{64,32},{96,64},{128,96},{160,128},{192,160},{224,1... | collective-permute-start | bytes 491528 | tf_op jit(solution)/shard_map/ppermute | solution.py:47
  52.3 23.5 %collective-permute-start.8 = (bf16[32,2560]{1,0:T(8,128)(2,1)S(1)}, bf16[32,2560]{1,0:T(8,128)(2,1)S(1)}, u32[]{:S(2)}, u32[]{:S(2)}) collective-permute-start(bf16[32,2560]{1,0:T(8,128)(2,1)S(1)} %pad_maximum_fusion.2), channel_id=1, source_target_pairs={{0,224},{32,0},{64,32},{96,64},{128,96},{160,128},{192,160},{224,1... | collective-permute-start | bytes 491528 | tf_op jit(solution)/shard_map/ppermute | solution.py:47
  55.1 20.7 %collective-permute-start.9 = (bf16[32,2560]{1,0:T(8,128)(2,1)S(1)}, bf16[32,2560]{1,0:T(8,128)(2,1)S(1)}, u32[]{:S(2)}, u32[]{:S(2)}) collective-permute-start(bf16[32,2560]{1,0:T(8,128)(2,1)S(1)} %pad_maximum_fusion.3), channel_id=1, source_target_pairs={{0,32},{32,64},{64,96},{96,128},{128,160},{160,192},{192,224},{224... | collective-permute-start | bytes 491528 | tf_op jit(solution)/shard_map/ppermute | solution.py:47
  56.2 19.6 %copy-start.7 = (bf16[96,640]{1,0:T(8,128)(2,1)}, bf16[96,640]{1,0:T(8,128)(2,1)S(1)}, u32[]{:S(2)}) copy-start(bf16[96,640]{1,0:T(8,128)(2,1)S(1)} %fusion.29) | copy-start | bytes 368644
  56.8 16.2 %collective-permute-start.14 = (bf16[32,1280]{1,0:T(8,128)(2,1)S(1)}, bf16[32,1280]{1,0:T(8,128)(2,1)S(1)}, u32[]{:S(2)}, u32[]{:S(2)}) collective-permute-start(bf16[32,1280]{1,0:T(8,128)(2,1)S(1)} %get-tuple-element.34), channel_id=1, source_target_pairs={{0,64},{32,96},{64,128},{96,160},{128,192},{160,224},{192,0},{224,... | collective-permute-start | bytes 245768 | tf_op jit(solution)/shard_map/ppermute | solution.py:47
  60.1 7.9 %collective-permute-start.11 = (bf16[32,1280]{1,0:T(8,128)(2,1)S(1)}, bf16[32,1280]{1,0:T(8,128)(2,1)S(1)}, u32[]{:S(2)}, u32[]{:S(2)}) collective-permute-start(bf16[32,1280]{1,0:T(8,128)(2,1)S(1)} %get-tuple-element.30), channel_id=1, source_target_pairs={{0,192},{32,224},{64,0},{96,32},{128,64},{160,96},{192,128},{224,1... | collective-permute-start | bytes 245768 | tf_op jit(solution)/shard_map/ppermute | solution.py:47
  61.0 6.0 %collective-permute-start.10 = (bf16[32,2560]{1,0:T(8,128)(2,1)S(1)}, bf16[32,2560]{1,0:T(8,128)(2,1)S(1)}, u32[]{:S(2)}, u32[]{:S(2)}) collective-permute-start(bf16[32,2560]{1,0:T(8,128)(2,1)S(1)} %pad_maximum_fusion.4), channel_id=1, source_target_pairs={{0,224},{32,0},{64,32},{96,64},{128,96},{160,128},{192,160},{224,1... | collective-permute-start | bytes 491528 | tf_op jit(solution)/shard_map/ppermute | solution.py:47
  67.0 5.4 %collective-permute-start.13 = (bf16[32,2560]{1,0:T(8,128)(2,1)S(1)}, bf16[32,2560]{1,0:T(8,128)(2,1)S(1)}, u32[]{:S(2)}, u32[]{:S(2)}) collective-permute-start(bf16[32,2560]{1,0:T(8,128)(2,1)S(1)} %pad_maximum_fusion.6), channel_id=1, source_target_pairs={{0,32},{32,64},{64,96},{96,128},{128,160},{160,192},{192,224},{224... | collective-permute-start | bytes 491528 | tf_op jit(solution)/shard_map/ppermute | solution.py:47
  72.4 6.9 %collective-permute-start.12 = (bf16[32,2560]{1,0:T(8,128)(2,1)S(1)}, bf16[32,2560]{1,0:T(8,128)(2,1)S(1)}, u32[]{:S(2)}, u32[]{:S(2)}) collective-permute-start(bf16[32,2560]{1,0:T(8,128)(2,1)S(1)} %pad_maximum_fusion.5), channel_id=1, source_target_pairs={{0,192},{32,224},{64,0},{96,32},{128,64},{160,96},{192,128},{224,1... | collective-permute-start | bytes 491528 | tf_op jit(solution)/shard_map/ppermute | solution.py:47
  73.0 8.3 %collective-permute-start.15 = (bf16[32,2560]{1,0:T(8,128)(2,1)S(1)}, bf16[32,2560]{1,0:T(8,128)(2,1)S(1)}, u32[]{:S(2)}, u32[]{:S(2)}) collective-permute-start(bf16[32,2560]{1,0:T(8,128)(2,1)S(1)} %pad_maximum_fusion.7), channel_id=1, source_target_pairs={{0,64},{32,96},{64,128},{96,160},{128,192},{160,224},{192,0},{224,... | collective-permute-start | bytes 491528 | tf_op jit(solution)/shard_map/ppermute | solution.py:47
  82.3 20.1 %all-to-all-start.1 = ((bf16[32,2,1280]{2,1,0:T(2,128)(2,1)}), bf16[32,2,1280]{2,1,0:T(2,128)(2,1)S(1)}, u32[]{:S(2)}, u32[]{:S(2)}) async-start(bf16[32,2,1280]{2,1,0:T(2,128)(2,1)} %copy.30), calls=%async_computation.1 | async-start | bytes 327680 | tf_op jit(solution)/shard_map/all_to_all | solution.py:51
  94.6 8.1 %copy-start.1 = (bf16[1,256,1280]{2,1,0:T(8,128)(2,1)S(1)}, bf16[1,256,1280]{2,1,0:T(8,128)(2,1)}, u32[]{:S(2)}) copy-start(bf16[1,256,1280]{2,1,0:T(8,128)(2,1)} %param.5) | copy-start | bytes 1966084
  102.6 2.6 %copy-start.5 = (bf16[32,1,1280]{2,1,0:T(2,128)(2,1)}, bf16[32,1,1280]{2,1,0:T(2,128)(2,1)S(1)}, u32[]{:S(2)}) copy-start(bf16[32,1,1280]{2,1,0:T(2,128)(2,1)S(1)} %get-tuple-element.48) | copy-start | bytes 245764
  106.1 20.3 %copy-start.6 = (bf16[32,1,1280]{2,1,0:T(2,128)(2,1)S(1)}, bf16[32,1,1280]{2,1,0:T(2,128)(2,1)}, u32[]{:S(2)}) copy-start(bf16[32,1,1280]{2,1,0:T(2,128)(2,1)} %copy-done.5) | copy-start | bytes 245764
  106.1 12.1 %all-to-all-start.2 = ((f32[32,1,1280]{2,1,0:T(1,128)}), f32[32,1,1280]{2,1,0:T(1,128)S(1)}, u32[]{:S(2)}, u32[]{:S(2)}) async-start(f32[32,1,1280]{2,1,0:T(1,128)} %copy.33), calls=%async_computation.2 | async-start | bytes 327680 | tf_op jit(solution)/shard_map/all_to_all | solution.py:51
  113.3 26.4 %copy-start.8 = (bf16[1280,32]{0,1:T(8,128)(2,1)S(1)}, bf16[1280,32]{0,1:T(8,128)(2,1)}, u32[]{:S(2)}) copy-start(bf16[1280,32]{0,1:T(8,128)(2,1)} %param.6) | copy-start | bytes 245764
  119.0 14.3 %all-to-all-start.3 = ((f32[8,1,1280]{2,1,0:T(1,128)}), f32[8,1,1280]{2,1,0:T(1,128)S(1)}, u32[]{:S(2)}, u32[]{:S(2)}) async-start(f32[8,1,1280]{2,1,0:T(1,128)} %broadcast_in_dim.11), calls=%async_computation.3 | async-start | bytes 81920 | tf_op jit(solution)/shard_map/all_to_all | solution.py:58
  134.1 13.4 %all-to-all-start.4 = ((f32[32,1,1280]{2,1,0:T(1,128)}), f32[32,1,1280]{2,1,0:T(1,128)S(1)}, u32[]{:S(2)}, u32[]{:S(2)}) async-start(f32[32,1,1280]{2,1,0:T(1,128)} %broadcast_in_dim.12), calls=%async_computation.4 | async-start | bytes 327680 | tf_op jit(solution)/shard_map/all_to_all | solution.py:51

commit v4 on v2

--- a/solution.py
+++ b/solution.py
@@ -86,6 +86,11 @@
     return swap(jnp.broadcast_to(jnp.sum(seen, axis=0, keepdims=True), (slots, width)))
 
 
+def paired_swap(first, second):
+    moved = swap(jnp.stack([first, second], axis=1))
+    return jnp.concatenate([moved[:, 0], moved[:, 1]], axis=1)
+
+
 def body(tokens, router, expert_in, expert_out, grad_out):
     patches, image_grad = tokens[0], grad_out[0]
     model_width = patches.shape[1]
@@ -101,7 +106,7 @@
     grad_part = jnp.dot(combine_rounded.T, image_grad, preferred_element_type=jnp.float32).astype(
         jnp.bfloat16
     )
-    rows = swap(jnp.concatenate([slot_part, grad_part], axis=1))
+    rows = paired_swap(slot_part, grad_part)
     gathered = gather_blocks(rows)
     all_in, all_grad = gathered[:, :model_width], gathered[:, model_width:]
     weight_in = expert_in[0]
@@ -126,7 +131,7 @@
     out_weight_gradient = lax.dot_general(
         hidden_act, all_grad, (((0,), (0,)), ((), ())), preferred_element_type=jnp.float32
     ).astype(jnp.bfloat16)[None]
-    back = swap(summed)
+    back = paired_swap(summed[:, :model_width], summed[:, model_width:])
     back_out, back_grad = back[:, :model_width], back[:, model_width:]
     grad_comb = lax.dot_general(
         image_grad, back_out, (((1,), (1,)), ((), ())), preferred_element_type=jnp.float32

time: 135 us -> 130 us (0.963)
  other arithmetic: 6.44 us -> 3.53 us
  local copies, waits for them, and re-layouts: 6.42 us -> 4.68 us
    all_to_all x4 -> x0, other arithmetic: 3.09 us -> none  [swap(): lax.all_to_all(value, ('tok', 'expert'), split_axis=0, concat_axis=0, til...]
    unnamed x27 -> x25, local copies, waits for them, and re-layouts: 3.57 us -> 0.84 us
where the time goes in v4:
time: 130 us; the launch traced here: 129 us
  starting transfers between devices  50.4 us (39%)
  waiting for transfers between devices  37.2 us (29%)
  matrix products  16.3 us (13%)
  blocking collectives  16.2 us (12%)
  local copies, waits for them, and re-layouts  4.68 us (4%)
  other arithmetic  3.53 us (3%)
    ppermute x16, starting transfers between devices, shift(): lax.ppermute(value, 'dp', [(i, (i + step) % size) for i in range(size)])  26.8 us
    all_to_all x3, starting transfers between devices, swap(): lax.all_to_all(value, ('tok', 'expert'), split_axis=0, concat_axis=0, til...  18.4 us
    ppermute x16, waiting for transfers between devices, shift(): lax.ppermute(value, 'dp', [(i, (i + step) % size) for i in range(size)])  17 us
    all_to_all x1, blocking collectives, swap(): lax.all_to_all(value, ('tok', 'expert'), split_axis=0, concat_axis=0, til...  16.2 us
    all_to_all x3, waiting for transfers between devices, swap(): lax.all_to_all(value, ('tok', 'expert'), split_axis=0, concat_axis=0, til...  14.7 us
    all_to_all x1, waiting for transfers between devices, sum_everywhere(): seen = lax.all_to_all(copies, 'dp', split_axis=0, concat_axis=0, tiled=True)  5.46 us
    all_to_all x1, starting transfers between devices, sum_everywhere(): seen = lax.all_to_all(copies, 'dp', split_axis=0, concat_axis=0, tiled=True)  5.23 us
    dot_general x1, matrix products, body(): lax.dot_general(hidden_act, all_grad, (((0,), (0,)), ((), ())), preferred...  3.2 us
  transfers between devices with their start and end apart: 20, of which 11 were waited for; matrix products, arithmetic and copies ran while one was open for 8% of the time, Pallas kernels for 0%

profile of v4, /device:TPU:1, one launch (start us, length us, event | category | flops | bytes accessed | tf_op | source)
XLA Modules:
  0.0 129.5 jit_solution(260576972723061936)
XLA Ops:
  0.7 1.6 %fusion.69 = (f32[256]{0:T(256)S(1)}, f32[256,32]{0,1:T(8,128)S(1)}) fusion(bf16[1280,32]{0,1:T(8,128)(2,1)} %param.6, bf16[1,256,1280]{2,1,0:T(8,128)(2,1)} %param.5), kind=kOutput, calls=%fused_computation.148 | convolution fusion | flops 20979456 | bytes 771072 | tf_op jit(solution)/shard_map/dot_general | solution.py:97
  2.3 0.1 subtract_reduce_fusion.3
  2.4 0.2 exponential_reduce_fusion.6
  2.7 0.1 exponential_reduce_fusion.5
  2.9 0.2 subtract_reduce_fusion.2
  3.1 0.2 exponential_reduce_fusion.4
  3.4 0.1 subtract_reduce_fusion.1
  3.5 0.2 exponential_reduce_fusion.2
  3.9 0.1 exponential_reduce_fusion.1
  4.0 0.2 subtract_reduce_fusion
  4.2 0.2 exponential_reduce_fusion
  4.4 0.3 fusion.5
  4.7 0.2 fusion.6
  4.9 0.2 copy.27
  5.1 16.2 %all_to_all.34 = bf16[32,2,1280]{2,1,0:T(2,128)(2,1)S(1)} all-to-all(bf16[32,2,1280]{2,1,0:T(2,128)(2,1)S(1)} %copy.27), channel_id=1, replica_groups=mesh['dp'=8,'tok'=2,'expert'=16] {'tok','expert'}, dimensions={0} | all-to-all | bytes 327680 | tf_op jit(solution)/shard_map/all_to_all | solution.py:78
  21.3 0.2 fusion.68
  21.6 6.1 %collective-permute-start.3 = (bf16[32,2560]{1,0:T(8,128)(2,1)S(1)}, bf16[32,2560]{1,0:T(8,128)(2,1)S(1)}, u32[]{:S(2)}, u32[]{:S(2)}) collective-permute-start(bf16[32,2560]{1,0:T(8,128)(2,1)S(1)} %get-tuple-element.24), channel_id=1, source_target_pairs={{0,192},{32,224},{64,0},{96,32},{128,64},{160,96},{192,128},{224,1... | collective-permute-start | bytes 491528 | tf_op jit(solution)/shard_map/ppermute | solution.py:47
  27.7 0.7 collective-permute-start
  28.5 2.4 %collective-permute-start.1 = (bf16[32,2560]{1,0:T(8,128)(2,1)S(1)}, bf16[32,2560]{1,0:T(8,128)(2,1)S(1)}, u32[]{:S(2)}, u32[]{:S(2)}) collective-permute-start(bf16[32,2560]{1,0:T(8,128)(2,1)S(1)} %get-tuple-element.24), channel_id=1, source_target_pairs={{0,224},{32,0},{64,32},{96,64},{128,96},{160,128},{192,160},{224,1... | collective-permute-start | bytes 491528 | tf_op jit(solution)/shard_map/ppermute | solution.py:47
  30.9 3.3 %collective-permute-done.3 = bf16[32,2560]{1,0:T(8,128)(2,1)S(1)} collective-permute-done((bf16[32,2560]{1,0:T(8,128)(2,1)S(1)}, bf16[32,2560]{1,0:T(8,128)(2,1)S(1)}, u32[]{:S(2)}, u32[]{:S(2)}) %collective-permute-start.3) | collective-permute-done | bytes 163872 | tf_op jit(solution)/shard_map/ppermute | solution.py:47
  34.1 4.8 %collective-permute-start.7 = (bf16[32,1280]{1,0:T(8,128)(2,1)S(1)}, bf16[32,1280]{1,0:T(8,128)(2,1)S(1)}, u32[]{:S(2)}, u32[]{:S(2)}) collective-permute-start(bf16[32,1280]{1,0:T(8,128)(2,1)S(1)} %slice.108), channel_id=1, source_target_pairs={{0,192},{32,224},{64,0},{96,32},{128,64},{160,96},{192,128},{224,1... | collective-permute-start | bytes 245768 | tf_op jit(solution)/shard_map/ppermute | solution.py:47
  39.1 2.9 %collective-permute-done = bf16[32,2560]{1,0:T(8,128)(2,1)S(1)} collective-permute-done((bf16[32,2560]{1,0:T(8,128)(2,1)S(1)}, bf16[32,2560]{1,0:T(8,128)(2,1)S(1)}, u32[]{:S(2)}, u32[]{:S(2)}) %collective-permute-start) | collective-permute-done | bytes 163872 | tf_op jit(solution)/shard_map/ppermute | solution.py:47
  42.1 4.4 %collective-permute-done.4 = bf16[32,2560]{1,0:T(8,128)(2,1)S(1)} collective-permute-done((bf16[32,2560]{1,0:T(8,128)(2,1)S(1)}, bf16[32,2560]{1,0:T(8,128)(2,1)S(1)}, u32[]{:S(2)}, u32[]{:S(2)}) %collective-permute-start.4) | collective-permute-done | bytes 163872 | tf_op jit(solution)/shard_map/ppermute | solution.py:47
  46.6 0.2 collective-permute-done.5
  46.8 0.7 fusion.13
  47.5 0.8 fusion.9
  48.3 0.8 fusion.18
  49.2 0.7 fusion.11
  49.9 0.1 fusion.2
  50.1 2.5 %collective-permute-start.10 = (bf16[32,2560]{1,0:T(8,128)(2,1)S(1)}, bf16[32,2560]{1,0:T(8,128)(2,1)S(1)}, u32[]{:S(2)}, u32[]{:S(2)}) collective-permute-start(bf16[32,2560]{1,0:T(8,128)(2,1)S(1)} %get-tuple-element.18), channel_id=1, source_target_pairs={{0,224},{32,0},{64,32},{96,64},{128,96},{160,128},{192,160},{224,1... | collective-permute-start | bytes 491528 | tf_op jit(solution)/shard_map/ppermute | solution.py:47
  52.7 3.6 %collective-permute-start.11 = (bf16[32,1280]{1,0:T(8,128)(2,1)S(1)}, bf16[32,1280]{1,0:T(8,128)(2,1)S(1)}, u32[]{:S(2)}, u32[]{:S(2)}) collective-permute-start(bf16[32,1280]{1,0:T(8,128)(2,1)S(1)} %slice.182), channel_id=1, source_target_pairs={{0,192},{32,224},{64,0},{96,32},{128,64},{160,96},{192,128},{224,1... | collective-permute-start | bytes 245768 | tf_op jit(solution)/shard_map/ppermute | solution.py:47
  56.3 0.4 collective-permute-start.9
  56.7 2.3 %collective-permute-start.8 = (bf16[32,2560]{1,0:T(8,128)(2,1)S(1)}, bf16[32,2560]{1,0:T(8,128)(2,1)S(1)}, u32[]{:S(2)}, u32[]{:S(2)}) collective-permute-start(bf16[32,2560]{1,0:T(8,128)(2,1)S(1)} %get-tuple-element.16), channel_id=1, source_target_pairs={{0,224},{32,0},{64,32},{96,64},{128,96},{160,128},{192,160},{224,1... | collective-permute-start | bytes 491528 | tf_op jit(solution)/shard_map/ppermute | solution.py:47
  59.1 0.5 collective-permute-done.14
  59.8 3.6 %collective-permute-start.12 = (bf16[32,2560]{1,0:T(8,128)(2,1)S(1)}, bf16[32,2560]{1,0:T(8,128)(2,1)S(1)}, u32[]{:S(2)}, u32[]{:S(2)}) collective-permute-start(bf16[32,2560]{1,0:T(8,128)(2,1)S(1)} %pad_maximum_fusion.3), channel_id=1, source_target_pairs={{0,192},{32,224},{64,0},{96,32},{128,64},{160,96},{192,128},{224,1... | collective-permute-start | bytes 491528 | tf_op jit(solution)/shard_map/ppermute | solution.py:47
  63.4 1.9 %collective-permute-done.9 = bf16[32,2560]{1,0:T(8,128)(2,1)S(1)} collective-permute-done((bf16[32,2560]{1,0:T(8,128)(2,1)S(1)}, bf16[32,2560]{1,0:T(8,128)(2,1)S(1)}, u32[]{:S(2)}, u32[]{:S(2)}) %collective-permute-start.9) | collective-permute-done | bytes 163872 | tf_op jit(solution)/shard_map/ppermute | solution.py:47
  65.3 3.9 %collective-permute-done.15 = bf16[32,2560]{1,0:T(8,128)(2,1)S(1)} collective-permute-done((bf16[32,2560]{1,0:T(8,128)(2,1)S(1)}, bf16[32,2560]{1,0:T(8,128)(2,1)S(1)}, u32[]{:S(2)}, u32[]{:S(2)}) %collective-permute-start.15) | collective-permute-done | bytes 163872 | tf_op jit(solution)/shard_map/ppermute | solution.py:47
  69.3 0.8 copy.30
  70.2 8.6 %all-to-all-start.1 = ((bf16[32,2,1280]{2,1,0:T(2,128)(2,1)}), bf16[32,2,1280]{2,1,0:T(2,128)(2,1)S(1)}, u32[]{:S(2)}, u32[]{:S(2)}) async-start(bf16[32,2,1280]{2,1,0:T(2,128)(2,1)} %copy.30), calls=%async_computation.1 | async-start | bytes 327680 | tf_op jit(solution)/shard_map/all_to_all | solution.py:78
  78.8 3.2 %fusion.1 = bf16[1,640,1280]{2,1,0:T(8,128)(2,1)} fusion(bf16[256,2560]{1,0:T(8,128)(2,1)} %copy-done.5, f32[256,640]{1,0:T(8,128)} %copy-done.4), kind=kOutput, calls=%fused_computation.10 | convolution fusion | flops 421724160 | bytes 2949120 | tf_op jit(solution)/shard_map/dot_general | solution.py:131
  82.0 4.6 %all-to-all-done.1 = bf16[32,2,1280]{2,1,0:T(2,128)(2,1)S(1)} async-done(((bf16[32,2,1280]{2,1,0:T(2,128)(2,1)}), bf16[32,2,1280]{2,1,0:T(2,128)(2,1)S(1)}, u32[]{:S(2)}, u32[]{:S(2)}) %all-to-all-start.1) | async-done | bytes 163872 | tf_op jit(solution)/shard_map/all_to_all | solution.py:78
  86.6 0.2 fusion.67
  86.8 0.4 fusion.70
  87.2 0.1 fusion.60
  87.4 0.2 fusion.51
  87.6 0.1 fusion.64
  87.7 0.1 fusion.52
  87.9 0.2 fusion.53
  88.1 0.4 multiply_reduce_fusion
  88.5 0.2 convolution_bitcast_fusion
  88.8 0.8 copy.33
  89.6 4.2 %all-to-all-start.2 = ((f32[32,1,1280]{2,1,0:T(1,128)}), f32[32,1,1280]{2,1,0:T(1,128)S(1)}, u32[]{:S(2)}, u32[]{:S(2)}) async-start(f32[32,1,1280]{2,1,0:T(1,128)} %copy.33), calls=%async_computation.2 | async-start | bytes 327680 | tf_op jit(solution)/shard_map/all_to_all | solution.py:78
  93.8 3.0 %fusion = bf16[1,1280,640]{2,1,0:T(8,128)(2,1)} fusion(bf16[256,640]{1,0:T(8,128)(2,1)S(1)} %fusion.18, bf16[256,2560]{1,0:T(8,128)(2,1)} %copy-done.5), kind=kOutput, calls=%fused_computation.9 | convolution fusion | flops 420249600 | bytes 2621440 | tf_op jit(solution)/shard_map/dot_general | solution.py:128
  96.8 4.8 %all-to-all-done.2 = f32[32,1,1280]{2,1,0:T(1,128)S(1)} async-done(((f32[32,1,1280]{2,1,0:T(1,128)}), f32[32,1,1280]{2,1,0:T(1,128)S(1)}, u32[]{:S(2)}, u32[]{:S(2)}) %all-to-all-start.2) | async-done | bytes 163872 | tf_op jit(solution)/shard_map/all_to_all | solution.py:78
  101.6 0.1 reduce_sum.198
  101.7 0.6 broadcast_in_dim.11
  102.4 5.2 %all-to-all-start.3 = ((f32[8,1,1280]{2,1,0:T(1,128)}), f32[8,1,1280]{2,1,0:T(1,128)S(1)}, u32[]{:S(2)}, u32[]{:S(2)}) async-start(f32[8,1,1280]{2,1,0:T(1,128)} %broadcast_in_dim.11), calls=%async_computation.3 | async-start | bytes 81920 | tf_op jit(solution)/shard_map/all_to_all | solution.py:85
  107.6 1.5 %fusion.48 = f32[256,1280]{1,0:T(8,128)} fusion(bf16[32,1,1280]{2,1,0:T(2,128)(2,1)S(1)} %copy-done.7, f32[32]{0:T(128)S(1)} %log_add_fusion.4, f32[256]{0:T(256)S(1)} %log_add_fusion, f32[256,32]{0,1:T(8,128)S(1)} %get-tuple-element.13, f32[32]{0:T(128)S(1)} %log_add_fusion.5, f32[256]{0:T(256)S(1)} %log_add_fusion.1), kind=kOutput, calls=%fused_computation.100 | convolution fusion | flops 21012480 | bytes 1427712 | tf_op jit(solution)/shard_map/dot_general | solution.py:153
  109.1 5.5 %all-to-all-done.3 = f32[8,1,1280]{2,1,0:T(1,128)S(1)} async-done(((f32[8,1,1280]{2,1,0:T(1,128)}), f32[8,1,1280]{2,1,0:T(1,128)S(1)}, u32[]{:S(2)}, u32[]{:S(2)}) %all-to-all-start.3) | async-done | bytes 40992 | tf_op jit(solution)/shard_map/all_to_all | solution.py:85
  114.6 0.8 broadcast_in_dim.12
  115.4 5.6 %all-to-all-start.4 = ((f32[32,1,1280]{2,1,0:T(1,128)}), f32[32,1,1280]{2,1,0:T(1,128)S(1)}, u32[]{:S(2)}, u32[]{:S(2)}) async-start(f32[32,1,1280]{2,1,0:T(1,128)} %broadcast_in_dim.12), calls=%async_computation.4 | async-start | bytes 327680 | tf_op jit(solution)/shard_map/all_to_all | solution.py:78
  121.0 2.5 %fusion.4 = bf16[1,256,1280]{2,1,0:T(8,128)(2,1)} fusion(f32[256,1280]{1,0:T(8,128)} %fusion.48, bf16[256,32]{0,1:T(8,128)(2,1)S(1)} %add_convert_fusion, bf16[1280,32]{0,1:T(8,128)(2,1)S(1)} %copy-done.8), kind=kOutput, calls=%fused_computation.14 | convolution fusion | flops 21626880 | bytes 2064384 | tf_op jit(solution)/shard_map/dot_general | solution.py:154
  123.5 5.3 %all-to-all-done.4 = f32[32,1,1280]{2,1,0:T(1,128)S(1)} async-done(((f32[32,1,1280]{2,1,0:T(1,128)}), f32[32,1,1280]{2,1,0:T(1,128)S(1)}, u32[]{:S(2)}, u32[]{:S(2)}) %all-to-all-start.4) | async-done | bytes 163872 | tf_op jit(solution)/shard_map/all_to_all | solution.py:78
  128.8 0.7 copy.53
  (83 shorter events, 1.7 us)
Async XLA Ops:
  0.6 46.9 %copy-start = (bf16[1,640,1280]{2,1,0:T(8,128)(2,1)S(1)}, bf16[1,640,1280]{2,1,0:T(8,128)(2,1)}, u32[]{:S(2)}) copy-start(bf16[1,640,1280]{2,1,0:T(8,128)(2,1)} %param.8) | copy-start | bytes 4915204
  0.6 3.7 %copy-start.1 = (bf16[1,256,1280]{2,1,0:T(8,128)(2,1)S(1)}, bf16[1,256,1280]{2,1,0:T(8,128)(2,1)}, u32[]{:S(2)}) copy-start(bf16[1,256,1280]{2,1,0:T(8,128)(2,1)} %param.5) | copy-start | bytes 1966084
  0.7 4.0 %copy-start.3 = (bf16[1,256,1280]{2,1,0:T(8,128)(2,1)S(1)}, bf16[1,256,1280]{2,1,0:T(8,128)(2,1)}, u32[]{:S(2)}) copy-start(bf16[1,256,1280]{2,1,0:T(8,128)(2,1)} %param.9) | copy-start | bytes 1966084
  21.6 25.2 %copy-start.2 = (bf16[1,1280,640]{2,1,0:T(8,128)(2,1)S(1)}, bf16[1,1280,640]{2,1,0:T(8,128)(2,1)}, u32[]{:S(2)}) copy-start(bf16[1,1280,640]{2,1,0:T(8,128)(2,1)} %param.7) | copy-start | bytes 4915204
  21.6 12.5 %collective-permute-start.3 = (bf16[32,2560]{1,0:T(8,128)(2,1)S(1)}, bf16[32,2560]{1,0:T(8,128)(2,1)S(1)}, u32[]{:S(2)}, u32[]{:S(2)}) collective-permute-start(bf16[32,2560]{1,0:T(8,128)(2,1)S(1)} %get-tuple-element.24), channel_id=1, source_target_pairs={{0,192},{32,224},{64,0},{96,32},{128,64},{160,96},{192,128},{224,1... | collective-permute-start | bytes 491528 | tf_op jit(solution)/shard_map/ppermute | solution.py:47
  27.7 11.2 %collective-permute-start.2 = (bf16[32,2560]{1,0:T(8,128)(2,1)S(1)}, bf16[32,2560]{1,0:T(8,128)(2,1)S(1)}, u32[]{:S(2)}, u32[]{:S(2)}) collective-permute-start(bf16[32,2560]{1,0:T(8,128)(2,1)S(1)} %get-tuple-element.24), channel_id=1, source_target_pairs={{0,64},{32,96},{64,128},{96,160},{128,192},{160,224},{192,0},{224,... | collective-permute-start | bytes 491528 | tf_op jit(solution)/shard_map/ppermute | solution.py:47
  27.7 14.3 %collective-permute-start = (bf16[32,2560]{1,0:T(8,128)(2,1)S(1)}, bf16[32,2560]{1,0:T(8,128)(2,1)S(1)}, u32[]{:S(2)}, u32[]{:S(2)}) collective-permute-start(bf16[32,2560]{1,0:T(8,128)(2,1)S(1)} %get-tuple-element.24), channel_id=1, source_target_pairs={{0,32},{32,64},{64,96},{96,128},{128,160},{160,192},{192,224},{224... | collective-permute-start | bytes 491528 | tf_op jit(solution)/shard_map/ppermute | solution.py:47
  28.5 13.6 %collective-permute-start.1 = (bf16[32,2560]{1,0:T(8,128)(2,1)S(1)}, bf16[32,2560]{1,0:T(8,128)(2,1)S(1)}, u32[]{:S(2)}, u32[]{:S(2)}) collective-permute-start(bf16[32,2560]{1,0:T(8,128)(2,1)S(1)} %get-tuple-element.24), channel_id=1, source_target_pairs={{0,224},{32,0},{64,32},{96,64},{128,96},{160,128},{192,160},{224,1... | collective-permute-start | bytes 491528 | tf_op jit(solution)/shard_map/ppermute | solution.py:47
  34.1 12.6 %collective-permute-start.7 = (bf16[32,1280]{1,0:T(8,128)(2,1)S(1)}, bf16[32,1280]{1,0:T(8,128)(2,1)S(1)}, u32[]{:S(2)}, u32[]{:S(2)}) collective-permute-start(bf16[32,1280]{1,0:T(8,128)(2,1)S(1)} %slice.108), channel_id=1, source_target_pairs={{0,192},{32,224},{64,0},{96,32},{128,64},{160,96},{192,128},{224,1... | collective-permute-start | bytes 245768 | tf_op jit(solution)/shard_map/ppermute | solution.py:47
  38.9 7.8 %collective-permute-start.6 = (bf16[32,1280]{1,0:T(8,128)(2,1)S(1)}, bf16[32,1280]{1,0:T(8,128)(2,1)S(1)}, u32[]{:S(2)}, u32[]{:S(2)}) collective-permute-start(bf16[32,1280]{1,0:T(8,128)(2,1)S(1)} %slice.107), channel_id=1, source_target_pairs={{0,64},{32,96},{64,128},{96,160},{128,192},{160,224},{192,0},{224,... | collective-permute-start | bytes 245768 | tf_op jit(solution)/shard_map/ppermute | solution.py:47
  39.0 7.5 %collective-permute-start.4 = (bf16[32,2560]{1,0:T(8,128)(2,1)S(1)}, bf16[32,2560]{1,0:T(8,128)(2,1)S(1)}, u32[]{:S(2)}, u32[]{:S(2)}) collective-permute-start(bf16[32,2560]{1,0:T(8,128)(2,1)S(1)} %collective-permute-done.2), channel_id=1, source_target_pairs={{0,32},{32,64},{64,96},{96,128},{128,160},{160,192},{192,224},{224... | collective-permute-start | bytes 491528 | tf_op jit(solution)/shard_map/ppermute | solution.py:47
  42.0 4.7 %collective-permute-start.5 = (bf16[32,2560]{1,0:T(8,128)(2,1)S(1)}, bf16[32,2560]{1,0:T(8,128)(2,1)S(1)}, u32[]{:S(2)}, u32[]{:S(2)}) collective-permute-start(bf16[32,2560]{1,0:T(8,128)(2,1)S(1)} %collective-permute-done.3), channel_id=1, source_target_pairs={{0,224},{32,0},{64,32},{96,64},{128,96},{160,128},{192,160},{224,1... | collective-permute-start | bytes 491528 | tf_op jit(solution)/shard_map/ppermute | solution.py:47
  46.8 1.5 %copy-start.5 = (bf16[256,2560]{1,0:T(8,128)(2,1)}, bf16[256,2560]{1,0:T(8,128)(2,1)S(1)}, u32[]{:S(2)}) copy-start(bf16[256,2560]{1,0:T(8,128)(2,1)S(1)} %maximum_dynamic-update-slice_fusion) | copy-start | bytes 3932164
  47.5 0.8 copy-start.4
  50.1 6.6 %collective-permute-start.10 = (bf16[32,2560]{1,0:T(8,128)(2,1)S(1)}, bf16[32,2560]{1,0:T(8,128)(2,1)S(1)}, u32[]{:S(2)}, u32[]{:S(2)}) collective-permute-start(bf16[32,2560]{1,0:T(8,128)(2,1)S(1)} %get-tuple-element.18), channel_id=1, source_target_pairs={{0,224},{32,0},{64,32},{96,64},{128,96},{160,128},{192,160},{224,1... | collective-permute-start | bytes 491528 | tf_op jit(solution)/shard_map/ppermute | solution.py:47
  52.6 6.4 %collective-permute-start.13 = (bf16[32,2560]{1,0:T(8,128)(2,1)S(1)}, bf16[32,2560]{1,0:T(8,128)(2,1)S(1)}, u32[]{:S(2)}, u32[]{:S(2)}) collective-permute-start(bf16[32,2560]{1,0:T(8,128)(2,1)S(1)} %get-tuple-element.17), channel_id=1, source_target_pairs={{0,32},{32,64},{64,96},{96,128},{128,160},{160,192},{192,224},{224... | collective-permute-start | bytes 491528 | tf_op jit(solution)/shard_map/ppermute | solution.py:47
  52.6 6.9 %collective-permute-start.14 = (bf16[32,1280]{1,0:T(8,128)(2,1)S(1)}, bf16[32,1280]{1,0:T(8,128)(2,1)S(1)}, u32[]{:S(2)}, u32[]{:S(2)}) collective-permute-start(bf16[32,1280]{1,0:T(8,128)(2,1)S(1)} %slice.179), channel_id=1, source_target_pairs={{0,64},{32,96},{64,128},{96,160},{128,192},{160,224},{192,0},{224,... | collective-permute-start | bytes 245768 | tf_op jit(solution)/shard_map/ppermute | solution.py:47
  52.7 7.0 %collective-permute-start.11 = (bf16[32,1280]{1,0:T(8,128)(2,1)S(1)}, bf16[32,1280]{1,0:T(8,128)(2,1)S(1)}, u32[]{:S(2)}, u32[]{:S(2)}) collective-permute-start(bf16[32,1280]{1,0:T(8,128)(2,1)S(1)} %slice.182), channel_id=1, source_target_pairs={{0,192},{32,224},{64,0},{96,32},{128,64},{160,96},{192,128},{224,1... | collective-permute-start | bytes 245768 | tf_op jit(solution)/shard_map/ppermute | solution.py:47
  56.3 9.0 %collective-permute-start.9 = (bf16[32,2560]{1,0:T(8,128)(2,1)S(1)}, bf16[32,2560]{1,0:T(8,128)(2,1)S(1)}, u32[]{:S(2)}, u32[]{:S(2)}) collective-permute-start(bf16[32,2560]{1,0:T(8,128)(2,1)S(1)} %get-tuple-element.19), channel_id=1, source_target_pairs={{0,32},{32,64},{64,96},{96,128},{128,160},{160,192},{192,224},{224... | collective-permute-start | bytes 491528 | tf_op jit(solution)/shard_map/ppermute | solution.py:47
  56.7 8.6 %collective-permute-start.8 = (bf16[32,2560]{1,0:T(8,128)(2,1)S(1)}, bf16[32,2560]{1,0:T(8,128)(2,1)S(1)}, u32[]{:S(2)}, u32[]{:S(2)}) collective-permute-start(bf16[32,2560]{1,0:T(8,128)(2,1)S(1)} %get-tuple-element.16), channel_id=1, source_target_pairs={{0,224},{32,0},{64,32},{96,64},{128,96},{160,128},{192,160},{224,1... | collective-permute-start | bytes 491528 | tf_op jit(solution)/shard_map/ppermute | solution.py:47
  59.6 9.6 %collective-permute-start.15 = (bf16[32,2560]{1,0:T(8,128)(2,1)S(1)}, bf16[32,2560]{1,0:T(8,128)(2,1)S(1)}, u32[]{:S(2)}, u32[]{:S(2)}) collective-permute-start(bf16[32,2560]{1,0:T(8,128)(2,1)S(1)} %pad_maximum_fusion.4), channel_id=1, source_target_pairs={{0,64},{32,96},{64,128},{96,160},{128,192},{160,224},{192,0},{224,... | collective-permute-start | bytes 491528 | tf_op jit(solution)/shard_map/ppermute | solution.py:47
  59.8 9.4 %collective-permute-start.12 = (bf16[32,2560]{1,0:T(8,128)(2,1)S(1)}, bf16[32,2560]{1,0:T(8,128)(2,1)S(1)}, u32[]{:S(2)}, u32[]{:S(2)}) collective-permute-start(bf16[32,2560]{1,0:T(8,128)(2,1)S(1)} %pad_maximum_fusion.3), channel_id=1, source_target_pairs={{0,192},{32,224},{64,0},{96,32},{128,64},{160,96},{192,128},{224,1... | collective-permute-start | bytes 491528 | tf_op jit(solution)/shard_map/ppermute | solution.py:47
  70.2 16.4 %all-to-all-start.1 = ((bf16[32,2,1280]{2,1,0:T(2,128)(2,1)}), bf16[32,2,1280]{2,1,0:T(2,128)(2,1)S(1)}, u32[]{:S(2)}, u32[]{:S(2)}) async-start(bf16[32,2,1280]{2,1,0:T(2,128)(2,1)} %copy.30), calls=%async_computation.1 | async-start | bytes 327680 | tf_op jit(solution)/shard_map/all_to_all | solution.py:78
  86.8 2.0 %copy-start.6 = (bf16[32,1,1280]{2,1,0:T(2,128)(2,1)}, bf16[32,1,1280]{2,1,0:T(2,128)(2,1)S(1)}, u32[]{:S(2)}) copy-start(bf16[32,1,1280]{2,1,0:T(2,128)(2,1)S(1)} %get-tuple-element.21) | copy-start | bytes 245764
  89.6 12.0 %all-to-all-start.2 = ((f32[32,1,1280]{2,1,0:T(1,128)}), f32[32,1,1280]{2,1,0:T(1,128)S(1)}, u32[]{:S(2)}, u32[]{:S(2)}) async-start(f32[32,1,1280]{2,1,0:T(1,128)} %copy.33), calls=%async_computation.2 | async-start | bytes 327680 | tf_op jit(solution)/shard_map/all_to_all | solution.py:78
  93.8 13.8 %copy-start.7 = (bf16[32,1,1280]{2,1,0:T(2,128)(2,1)S(1)}, bf16[32,1,1280]{2,1,0:T(2,128)(2,1)}, u32[]{:S(2)}) copy-start(bf16[32,1,1280]{2,1,0:T(2,128)(2,1)} %copy-done.6) | copy-start | bytes 245764
  96.8 24.2 %copy-start.8 = (bf16[1280,32]{0,1:T(8,128)(2,1)S(1)}, bf16[1280,32]{0,1:T(8,128)(2,1)}, u32[]{:S(2)}) copy-start(bf16[1280,32]{0,1:T(8,128)(2,1)} %param.6) | copy-start | bytes 245764
  102.4 12.2 %all-to-all-start.3 = ((f32[8,1,1280]{2,1,0:T(1,128)}), f32[8,1,1280]{2,1,0:T(1,128)S(1)}, u32[]{:S(2)}, u32[]{:S(2)}) async-start(f32[8,1,1280]{2,1,0:T(1,128)} %broadcast_in_dim.11), calls=%async_computation.3 | async-start | bytes 81920 | tf_op jit(solution)/shard_map/all_to_all | solution.py:85
  115.4 13.4 %all-to-all-start.4 = ((f32[32,1,1280]{2,1,0:T(1,128)}), f32[32,1,1280]{2,1,0:T(1,128)S(1)}, u32[]{:S(2)}, u32[]{:S(2)}) async-start(f32[32,1,1280]{2,1,0:T(1,128)} %broadcast_in_dim.12), calls=%async_computation.4 | async-start | bytes 327680 | tf_op jit(solution)/shard_map/all_to_all | solution.py:78

commit v5 on v4

--- a/solution.py
+++ b/solution.py
@@ -64,10 +64,15 @@
     half = partial.shape[1] // 2
     block = [partial[i * rows : (i + 1) * rows] for i in range(8)]
     own, behind_one, ahead_one, behind_two, ahead_two, behind_three, ahead_three, away = block
-    send = lambda value, step: shift(value.astype(jnp.bfloat16), step).astype(jnp.float32)
-    down, up = send(behind_three, -1), send(ahead_three, 1)
+    narrow = jnp.bfloat16
+    send = lambda value, step: shift(value.astype(narrow), step).astype(jnp.float32)
+    down, up = shift(behind_three.astype(narrow), -1), shift(ahead_three.astype(narrow), 1)
     away_down, away_up = send(away[:, :half], -2), send(away[:, half:], 2)
-    near = send(behind_one, -1) + send(ahead_one, 1)
+    down, up, to_behind, to_ahead = lax.optimization_barrier(
+        (down, up, behind_one.astype(narrow), ahead_one.astype(narrow))
+    )
+    near = send(to_behind, -1) + send(to_ahead, 1)
+    down, up = down.astype(jnp.float32), up.astype(jnp.float32)
     down, up = down + behind_two, up + ahead_two
     down = jnp.concatenate([down[:, :half] + away_down, down[:, half:]], axis=1)
     up = jnp.concatenate([up[:, :half], up[:, half:] + away_up], axis=1)

time: 130 us -> 130 us (level)
  waiting for transfers between devices: 37.2 us -> 40.1 us
  starting transfers between devices: 50.4 us -> 47.7 us
    ppermute x16, waiting for transfers between devices: 17 us -> 20 us  [shift(): lax.ppermute(value, 'dp', [(i, (i + step) % size) for i in range(size)])]
    all_to_all x1, starting transfers between devices: 5.23 us -> 3.55 us  [sum_everywhere(): seen = lax.all_to_all(copies, 'dp', split_axis=0, concat_axis=0, tiled=True)]
  transfers between devices with their start and end apart: 20 -> 20, of which waited for: 11 -> 12; matrix products, arithmetic and copies ran while one was open for 8% -> 8% of each run, Pallas kernels for 0% -> 0%
where the time goes in v5:
time: 130 us
  starting transfers between devices  47.7 us (37%)
  waiting for transfers between devices  40.1 us (31%)
  matrix products  16.3 us (13%)
  blocking collectives  16.2 us (12%)
  local copies, waits for them, and re-layouts  4.68 us (4%)
  other arithmetic  3.52 us (3%)
    ppermute x16, starting transfers between devices, shift(): lax.ppermute(value, 'dp', [(i, (i + step) % size) for i in range(size)])  26.8 us
    ppermute x16, waiting for transfers between devices, shift(): lax.ppermute(value, 'dp', [(i, (i + step) % size) for i in range(size)])  20 us
    all_to_all x3, starting transfers between devices, swap(): lax.all_to_all(value, ('tok', 'expert'), split_axis=0, concat_axis=0, til...  17.4 us
    all_to_all x1, blocking collectives, swap(): lax.all_to_all(value, ('tok', 'expert'), split_axis=0, concat_axis=0, til...  16.2 us
    all_to_all x3, waiting for transfers between devices, swap(): lax.all_to_all(value, ('tok', 'expert'), split_axis=0, concat_axis=0, til...  14.7 us
    all_to_all x1, waiting for transfers between devices, sum_everywhere(): seen = lax.all_to_all(copies, 'dp', split_axis=0, concat_axis=0, tiled=True)  5.46 us
    all_to_all x1, starting transfers between devices, sum_everywhere(): seen = lax.all_to_all(copies, 'dp', split_axis=0, concat_axis=0, tiled=True)  3.55 us
    dot_general x1, matrix products, body(): lax.dot_general(hidden_act, all_grad, (((0,), (0,)), ((), ())), preferred...  3.2 us
  transfers between devices with their start and end apart: 20, of which 12 were waited for; matrix products, arithmetic and copies ran while one was open for 8% of the time, Pallas kernels for 0%

profile of v5, /device:TPU:1, one launch (start us, length us, event | category | flops | bytes accessed | tf_op | source)
XLA Modules:
  0.0 129.7 jit_solution(4939769270609785774)
XLA Ops:
  0.7 1.6 %fusion.69 = (f32[256]{0:T(256)S(1)}, f32[256,32]{0,1:T(8,128)S(1)}) fusion(bf16[1280,32]{0,1:T(8,128)(2,1)} %param.6, bf16[1,256,1280]{2,1,0:T(8,128)(2,1)} %param.5), kind=kOutput, calls=%fused_computation.148 | convolution fusion | flops 20979456 | bytes 771072 | tf_op jit(solution)/shard_map/dot_general | solution.py:102
  2.3 0.1 subtract_reduce_fusion.3
  2.4 0.2 exponential_reduce_fusion.6
  2.7 0.1 exponential_reduce_fusion.5
  2.9 0.2 subtract_reduce_fusion.2
  3.1 0.2 exponential_reduce_fusion.4
  3.4 0.1 subtract_reduce_fusion.1
  3.5 0.2 exponential_reduce_fusion.2
  4.0 0.2 subtract_reduce_fusion
  4.2 0.2 exponential_reduce_fusion
  4.4 0.3 fusion.5
  4.7 0.2 fusion.6
  4.9 0.2 copy.27
  5.1 16.2 %all_to_all.34 = bf16[32,2,1280]{2,1,0:T(2,128)(2,1)S(1)} all-to-all(bf16[32,2,1280]{2,1,0:T(2,128)(2,1)S(1)} %copy.27), channel_id=1, replica_groups=mesh['dp'=8,'tok'=2,'expert'=16] {'tok','expert'}, dimensions={0} | all-to-all | bytes 327680 | tf_op jit(solution)/shard_map/all_to_all | solution.py:83
  21.3 0.2 fusion.68
  21.6 6.1 %collective-permute-start.3 = (bf16[32,2560]{1,0:T(8,128)(2,1)S(1)}, bf16[32,2560]{1,0:T(8,128)(2,1)S(1)}, u32[]{:S(2)}, u32[]{:S(2)}) collective-permute-start(bf16[32,2560]{1,0:T(8,128)(2,1)S(1)} %get-tuple-element.32), channel_id=1, source_target_pairs={{0,192},{32,224},{64,0},{96,32},{128,64},{160,96},{192,128},{224,1... | collective-permute-start | bytes 491528 | tf_op jit(solution)/shard_map/ppermute | solution.py:47
  27.7 0.7 collective-permute-start
  28.5 2.4 %collective-permute-start.1 = (bf16[32,2560]{1,0:T(8,128)(2,1)S(1)}, bf16[32,2560]{1,0:T(8,128)(2,1)S(1)}, u32[]{:S(2)}, u32[]{:S(2)}) collective-permute-start(bf16[32,2560]{1,0:T(8,128)(2,1)S(1)} %get-tuple-element.32), channel_id=1, source_target_pairs={{0,224},{32,0},{64,32},{96,64},{128,96},{160,128},{192,160},{224,1... | collective-permute-start | bytes 491528 | tf_op jit(solution)/shard_map/ppermute | solution.py:47
  30.9 3.3 %collective-permute-done.3 = bf16[32,2560]{1,0:T(8,128)(2,1)S(1)} collective-permute-done((bf16[32,2560]{1,0:T(8,128)(2,1)S(1)}, bf16[32,2560]{1,0:T(8,128)(2,1)S(1)}, u32[]{:S(2)}, u32[]{:S(2)}) %collective-permute-start.3) | collective-permute-done | bytes 163872 | tf_op jit(solution)/shard_map/ppermute | solution.py:47
  34.1 4.8 %collective-permute-start.7 = (bf16[32,1280]{1,0:T(8,128)(2,1)S(1)}, bf16[32,1280]{1,0:T(8,128)(2,1)S(1)}, u32[]{:S(2)}, u32[]{:S(2)}) collective-permute-start(bf16[32,1280]{1,0:T(8,128)(2,1)S(1)} %slice.108), channel_id=1, source_target_pairs={{0,192},{32,224},{64,0},{96,32},{128,64},{160,96},{192,128},{224,1... | collective-permute-start | bytes 245768 | tf_op jit(solution)/shard_map/ppermute | solution.py:47
  39.1 2.9 %collective-permute-done = bf16[32,2560]{1,0:T(8,128)(2,1)S(1)} collective-permute-done((bf16[32,2560]{1,0:T(8,128)(2,1)S(1)}, bf16[32,2560]{1,0:T(8,128)(2,1)S(1)}, u32[]{:S(2)}, u32[]{:S(2)}) %collective-permute-start) | collective-permute-done | bytes 163872 | tf_op jit(solution)/shard_map/ppermute | solution.py:47
  42.1 4.4 %collective-permute-done.4 = bf16[32,2560]{1,0:T(8,128)(2,1)S(1)} collective-permute-done((bf16[32,2560]{1,0:T(8,128)(2,1)S(1)}, bf16[32,2560]{1,0:T(8,128)(2,1)S(1)}, u32[]{:S(2)}, u32[]{:S(2)}) %collective-permute-start.4) | collective-permute-done | bytes 163872 | tf_op jit(solution)/shard_map/ppermute | solution.py:47
  46.6 0.2 collective-permute-done.5
  46.8 0.7 fusion.13
  47.5 0.8 fusion.9
  48.3 0.8 fusion.18
  49.2 0.7 fusion.11
  49.9 0.1 fusion.2
  50.1 2.5 %collective-permute-start.8 = (bf16[32,2560]{1,0:T(8,128)(2,1)S(1)}, bf16[32,2560]{1,0:T(8,128)(2,1)S(1)}, u32[]{:S(2)}, u32[]{:S(2)}) collective-permute-start(bf16[32,2560]{1,0:T(8,128)(2,1)S(1)} %get-tuple-element.27), channel_id=1, source_target_pairs={{0,224},{32,0},{64,32},{96,64},{128,96},{160,128},{192,160},{224,1... | collective-permute-start | bytes 491528 | tf_op jit(solution)/shard_map/ppermute | solution.py:47
  52.7 3.6 %collective-permute-start.12 = (bf16[32,1280]{1,0:T(8,128)(2,1)S(1)}, bf16[32,1280]{1,0:T(8,128)(2,1)S(1)}, u32[]{:S(2)}, u32[]{:S(2)}) collective-permute-start(bf16[32,1280]{1,0:T(8,128)(2,1)S(1)} %slice.182), channel_id=1, source_target_pairs={{0,192},{32,224},{64,0},{96,32},{128,64},{160,96},{192,128},{224,1... | collective-permute-start | bytes 245768 | tf_op jit(solution)/shard_map/ppermute | solution.py:47
  56.3 2.3 %collective-permute-done.9 = bf16[32,2560]{1,0:T(8,128)(2,1)S(1)} collective-permute-done((bf16[32,2560]{1,0:T(8,128)(2,1)S(1)}, bf16[32,2560]{1,0:T(8,128)(2,1)S(1)}, u32[]{:S(2)}, u32[]{:S(2)}) %collective-permute-start.9) | collective-permute-done | bytes 163872 | tf_op jit(solution)/shard_map/ppermute | solution.py:47
  58.7 0.8 collective-permute-done.14
  59.8 3.6 %collective-permute-start.13 = (bf16[32,2560]{1,0:T(8,128)(2,1)S(1)}, bf16[32,2560]{1,0:T(8,128)(2,1)S(1)}, u32[]{:S(2)}, u32[]{:S(2)}) collective-permute-start(bf16[32,2560]{1,0:T(8,128)(2,1)S(1)} %pad_maximum_fusion.3), channel_id=1, source_target_pairs={{0,192},{32,224},{64,0},{96,32},{128,64},{160,96},{192,128},{224,1... | collective-permute-start | bytes 491528 | tf_op jit(solution)/shard_map/ppermute | solution.py:47
  63.4 2.1 %collective-permute-start.11 = (bf16[32,2560]{1,0:T(8,128)(2,1)S(1)}, bf16[32,2560]{1,0:T(8,128)(2,1)S(1)}, u32[]{:S(2)}, u32[]{:S(2)}) collective-permute-start(bf16[32,2560]{1,0:T(8,128)(2,1)S(1)} %get-tuple-element.9), channel_id=1, source_target_pairs={{0,32},{32,64},{64,96},{96,128},{128,160},{160,192},{192,224},{224... | collective-permute-start | bytes 491528 | tf_op jit(solution)/shard_map/ppermute | solution.py:47
  65.5 0.6 collective-permute-start.10
  66.1 1.5 %collective-permute-done.15 = bf16[32,2560]{1,0:T(8,128)(2,1)S(1)} collective-permute-done((bf16[32,2560]{1,0:T(8,128)(2,1)S(1)}, bf16[32,2560]{1,0:T(8,128)(2,1)S(1)}, u32[]{:S(2)}, u32[]{:S(2)}) %collective-permute-start.15) | collective-permute-done | bytes 163872 | tf_op jit(solution)/shard_map/ppermute | solution.py:47
  67.6 4.5 %collective-permute-done.11 = bf16[32,2560]{1,0:T(8,128)(2,1)S(1)} collective-permute-done((bf16[32,2560]{1,0:T(8,128)(2,1)S(1)}, bf16[32,2560]{1,0:T(8,128)(2,1)S(1)}, u32[]{:S(2)}, u32[]{:S(2)}) %collective-permute-start.11) | collective-permute-done | bytes 163872 | tf_op jit(solution)/shard_map/ppermute | solution.py:47
  72.3 0.8 copy.30
  73.1 7.6 %all-to-all-start.1 = ((bf16[32,2,1280]{2,1,0:T(2,128)(2,1)}), bf16[32,2,1280]{2,1,0:T(2,128)(2,1)S(1)}, u32[]{:S(2)}, u32[]{:S(2)}) async-start(bf16[32,2,1280]{2,1,0:T(2,128)(2,1)} %copy.30), calls=%async_computation.1 | async-start | bytes 327680 | tf_op jit(solution)/shard_map/all_to_all | solution.py:83
  80.7 3.2 %fusion.1 = bf16[1,640,1280]{2,1,0:T(8,128)(2,1)} fusion(bf16[256,2560]{1,0:T(8,128)(2,1)} %copy-done.5, f32[256,640]{1,0:T(8,128)} %copy-done.4), kind=kOutput, calls=%fused_computation.10 | convolution fusion | flops 421724160 | bytes 2949120 | tf_op jit(solution)/shard_map/dot_general | solution.py:136
  83.9 4.6 %all-to-all-done.1 = bf16[32,2,1280]{2,1,0:T(2,128)(2,1)S(1)} async-done(((bf16[32,2,1280]{2,1,0:T(2,128)(2,1)}), bf16[32,2,1280]{2,1,0:T(2,128)(2,1)S(1)}, u32[]{:S(2)}, u32[]{:S(2)}) %all-to-all-start.1) | async-done | bytes 163872 | tf_op jit(solution)/shard_map/all_to_all | solution.py:83
  88.5 0.2 fusion.67
  88.8 0.4 fusion.70
  89.2 0.1 fusion.60
  89.3 0.2 fusion.51
  89.5 0.1 fusion.64
  89.6 0.1 fusion.52
  89.8 0.2 fusion.53
  90.0 0.4 multiply_reduce_fusion
  90.5 0.2 convolution_bitcast_fusion
  90.7 0.8 copy.33
  91.6 4.2 %all-to-all-start.2 = ((f32[32,1,1280]{2,1,0:T(1,128)}), f32[32,1,1280]{2,1,0:T(1,128)S(1)}, u32[]{:S(2)}, u32[]{:S(2)}) async-start(f32[32,1,1280]{2,1,0:T(1,128)} %copy.33), calls=%async_computation.2 | async-start | bytes 327680 | tf_op jit(solution)/shard_map/all_to_all | solution.py:83
  95.8 3.0 %fusion = bf16[1,1280,640]{2,1,0:T(8,128)(2,1)} fusion(bf16[256,640]{1,0:T(8,128)(2,1)S(1)} %fusion.18, bf16[256,2560]{1,0:T(8,128)(2,1)} %copy-done.5), kind=kOutput, calls=%fused_computation.9 | convolution fusion | flops 420249600 | bytes 2621440 | tf_op jit(solution)/shard_map/dot_general | solution.py:133
  98.8 4.8 %all-to-all-done.2 = f32[32,1,1280]{2,1,0:T(1,128)S(1)} async-done(((f32[32,1,1280]{2,1,0:T(1,128)}), f32[32,1,1280]{2,1,0:T(1,128)S(1)}, u32[]{:S(2)}, u32[]{:S(2)}) %all-to-all-start.2) | async-done | bytes 163872 | tf_op jit(solution)/shard_map/all_to_all | solution.py:83
  103.6 0.1 reduce_sum.198
  103.7 0.6 broadcast_in_dim.11
  104.3 3.5 %all-to-all-start.3 = ((f32[8,1,1280]{2,1,0:T(1,128)}), f32[8,1,1280]{2,1,0:T(1,128)S(1)}, u32[]{:S(2)}, u32[]{:S(2)}) async-start(f32[8,1,1280]{2,1,0:T(1,128)} %broadcast_in_dim.11), calls=%async_computation.3 | async-start | bytes 81920 | tf_op jit(solution)/shard_map/all_to_all | solution.py:90
  107.9 1.5 %fusion.48 = f32[256,1280]{1,0:T(8,128)} fusion(bf16[32,1,1280]{2,1,0:T(2,128)(2,1)S(1)} %copy-done.7, f32[32]{0:T(128)S(1)} %log_add_fusion.4, f32[256]{0:T(256)S(1)} %log_add_fusion, f32[256,32]{0,1:T(8,128)S(1)} %get-tuple-element.21, f32[32]{0:T(128)S(1)} %log_add_fusion.5, f32[256]{0:T(256)S(1)} %log_add_fusion.1), kind=kOutput, calls=%fused_computation.100 | convolution fusion | flops 21012480 | bytes 1427712 | tf_op jit(solution)/shard_map/dot_general | solution.py:158
  109.4 5.5 %all-to-all-done.3 = f32[8,1,1280]{2,1,0:T(1,128)S(1)} async-done(((f32[8,1,1280]{2,1,0:T(1,128)}), f32[8,1,1280]{2,1,0:T(1,128)S(1)}, u32[]{:S(2)}, u32[]{:S(2)}) %all-to-all-start.3) | async-done | bytes 40992 | tf_op jit(solution)/shard_map/all_to_all | solution.py:90
  114.9 0.8 broadcast_in_dim.12
  115.6 5.6 %all-to-all-start.4 = ((f32[32,1,1280]{2,1,0:T(1,128)}), f32[32,1,1280]{2,1,0:T(1,128)S(1)}, u32[]{:S(2)}, u32[]{:S(2)}) async-start(f32[32,1,1280]{2,1,0:T(1,128)} %broadcast_in_dim.12), calls=%async_computation.4 | async-start | bytes 327680 | tf_op jit(solution)/shard_map/all_to_all | solution.py:83
  121.3 2.5 %fusion.4 = bf16[1,256,1280]{2,1,0:T(8,128)(2,1)} fusion(f32[256,1280]{1,0:T(8,128)} %fusion.48, bf16[256,32]{0,1:T(8,128)(2,1)S(1)} %add_convert_fusion, bf16[1280,32]{0,1:T(8,128)(2,1)S(1)} %copy-done.8), kind=kOutput, calls=%fused_computation.14 | convolution fusion | flops 21626880 | bytes 2064384 | tf_op jit(solution)/shard_map/dot_general | solution.py:159
  123.8 5.3 %all-to-all-done.4 = f32[32,1,1280]{2,1,0:T(1,128)S(1)} async-done(((f32[32,1,1280]{2,1,0:T(1,128)}), f32[32,1,1280]{2,1,0:T(1,128)S(1)}, u32[]{:S(2)}, u32[]{:S(2)}) %all-to-all-start.4) | async-done | bytes 163872 | tf_op jit(solution)/shard_map/all_to_all | solution.py:83
  129.1 0.7 copy.53
  (83 shorter events, 1.8 us)
Async XLA Ops:
  0.6 46.9 %copy-start = (bf16[1,640,1280]{2,1,0:T(8,128)(2,1)S(1)}, bf16[1,640,1280]{2,1,0:T(8,128)(2,1)}, u32[]{:S(2)}) copy-start(bf16[1,640,1280]{2,1,0:T(8,128)(2,1)} %param.8) | copy-start | bytes 4915204
  0.6 3.7 %copy-start.1 = (bf16[1,256,1280]{2,1,0:T(8,128)(2,1)S(1)}, bf16[1,256,1280]{2,1,0:T(8,128)(2,1)}, u32[]{:S(2)}) copy-start(bf16[1,256,1280]{2,1,0:T(8,128)(2,1)} %param.5) | copy-start | bytes 1966084
  0.7 4.0 %copy-start.3 = (bf16[1,256,1280]{2,1,0:T(8,128)(2,1)S(1)}, bf16[1,256,1280]{2,1,0:T(8,128)(2,1)}, u32[]{:S(2)}) copy-start(bf16[1,256,1280]{2,1,0:T(8,128)(2,1)} %param.9) | copy-start | bytes 1966084
  21.6 25.2 %copy-start.2 = (bf16[1,1280,640]{2,1,0:T(8,128)(2,1)S(1)}, bf16[1,1280,640]{2,1,0:T(8,128)(2,1)}, u32[]{:S(2)}) copy-start(bf16[1,1280,640]{2,1,0:T(8,128)(2,1)} %param.7) | copy-start | bytes 4915204
  21.6 12.5 %collective-permute-start.3 = (bf16[32,2560]{1,0:T(8,128)(2,1)S(1)}, bf16[32,2560]{1,0:T(8,128)(2,1)S(1)}, u32[]{:S(2)}, u32[]{:S(2)}) collective-permute-start(bf16[32,2560]{1,0:T(8,128)(2,1)S(1)} %get-tuple-element.32), channel_id=1, source_target_pairs={{0,192},{32,224},{64,0},{96,32},{128,64},{160,96},{192,128},{224,1... | collective-permute-start | bytes 491528 | tf_op jit(solution)/shard_map/ppermute | solution.py:47
  27.7 11.2 %collective-permute-start.2 = (bf16[32,2560]{1,0:T(8,128)(2,1)S(1)}, bf16[32,2560]{1,0:T(8,128)(2,1)S(1)}, u32[]{:S(2)}, u32[]{:S(2)}) collective-permute-start(bf16[32,2560]{1,0:T(8,128)(2,1)S(1)} %get-tuple-element.32), channel_id=1, source_target_pairs={{0,64},{32,96},{64,128},{96,160},{128,192},{160,224},{192,0},{224,... | collective-permute-start | bytes 491528 | tf_op jit(solution)/shard_map/ppermute | solution.py:47
  27.7 14.3 %collective-permute-start = (bf16[32,2560]{1,0:T(8,128)(2,1)S(1)}, bf16[32,2560]{1,0:T(8,128)(2,1)S(1)}, u32[]{:S(2)}, u32[]{:S(2)}) collective-permute-start(bf16[32,2560]{1,0:T(8,128)(2,1)S(1)} %get-tuple-element.32), channel_id=1, source_target_pairs={{0,32},{32,64},{64,96},{96,128},{128,160},{160,192},{192,224},{224... | collective-permute-start | bytes 491528 | tf_op jit(solution)/shard_map/ppermute | solution.py:47
  28.5 13.6 %collective-permute-start.1 = (bf16[32,2560]{1,0:T(8,128)(2,1)S(1)}, bf16[32,2560]{1,0:T(8,128)(2,1)S(1)}, u32[]{:S(2)}, u32[]{:S(2)}) collective-permute-start(bf16[32,2560]{1,0:T(8,128)(2,1)S(1)} %get-tuple-element.32), channel_id=1, source_target_pairs={{0,224},{32,0},{64,32},{96,64},{128,96},{160,128},{192,160},{224,1... | collective-permute-start | bytes 491528 | tf_op jit(solution)/shard_map/ppermute | solution.py:47
  34.1 12.6 %collective-permute-start.7 = (bf16[32,1280]{1,0:T(8,128)(2,1)S(1)}, bf16[32,1280]{1,0:T(8,128)(2,1)S(1)}, u32[]{:S(2)}, u32[]{:S(2)}) collective-permute-start(bf16[32,1280]{1,0:T(8,128)(2,1)S(1)} %slice.108), channel_id=1, source_target_pairs={{0,192},{32,224},{64,0},{96,32},{128,64},{160,96},{192,128},{224,1... | collective-permute-start | bytes 245768 | tf_op jit(solution)/shard_map/ppermute | solution.py:47
  38.9 7.8 %collective-permute-start.6 = (bf16[32,1280]{1,0:T(8,128)(2,1)S(1)}, bf16[32,1280]{1,0:T(8,128)(2,1)S(1)}, u32[]{:S(2)}, u32[]{:S(2)}) collective-permute-start(bf16[32,1280]{1,0:T(8,128)(2,1)S(1)} %slice.107), channel_id=1, source_target_pairs={{0,64},{32,96},{64,128},{96,160},{128,192},{160,224},{192,0},{224,... | collective-permute-start | bytes 245768 | tf_op jit(solution)/shard_map/ppermute | solution.py:47
  39.0 7.5 %collective-permute-start.4 = (bf16[32,2560]{1,0:T(8,128)(2,1)S(1)}, bf16[32,2560]{1,0:T(8,128)(2,1)S(1)}, u32[]{:S(2)}, u32[]{:S(2)}) collective-permute-start(bf16[32,2560]{1,0:T(8,128)(2,1)S(1)} %collective-permute-done.2), channel_id=1, source_target_pairs={{0,32},{32,64},{64,96},{96,128},{128,160},{160,192},{192,224},{224... | collective-permute-start | bytes 491528 | tf_op jit(solution)/shard_map/ppermute | solution.py:47
  42.0 4.7 %collective-permute-start.5 = (bf16[32,2560]{1,0:T(8,128)(2,1)S(1)}, bf16[32,2560]{1,0:T(8,128)(2,1)S(1)}, u32[]{:S(2)}, u32[]{:S(2)}) collective-permute-start(bf16[32,2560]{1,0:T(8,128)(2,1)S(1)} %collective-permute-done.3), channel_id=1, source_target_pairs={{0,224},{32,0},{64,32},{96,64},{128,96},{160,128},{192,160},{224,1... | collective-permute-start | bytes 491528 | tf_op jit(solution)/shard_map/ppermute | solution.py:47
  46.8 1.5 %copy-start.5 = (bf16[256,2560]{1,0:T(8,128)(2,1)}, bf16[256,2560]{1,0:T(8,128)(2,1)S(1)}, u32[]{:S(2)}) copy-start(bf16[256,2560]{1,0:T(8,128)(2,1)S(1)} %maximum_dynamic-update-slice_fusion) | copy-start | bytes 3932164
  47.5 0.8 copy-start.4
  50.1 6.2 %collective-permute-start.8 = (bf16[32,2560]{1,0:T(8,128)(2,1)S(1)}, bf16[32,2560]{1,0:T(8,128)(2,1)S(1)}, u32[]{:S(2)}, u32[]{:S(2)}) collective-permute-start(bf16[32,2560]{1,0:T(8,128)(2,1)S(1)} %get-tuple-element.27), channel_id=1, source_target_pairs={{0,224},{32,0},{64,32},{96,64},{128,96},{160,128},{192,160},{224,1... | collective-permute-start | bytes 491528 | tf_op jit(solution)/shard_map/ppermute | solution.py:47
  52.6 6.0 %collective-permute-start.9 = (bf16[32,2560]{1,0:T(8,128)(2,1)S(1)}, bf16[32,2560]{1,0:T(8,128)(2,1)S(1)}, u32[]{:S(2)}, u32[]{:S(2)}) collective-permute-start(bf16[32,2560]{1,0:T(8,128)(2,1)S(1)} %get-tuple-element.26), channel_id=1, source_target_pairs={{0,32},{32,64},{64,96},{96,128},{128,160},{160,192},{192,224},{224... | collective-permute-start | bytes 491528 | tf_op jit(solution)/shard_map/ppermute | solution.py:47
  52.6 6.9 %collective-permute-start.14 = (bf16[32,1280]{1,0:T(8,128)(2,1)S(1)}, bf16[32,1280]{1,0:T(8,128)(2,1)S(1)}, u32[]{:S(2)}, u32[]{:S(2)}) collective-permute-start(bf16[32,1280]{1,0:T(8,128)(2,1)S(1)} %slice.179), channel_id=1, source_target_pairs={{0,64},{32,96},{64,128},{96,160},{128,192},{160,224},{192,0},{224,... | collective-permute-start | bytes 245768 | tf_op jit(solution)/shard_map/ppermute | solution.py:47
  52.7 7.0 %collective-permute-start.12 = (bf16[32,1280]{1,0:T(8,128)(2,1)S(1)}, bf16[32,1280]{1,0:T(8,128)(2,1)S(1)}, u32[]{:S(2)}, u32[]{:S(2)}) collective-permute-start(bf16[32,1280]{1,0:T(8,128)(2,1)S(1)} %slice.182), channel_id=1, source_target_pairs={{0,192},{32,224},{64,0},{96,32},{128,64},{160,96},{192,128},{224,1... | collective-permute-start | bytes 245768 | tf_op jit(solution)/shard_map/ppermute | solution.py:47
  59.6 8.0 %collective-permute-start.15 = (bf16[32,2560]{1,0:T(8,128)(2,1)S(1)}, bf16[32,2560]{1,0:T(8,128)(2,1)S(1)}, u32[]{:S(2)}, u32[]{:S(2)}) collective-permute-start(bf16[32,2560]{1,0:T(8,128)(2,1)S(1)} %pad_maximum_fusion.4), channel_id=1, source_target_pairs={{0,64},{32,96},{64,128},{96,160},{128,192},{160,224},{192,0},{224,... | collective-permute-start | bytes 491528 | tf_op jit(solution)/shard_map/ppermute | solution.py:47
  59.8 7.9 %collective-permute-start.13 = (bf16[32,2560]{1,0:T(8,128)(2,1)S(1)}, bf16[32,2560]{1,0:T(8,128)(2,1)S(1)}, u32[]{:S(2)}, u32[]{:S(2)}) collective-permute-start(bf16[32,2560]{1,0:T(8,128)(2,1)S(1)} %pad_maximum_fusion.3), channel_id=1, source_target_pairs={{0,192},{32,224},{64,0},{96,32},{128,64},{160,96},{192,128},{224,1... | collective-permute-start | bytes 491528 | tf_op jit(solution)/shard_map/ppermute | solution.py:47
  63.4 8.7 %collective-permute-start.11 = (bf16[32,2560]{1,0:T(8,128)(2,1)S(1)}, bf16[32,2560]{1,0:T(8,128)(2,1)S(1)}, u32[]{:S(2)}, u32[]{:S(2)}) collective-permute-start(bf16[32,2560]{1,0:T(8,128)(2,1)S(1)} %get-tuple-element.9), channel_id=1, source_target_pairs={{0,32},{32,64},{64,96},{96,128},{128,160},{160,192},{192,224},{224... | collective-permute-start | bytes 491528 | tf_op jit(solution)/shard_map/ppermute | solution.py:47
  65.5 6.6 %collective-permute-start.10 = (bf16[32,2560]{1,0:T(8,128)(2,1)S(1)}, bf16[32,2560]{1,0:T(8,128)(2,1)S(1)}, u32[]{:S(2)}, u32[]{:S(2)}) collective-permute-start(bf16[32,2560]{1,0:T(8,128)(2,1)S(1)} %get-tuple-element.8), channel_id=1, source_target_pairs={{0,224},{32,0},{64,32},{96,64},{128,96},{160,128},{192,160},{224,1... | collective-permute-start | bytes 491528 | tf_op jit(solution)/shard_map/ppermute | solution.py:47
  73.1 15.4 %all-to-all-start.1 = ((bf16[32,2,1280]{2,1,0:T(2,128)(2,1)}), bf16[32,2,1280]{2,1,0:T(2,128)(2,1)S(1)}, u32[]{:S(2)}, u32[]{:S(2)}) async-start(bf16[32,2,1280]{2,1,0:T(2,128)(2,1)} %copy.30), calls=%async_computation.1 | async-start | bytes 327680 | tf_op jit(solution)/shard_map/all_to_all | solution.py:83
  88.7 2.0 %copy-start.6 = (bf16[32,1,1280]{2,1,0:T(2,128)(2,1)}, bf16[32,1,1280]{2,1,0:T(2,128)(2,1)S(1)}, u32[]{:S(2)}) copy-start(bf16[32,1,1280]{2,1,0:T(2,128)(2,1)S(1)} %get-tuple-element.29) | copy-start | bytes 245764
  91.6 12.0 %all-to-all-start.2 = ((f32[32,1,1280]{2,1,0:T(1,128)}), f32[32,1,1280]{2,1,0:T(1,128)S(1)}, u32[]{:S(2)}, u32[]{:S(2)}) async-start(f32[32,1,1280]{2,1,0:T(1,128)} %copy.33), calls=%async_computation.2 | async-start | bytes 327680 | tf_op jit(solution)/shard_map/all_to_all | solution.py:83
  95.8 12.1 %copy-start.7 = (bf16[32,1,1280]{2,1,0:T(2,128)(2,1)S(1)}, bf16[32,1,1280]{2,1,0:T(2,128)(2,1)}, u32[]{:S(2)}) copy-start(bf16[32,1,1280]{2,1,0:T(2,128)(2,1)} %copy-done.6) | copy-start | bytes 245764
  98.8 22.5 %copy-start.8 = (bf16[1280,32]{0,1:T(8,128)(2,1)S(1)}, bf16[1280,32]{0,1:T(8,128)(2,1)}, u32[]{:S(2)}) copy-start(bf16[1280,32]{0,1:T(8,128)(2,1)} %param.6) | copy-start | bytes 245764
  104.3 10.5 %all-to-all-start.3 = ((f32[8,1,1280]{2,1,0:T(1,128)}), f32[8,1,1280]{2,1,0:T(1,128)S(1)}, u32[]{:S(2)}, u32[]{:S(2)}) async-start(f32[8,1,1280]{2,1,0:T(1,128)} %broadcast_in_dim.11), calls=%async_computation.3 | async-start | bytes 81920 | tf_op jit(solution)/shard_map/all_to_all | solution.py:90
  115.6 13.4 %all-to-all-start.4 = ((f32[32,1,1280]{2,1,0:T(1,128)}), f32[32,1,1280]{2,1,0:T(1,128)S(1)}, u32[]{:S(2)}, u32[]{:S(2)}) async-start(f32[32,1,1280]{2,1,0:T(1,128)} %broadcast_in_dim.12), calls=%async_computation.4 | async-start | bytes 327680 | tf_op jit(solution)/shard_map/all_to_all | solution.py:83

commit v6 on v4

--- a/solution.py
+++ b/solution.py
@@ -47,31 +47,42 @@
     return lax.ppermute(value, "dp", [(i, (i + step) % size) for i in range(size)])
 
 
+def shift_two(value):
+    size = lax.axis_size("dp")
+    pairs = [(i, (i + (2 if i % 2 == 0 else -2)) % size) for i in range(size)]
+    return lax.ppermute(value, "dp", pairs)
+
+
+def is_even():
+    return lax.axis_index("dp") % 2 == 0
+
+
 def gather_blocks(rows):
-    half = rows.shape[1] // 2
     behind_two, ahead_two = shift(rows, 2), shift(rows, -2)
-    behind_one, ahead_one = shift(rows, 1), shift(rows, -1)
-    behind_three, ahead_three = shift(behind_two, 1), shift(ahead_two, -1)
-    away = jnp.concatenate(
-        [shift(behind_two[:, :half], 2), shift(ahead_two[:, half:], -2)], axis=1
-    )
-    return jnp.concatenate(
-        [rows, behind_one, ahead_one, behind_two, ahead_two, behind_three, ahead_three, away], axis=0
-    )
+    behind = shift(jnp.concatenate([rows, behind_two], axis=0), 1)
+    ahead = shift(jnp.concatenate([rows, ahead_two], axis=0), -1)
+    away = shift_two(jnp.where(is_even(), behind_two, ahead_two))
+    return jnp.concatenate([rows, behind, ahead, behind_two, ahead_two, away], axis=0)
 
 
 def reduce_blocks(partial, rows):
-    half = partial.shape[1] // 2
-    block = [partial[i * rows : (i + 1) * rows] for i in range(8)]
-    own, behind_one, ahead_one, behind_two, ahead_two, behind_three, ahead_three, away = block
-    send = lambda value, step: shift(value.astype(jnp.bfloat16), step).astype(jnp.float32)
-    down, up = send(behind_three, -1), send(ahead_three, 1)
-    away_down, away_up = send(away[:, :half], -2), send(away[:, half:], 2)
-    near = send(behind_one, -1) + send(ahead_one, 1)
-    down, up = down + behind_two, up + ahead_two
-    down = jnp.concatenate([down[:, :half] + away_down, down[:, half:]], axis=1)
-    up = jnp.concatenate([up[:, :half], up[:, half:] + away_up], axis=1)
-    return own + near + (send(down, -2) + send(up, 2))
+    wide = jnp.float32
+    narrow = partial.astype(jnp.bfloat16)
+    own = partial[:rows]
+    down, up = shift(narrow[rows : 3 * rows], -1), shift(narrow[3 * rows : 5 * rows], 1)
+    away = shift_two(narrow[7 * rows :]).astype(wide)
+    near = down[:rows].astype(wide) + up[:rows].astype(wide)
+    nothing = jnp.zeros_like(away)
+    down_sum = partial[5 * rows : 6 * rows] + down[rows:].astype(wide)
+    up_sum = partial[6 * rows : 7 * rows] + up[rows:].astype(wide)
+    up_sum = up_sum + jnp.where(is_even(), away, nothing)
+    down_sum = down_sum + jnp.where(is_even(), nothing, away)
+    return (
+        own
+        + near
+        + shift(down_sum.astype(jnp.bfloat16), -2).astype(wide)
+        + shift(up_sum.astype(jnp.bfloat16), 2).astype(wide)
+    )
 
 
 def swap(value):

time: 130 us -> 145 us (1.12)
  waiting for transfers between devices: 37.2 us -> 53.7 us
  starting transfers between devices: 50.4 us -> 41.8 us
  local copies, waits for them, and re-layouts: 4.68 us -> 8.44 us
  other arithmetic: 3.53 us -> 5.73 us
    ppermute x16 -> x8, starting transfers between devices: 26.8 us -> 13.9 us  [shift(): lax.ppermute(value, 'dp', [(i, (i + step) % size) for i in range(size)])]
    ppermute x0 -> x2, waiting for transfers between devices: none -> 12.2 us  [shift_two(): return lax.ppermute(value, 'dp', pairs)]
    ppermute x16 -> x8, waiting for transfers between devices: 17 us -> 21.4 us  [shift(): lax.ppermute(value, 'dp', [(i, (i + step) % size) for i in range(size)])]
    unnamed x25 -> x22, local copies, waits for them, and re-layouts: 0.84 us -> 3.98 us
    all_to_all x3, starting transfers between devices: 18.4 us -> 20.8 us  [swap(): lax.all_to_all(value, ('tok', 'expert'), split_axis=0, concat_axis=0, til...]
    ppermute x0 -> x2, starting transfers between devices: none -> 1.99 us  [shift_two(): return lax.ppermute(value, 'dp', pairs)]
  transfers between devices with their start and end apart: 20 -> 14, of which waited for: 11 -> 12; matrix products, arithmetic and copies ran while one was open for 8% -> 8% of each run, Pallas kernels for 0% -> 0%
where the time goes in v6:
time: 145 us; the launch traced here: 144 us
  waiting for transfers between devices  53.7 us (37%)
  starting transfers between devices  41.8 us (29%)
  matrix products  17.5 us (12%)
  blocking collectives  16.2 us (11%)
  local copies, waits for them, and re-layouts  8.44 us (6%)
  other arithmetic  5.73 us (4%)
    ppermute x8, waiting for transfers between devices, shift(): lax.ppermute(value, 'dp', [(i, (i + step) % size) for i in range(size)])  21.4 us
    all_to_all x3, starting transfers between devices, swap(): lax.all_to_all(value, ('tok', 'expert'), split_axis=0, concat_axis=0, til...  20.8 us
    all_to_all x1, blocking collectives, swap(): lax.all_to_all(value, ('tok', 'expert'), split_axis=0, concat_axis=0, til...  16.2 us
    all_to_all x3, waiting for transfers between devices, swap(): lax.all_to_all(value, ('tok', 'expert'), split_axis=0, concat_axis=0, til...  14.7 us
    ppermute x8, starting transfers between devices, shift(): lax.ppermute(value, 'dp', [(i, (i + step) % size) for i in range(size)])  13.9 us
    ppermute x2, waiting for transfers between devices, shift_two(): return lax.ppermute(value, 'dp', pairs)  12.2 us
    all_to_all x1, waiting for transfers between devices, sum_everywhere(): seen = lax.all_to_all(copies, 'dp', split_axis=0, concat_axis=0, tiled=True)  5.46 us
    all_to_all x1, starting transfers between devices, sum_everywhere(): seen = lax.all_to_all(copies, 'dp', split_axis=0, concat_axis=0, tiled=True)  5.13 us
  transfers between devices with their start and end apart: 14, of which 12 were waited for; matrix products, arithmetic and copies ran while one was open for 8% of the time, Pallas kernels for 0%

profile of v6, /device:TPU:1, one launch (start us, length us, event | category | flops | bytes accessed | tf_op | source)
XLA Modules:
  0.0 144.4 jit_solution(18037331673126123658)
XLA Ops:
  0.7 1.6 %fusion.72 = (f32[256]{0:T(256)S(1)}, f32[256,32]{0,1:T(8,128)S(1)}) fusion(bf16[1280,32]{0,1:T(8,128)(2,1)} %param.6, bf16[1,256,1280]{2,1,0:T(8,128)(2,1)} %param.5), kind=kOutput, calls=%fused_computation.147 | convolution fusion | flops 20979456 | bytes 771072 | tf_op jit(solution)/shard_map/dot_general | solution.py:108
  2.4 0.2 exponential_reduce_fusion.6
  2.9 0.2 subtract_reduce_fusion.2
  3.1 0.2 exponential_reduce_fusion.4
  3.5 0.2 exponential_reduce_fusion.2
  4.0 0.2 subtract_reduce_fusion
  4.2 0.2 exponential_reduce_fusion
  4.4 0.3 fusion.5
  4.7 0.2 fusion.6
  4.9 0.2 copy.28
  5.1 16.2 %all_to_all.34 = bf16[32,2,1280]{2,1,0:T(2,128)(2,1)S(1)} all-to-all(bf16[32,2,1280]{2,1,0:T(2,128)(2,1)S(1)} %copy.28), channel_id=1, replica_groups=mesh['dp'=8,'tok'=2,'expert'=16] {'tok','expert'}, dimensions={0} | all-to-all | bytes 327680 | tf_op jit(solution)/shard_map/all_to_all | solution.py:89
  21.3 0.2 fusion.71
  21.6 0.7 pad_maximum_fusion.5
  22.2 3.0 %collective-permute-start = (bf16[32,2560]{1,0:T(8,128)(2,1)S(1)}, bf16[32,2560]{1,0:T(8,128)(2,1)S(1)}, u32[]{:S(2)}, u32[]{:S(2)}) collective-permute-start(bf16[32,2560]{1,0:T(8,128)(2,1)S(1)} %get-tuple-element.26), channel_id=1, source_target_pairs={{0,64},{32,96},{64,128},{96,160},{128,192},{160,224},{192,0},{224,... | collective-permute-start | bytes 491528 | tf_op jit(solution)/shard_map/ppermute | solution.py:47
  25.2 3.0 %collective-permute-start.2 = (bf16[32,2560]{1,0:T(8,128)(2,1)S(1)}, bf16[32,2560]{1,0:T(8,128)(2,1)S(1)}, u32[]{:S(2)}, u32[]{:S(2)}) collective-permute-start(bf16[32,2560]{1,0:T(8,128)(2,1)S(1)} %get-tuple-element.26), channel_id=1, source_target_pairs={{0,192},{32,224},{64,0},{96,32},{128,64},{160,96},{192,128},{224,1... | collective-permute-start | bytes 491528 | tf_op jit(solution)/shard_map/ppermute | solution.py:47
  28.3 4.6 %collective-permute-done = bf16[32,2560]{1,0:T(8,128)(2,1)S(1)} collective-permute-done((bf16[32,2560]{1,0:T(8,128)(2,1)S(1)}, bf16[32,2560]{1,0:T(8,128)(2,1)S(1)}, u32[]{:S(2)}, u32[]{:S(2)}) %collective-permute-start) | collective-permute-done | bytes 163872 | tf_op jit(solution)/shard_map/ppermute | solution.py:47
  32.9 4.2 %collective-permute-done.2 = bf16[32,2560]{1,0:T(8,128)(2,1)S(1)} collective-permute-done((bf16[32,2560]{1,0:T(8,128)(2,1)S(1)}, bf16[32,2560]{1,0:T(8,128)(2,1)S(1)}, u32[]{:S(2)}, u32[]{:S(2)}) %collective-permute-start.2) | collective-permute-done | bytes 163872 | tf_op jit(solution)/shard_map/ppermute | solution.py:47
  37.2 0.9 pad_maximum_fusion.3
  38.0 2.7 %collective-permute-start.3 = (bf16[64,2560]{1,0:T(8,128)(2,1)}, bf16[64,2560]{1,0:T(8,128)(2,1)S(1)}, u32[]{:S(2)}, u32[]{:S(2)}) collective-permute-start(bf16[64,2560]{1,0:T(8,128)(2,1)} %get-tuple-element.24), channel_id=1, source_target_pairs={{0,224},{32,0},{64,32},{96,64},{128,96},{160,128},{192,160},{224,1... | collective-permute-start | bytes 983048 | tf_op jit(solution)/shard_map/ppermute | solution.py:47
  40.7 7.1 %collective-permute-done.1 = bf16[64,2560]{1,0:T(8,128)(2,1)} collective-permute-done((bf16[64,2560]{1,0:T(8,128)(2,1)}, bf16[64,2560]{1,0:T(8,128)(2,1)}, u32[]{:S(2)}, u32[]{:S(2)}) %collective-permute-start.1) | collective-permute-done | bytes 327712 | tf_op jit(solution)/shard_map/ppermute | solution.py:47
  47.8 1.8 %constant_dynamic-update-slice_fusion.4 = bf16[256,2560]{1,0:T(8,128)(2,1)} fusion(bf16[256,2560]{1,0:T(8,128)(2,1)} %get-tuple-element.27, bf16[64,2560]{1,0:T(8,128)(2,1)} %collective-permute-done.1), kind=kLoop, calls=%fused_computation.119 | loop fusion | bytes 655360
  49.7 0.7 constant_dynamic-update-slice_fusion.3
  50.4 0.7 constant_dynamic-update-slice_fusion.2
  51.1 0.7 broadcast_select_fusion
  51.8 1.6 %collective-permute-start.4 = (bf16[32,2560]{1,0:T(8,128)(2,1)S(1)}, bf16[32,2560]{1,0:T(8,128)(2,1)S(1)}, u32[]{:S(2)}, u32[]{:S(2)}) collective-permute-start(bf16[32,2560]{1,0:T(8,128)(2,1)S(1)} %get-tuple-element.22), channel_id=1, source_target_pairs={{0,64},{32,224},{64,128},{96,32},{128,192},{160,96},{192,0},{224,1... | collective-permute-start | bytes 491528 | tf_op jit(solution)/shard_map/ppermute | solution.py:53
  53.3 4.7 %collective-permute-done.4 = bf16[32,2560]{1,0:T(8,128)(2,1)S(1)} collective-permute-done((bf16[32,2560]{1,0:T(8,128)(2,1)S(1)}, bf16[32,2560]{1,0:T(8,128)(2,1)S(1)}, u32[]{:S(2)}, u32[]{:S(2)}) %collective-permute-start.4) | collective-permute-done | bytes 163872 | tf_op jit(solution)/shard_map/ppermute | solution.py:53
  58.1 0.7 constant_dynamic-update-slice_fusion
  58.7 1.9 %fusion.13 = f32[256,640]{1,0:T(8,128)S(1)} fusion(bf16[1,1280,640]{2,1,0:T(8,128)(2,1)S(1)} %copy-done.2, bf16[256,2560]{1,0:T(8,128)(2,1)} %constant_dynamic-update-slice_fusion), kind=kOutput, calls=%fused_computation.26 | convolution fusion | flops 419430400 | bytes 2949120 | tf_op jit(solution)/shard_map/dot_general | solution.py:125
  60.7 0.8 fusion.18
  61.5 0.8 fusion.9
  62.3 0.7 fusion.11
  63.0 0.1 fusion.2
  63.2 0.5 collective-permute-start.5
  63.7 1.0 collective-permute-start.6
  64.8 0.4 collective-permute-start.7
  65.2 7.5 %collective-permute-done.7 = bf16[32,2560]{1,0:T(8,128)(2,1)S(1)} collective-permute-done((bf16[32,2560]{1,0:T(8,128)(2,1)S(1)}, bf16[32,2560]{1,0:T(8,128)(2,1)S(1)}, u32[]{:S(2)}, u32[]{:S(2)}) %collective-permute-start.7) | collective-permute-done | bytes 163872 | tf_op jit(solution)/shard_map/ppermute | solution.py:53
  72.7 0.8 collective-permute-done.6
  73.6 1.4 collective-permute-start.9
  75.0 2.2 %collective-permute-start.8 = (bf16[32,2560]{1,0:T(8,128)(2,1)S(1)}, bf16[32,2560]{1,0:T(8,128)(2,1)S(1)}, u32[]{:S(2)}, u32[]{:S(2)}) collective-permute-start(bf16[32,2560]{1,0:T(8,128)(2,1)S(1)} %get-tuple-element.14), channel_id=1, source_target_pairs={{0,192},{32,224},{64,0},{96,32},{128,64},{160,96},{192,128},{224,1... | collective-permute-start | bytes 491528 | tf_op jit(solution)/shard_map/ppermute | solution.py:47
  77.2 2.9 %collective-permute-done.9 = bf16[32,2560]{1,0:T(8,128)(2,1)S(1)} collective-permute-done((bf16[32,2560]{1,0:T(8,128)(2,1)S(1)}, bf16[32,2560]{1,0:T(8,128)(2,1)S(1)}, u32[]{:S(2)}, u32[]{:S(2)}) %collective-permute-start.9) | collective-permute-done | bytes 163872 | tf_op jit(solution)/shard_map/ppermute | solution.py:47
  80.1 1.8 %collective-permute-done.8 = bf16[32,2560]{1,0:T(8,128)(2,1)S(1)} collective-permute-done((bf16[32,2560]{1,0:T(8,128)(2,1)S(1)}, bf16[32,2560]{1,0:T(8,128)(2,1)S(1)}, u32[]{:S(2)}, u32[]{:S(2)}) %collective-permute-start.8) | collective-permute-done | bytes 163872 | tf_op jit(solution)/shard_map/ppermute | solution.py:47
  82.0 0.8 copy.31
  82.8 11.0 %all-to-all-start.1 = ((bf16[32,2,1280]{2,1,0:T(2,128)(2,1)}), bf16[32,2,1280]{2,1,0:T(2,128)(2,1)S(1)}, u32[]{:S(2)}, u32[]{:S(2)}) async-start(bf16[32,2,1280]{2,1,0:T(2,128)(2,1)} %copy.31), calls=%async_computation.1 | async-start | bytes 327680 | tf_op jit(solution)/shard_map/all_to_all | solution.py:89
  93.8 3.2 %fusion.1 = bf16[1,640,1280]{2,1,0:T(8,128)(2,1)} fusion(bf16[256,2560]{1,0:T(8,128)(2,1)} %constant_dynamic-update-slice_fusion, f32[256,640]{1,0:T(8,128)} %copy-done.4), kind=kOutput, calls=%fused_computation.10 | convolution fusion | flops 421724160 | bytes 2949120 | tf_op jit(solution)/shard_map/dot_general | solution.py:142
  97.0 4.6 %all-to-all-done.1 = bf16[32,2,1280]{2,1,0:T(2,128)(2,1)S(1)} async-done(((bf16[32,2,1280]{2,1,0:T(2,128)(2,1)}), bf16[32,2,1280]{2,1,0:T(2,128)(2,1)S(1)}, u32[]{:S(2)}, u32[]{:S(2)}) %all-to-all-start.1) | async-done | bytes 163872 | tf_op jit(solution)/shard_map/all_to_all | solution.py:89
  101.6 0.2 fusion.70
  101.9 0.4 fusion.73
  102.4 0.2 fusion.54
  102.9 0.2 fusion.56
  103.1 0.4 multiply_reduce_fusion
  103.6 0.2 convolution_bitcast_fusion
  103.8 0.8 copy.34
  104.7 4.2 %all-to-all-start.2 = ((f32[32,1,1280]{2,1,0:T(1,128)}), f32[32,1,1280]{2,1,0:T(1,128)S(1)}, u32[]{:S(2)}, u32[]{:S(2)}) async-start(f32[32,1,1280]{2,1,0:T(1,128)} %copy.34), calls=%async_computation.2 | async-start | bytes 327680 | tf_op jit(solution)/shard_map/all_to_all | solution.py:89
  108.9 3.0 %fusion = bf16[1,1280,640]{2,1,0:T(8,128)(2,1)} fusion(bf16[256,640]{1,0:T(8,128)(2,1)S(1)} %fusion.18, bf16[256,2560]{1,0:T(8,128)(2,1)} %constant_dynamic-update-slice_fusion), kind=kOutput, calls=%fused_computation.9 | convolution fusion | flops 420249600 | bytes 2621440 | tf_op jit(solution)/shard_map/dot_general | solution.py:139
  111.9 4.8 %all-to-all-done.2 = f32[32,1,1280]{2,1,0:T(1,128)S(1)} async-done(((f32[32,1,1280]{2,1,0:T(1,128)}), f32[32,1,1280]{2,1,0:T(1,128)S(1)}, u32[]{:S(2)}, u32[]{:S(2)}) %all-to-all-start.2) | async-done | bytes 163872 | tf_op jit(solution)/shard_map/all_to_all | solution.py:89
  116.8 0.6 broadcast_in_dim.14
  117.4 5.1 %all-to-all-start.3 = ((f32[8,1,1280]{2,1,0:T(1,128)}), f32[8,1,1280]{2,1,0:T(1,128)S(1)}, u32[]{:S(2)}, u32[]{:S(2)}) async-start(f32[8,1,1280]{2,1,0:T(1,128)} %broadcast_in_dim.14), calls=%async_computation.3 | async-start | bytes 81920 | tf_op jit(solution)/shard_map/all_to_all | solution.py:96
  122.6 1.5 %fusion.51 = f32[256,1280]{1,0:T(8,128)} fusion(bf16[32,1,1280]{2,1,0:T(2,128)(2,1)S(1)} %copy-done.7, f32[32]{0:T(128)S(1)} %log_add_fusion.4, f32[256]{0:T(256)S(1)} %log_add_fusion, f32[256,32]{0,1:T(8,128)S(1)} %get-tuple-element.13, f32[32]{0:T(128)S(1)} %log_add_fusion.5, f32[256]{0:T(256)S(1)} %log_add_fusion.1), kind=kOutput, calls=%fused_computation.100 | convolution fusion | flops 21012480 | bytes 1427712 | tf_op jit(solution)/shard_map/dot_general | solution.py:164
  124.1 5.5 %all-to-all-done.3 = f32[8,1,1280]{2,1,0:T(1,128)S(1)} async-done(((f32[8,1,1280]{2,1,0:T(1,128)}), f32[8,1,1280]{2,1,0:T(1,128)S(1)}, u32[]{:S(2)}, u32[]{:S(2)}) %all-to-all-start.3) | async-done | bytes 40992 | tf_op jit(solution)/shard_map/all_to_all | solution.py:96
  129.6 0.8 broadcast_in_dim.15
  130.3 5.6 %all-to-all-start.4 = ((f32[32,1,1280]{2,1,0:T(1,128)}), f32[32,1,1280]{2,1,0:T(1,128)S(1)}, u32[]{:S(2)}, u32[]{:S(2)}) async-start(f32[32,1,1280]{2,1,0:T(1,128)} %broadcast_in_dim.15), calls=%async_computation.4 | async-start | bytes 327680 | tf_op jit(solution)/shard_map/all_to_all | solution.py:89
  136.0 2.5 %fusion.4 = bf16[1,256,1280]{2,1,0:T(8,128)(2,1)} fusion(f32[256,1280]{1,0:T(8,128)} %fusion.51, bf16[256,32]{0,1:T(8,128)(2,1)S(1)} %add_convert_fusion, bf16[1280,32]{0,1:T(8,128)(2,1)S(1)} %copy-done.8), kind=kOutput, calls=%fused_computation.14 | convolution fusion | flops 21626880 | bytes 2064384 | tf_op jit(solution)/shard_map/dot_general | solution.py:165
  138.5 5.3 %all-to-all-done.4 = f32[32,1,1280]{2,1,0:T(1,128)S(1)} async-done(((f32[32,1,1280]{2,1,0:T(1,128)}), f32[32,1,1280]{2,1,0:T(1,128)S(1)}, u32[]{:S(2)}, u32[]{:S(2)}) %all-to-all-start.4) | async-done | bytes 163872 | tf_op jit(solution)/shard_map/all_to_all | solution.py:89
  143.8 0.7 copy.54
  (61 shorter events, 2.0 us)
Async XLA Ops:
  0.6 60.0 %copy-start = (bf16[1,640,1280]{2,1,0:T(8,128)(2,1)S(1)}, bf16[1,640,1280]{2,1,0:T(8,128)(2,1)}, u32[]{:S(2)}) copy-start(bf16[1,640,1280]{2,1,0:T(8,128)(2,1)} %param.8) | copy-start | bytes 4915204
  0.6 3.7 %copy-start.1 = (bf16[1,256,1280]{2,1,0:T(8,128)(2,1)S(1)}, bf16[1,256,1280]{2,1,0:T(8,128)(2,1)}, u32[]{:S(2)}) copy-start(bf16[1,256,1280]{2,1,0:T(8,128)(2,1)} %param.5) | copy-start | bytes 1966084
  0.7 4.0 %copy-start.3 = (bf16[1,256,1280]{2,1,0:T(8,128)(2,1)S(1)}, bf16[1,256,1280]{2,1,0:T(8,128)(2,1)}, u32[]{:S(2)}) copy-start(bf16[1,256,1280]{2,1,0:T(8,128)(2,1)} %param.9) | copy-start | bytes 1966084
  22.2 10.7 %collective-permute-start = (bf16[32,2560]{1,0:T(8,128)(2,1)S(1)}, bf16[32,2560]{1,0:T(8,128)(2,1)S(1)}, u32[]{:S(2)}, u32[]{:S(2)}) collective-permute-start(bf16[32,2560]{1,0:T(8,128)(2,1)S(1)} %get-tuple-element.26), channel_id=1, source_target_pairs={{0,64},{32,96},{64,128},{96,160},{128,192},{160,224},{192,0},{224,... | collective-permute-start | bytes 491528 | tf_op jit(solution)/shard_map/ppermute | solution.py:47
  25.2 11.9 %collective-permute-start.2 = (bf16[32,2560]{1,0:T(8,128)(2,1)S(1)}, bf16[32,2560]{1,0:T(8,128)(2,1)S(1)}, u32[]{:S(2)}, u32[]{:S(2)}) collective-permute-start(bf16[32,2560]{1,0:T(8,128)(2,1)S(1)} %get-tuple-element.26), channel_id=1, source_target_pairs={{0,192},{32,224},{64,0},{96,32},{128,64},{160,96},{192,128},{224,1... | collective-permute-start | bytes 491528 | tf_op jit(solution)/shard_map/ppermute | solution.py:47
  38.0 9.8 %collective-permute-start.1 = (bf16[64,2560]{1,0:T(8,128)(2,1)}, bf16[64,2560]{1,0:T(8,128)(2,1)}, u32[]{:S(2)}, u32[]{:S(2)}) collective-permute-start(bf16[64,2560]{1,0:T(8,128)(2,1)} %get-tuple-element.25), channel_id=1, source_target_pairs={{0,32},{32,64},{64,96},{96,128},{128,160},{160,192},{192,224},{224... | collective-permute-start | bytes 983048 | tf_op jit(solution)/shard_map/ppermute | solution.py:47
  38.0 11.6 %collective-permute-start.3 = (bf16[64,2560]{1,0:T(8,128)(2,1)}, bf16[64,2560]{1,0:T(8,128)(2,1)S(1)}, u32[]{:S(2)}, u32[]{:S(2)}) collective-permute-start(bf16[64,2560]{1,0:T(8,128)(2,1)} %get-tuple-element.24), channel_id=1, source_target_pairs={{0,224},{32,0},{64,32},{96,64},{128,96},{160,128},{192,160},{224,1... | collective-permute-start | bytes 983048 | tf_op jit(solution)/shard_map/ppermute | solution.py:47
  47.8 10.9 %copy-start.2 = (bf16[1,1280,640]{2,1,0:T(8,128)(2,1)S(1)}, bf16[1,1280,640]{2,1,0:T(8,128)(2,1)}, u32[]{:S(2)}) copy-start(bf16[1,1280,640]{2,1,0:T(8,128)(2,1)} %param.7) | copy-start | bytes 4915204
  51.8 6.3 %collective-permute-start.4 = (bf16[32,2560]{1,0:T(8,128)(2,1)S(1)}, bf16[32,2560]{1,0:T(8,128)(2,1)S(1)}, u32[]{:S(2)}, u32[]{:S(2)}) collective-permute-start(bf16[32,2560]{1,0:T(8,128)(2,1)S(1)} %get-tuple-element.22), channel_id=1, source_target_pairs={{0,64},{32,224},{64,128},{96,32},{128,192},{160,96},{192,0},{224,1... | collective-permute-start | bytes 491528 | tf_op jit(solution)/shard_map/ppermute | solution.py:53
  58.7 1.9 %copy-start.5 = (bf16[256,2560]{1,0:T(8,128)(2,1)S(1)}, bf16[256,2560]{1,0:T(8,128)(2,1)}, u32[]{:S(2)}) copy-start(bf16[256,2560]{1,0:T(8,128)(2,1)} %constant_dynamic-update-slice_fusion) | copy-start | bytes 3932164
  60.7 0.8 copy-start.4
  63.2 9.5 %collective-permute-start.5 = (bf16[64,2560]{1,0:T(8,128)(2,1)S(1)}, bf16[64,2560]{1,0:T(8,128)(2,1)S(1)}, u32[]{:S(2)}, u32[]{:S(2)}) collective-permute-start(bf16[64,2560]{1,0:T(8,128)(2,1)S(1)} %get-tuple-element.16), channel_id=1, source_target_pairs={{0,224},{32,0},{64,32},{96,64},{128,96},{160,128},{192,160},{224,1... | collective-permute-start | bytes 983048 | tf_op jit(solution)/shard_map/ppermute | solution.py:47
  63.7 9.7 %collective-permute-start.6 = (bf16[64,2560]{1,0:T(8,128)(2,1)S(1)}, bf16[64,2560]{1,0:T(8,128)(2,1)S(1)}, u32[]{:S(2)}, u32[]{:S(2)}) collective-permute-start(bf16[64,2560]{1,0:T(8,128)(2,1)S(1)} %get-tuple-element.17), channel_id=1, source_target_pairs={{0,32},{32,64},{64,96},{96,128},{128,160},{160,192},{192,224},{224... | collective-permute-start | bytes 983048 | tf_op jit(solution)/shard_map/ppermute | solution.py:47
  64.8 7.9 %collective-permute-start.7 = (bf16[32,2560]{1,0:T(8,128)(2,1)S(1)}, bf16[32,2560]{1,0:T(8,128)(2,1)S(1)}, u32[]{:S(2)}, u32[]{:S(2)}) collective-permute-start(bf16[32,2560]{1,0:T(8,128)(2,1)S(1)} %slice.85), channel_id=1, source_target_pairs={{0,64},{32,224},{64,128},{96,32},{128,192},{160,96},{192,0},{224,1... | collective-permute-start | bytes 491528 | tf_op jit(solution)/shard_map/ppermute | solution.py:53
  73.6 6.5 %collective-permute-start.9 = (bf16[32,2560]{1,0:T(8,128)(2,1)S(1)}, bf16[32,2560]{1,0:T(8,128)(2,1)S(1)}, u32[]{:S(2)}, u32[]{:S(2)}) collective-permute-start(bf16[32,2560]{1,0:T(8,128)(2,1)S(1)} %get-tuple-element.15), channel_id=1, source_target_pairs={{0,64},{32,96},{64,128},{96,160},{128,192},{160,224},{192,0},{224,... | collective-permute-start | bytes 491528 | tf_op jit(solution)/shard_map/ppermute | solution.py:47
  75.0 6.9 %collective-permute-start.8 = (bf16[32,2560]{1,0:T(8,128)(2,1)S(1)}, bf16[32,2560]{1,0:T(8,128)(2,1)S(1)}, u32[]{:S(2)}, u32[]{:S(2)}) collective-permute-start(bf16[32,2560]{1,0:T(8,128)(2,1)S(1)} %get-tuple-element.14), channel_id=1, source_target_pairs={{0,192},{32,224},{64,0},{96,32},{128,64},{160,96},{192,128},{224,1... | collective-permute-start | bytes 491528 | tf_op jit(solution)/shard_map/ppermute | solution.py:47
  82.8 18.8 %all-to-all-start.1 = ((bf16[32,2,1280]{2,1,0:T(2,128)(2,1)}), bf16[32,2,1280]{2,1,0:T(2,128)(2,1)S(1)}, u32[]{:S(2)}, u32[]{:S(2)}) async-start(bf16[32,2,1280]{2,1,0:T(2,128)(2,1)} %copy.31), calls=%async_computation.1 | async-start | bytes 327680 | tf_op jit(solution)/shard_map/all_to_all | solution.py:89
  101.8 2.0 %copy-start.6 = (bf16[32,1,1280]{2,1,0:T(2,128)(2,1)}, bf16[32,1,1280]{2,1,0:T(2,128)(2,1)S(1)}, u32[]{:S(2)}) copy-start(bf16[32,1,1280]{2,1,0:T(2,128)(2,1)S(1)} %get-tuple-element.19) | copy-start | bytes 245764
  104.7 12.0 %all-to-all-start.2 = ((f32[32,1,1280]{2,1,0:T(1,128)}), f32[32,1,1280]{2,1,0:T(1,128)S(1)}, u32[]{:S(2)}, u32[]{:S(2)}) async-start(f32[32,1,1280]{2,1,0:T(1,128)} %copy.34), calls=%async_computation.2 | async-start | bytes 327680 | tf_op jit(solution)/shard_map/all_to_all | solution.py:89
  108.9 13.7 %copy-start.7 = (bf16[32,1,1280]{2,1,0:T(2,128)(2,1)S(1)}, bf16[32,1,1280]{2,1,0:T(2,128)(2,1)}, u32[]{:S(2)}) copy-start(bf16[32,1,1280]{2,1,0:T(2,128)(2,1)} %copy-done.6) | copy-start | bytes 245764
  111.9 24.1 %copy-start.8 = (bf16[1280,32]{0,1:T(8,128)(2,1)S(1)}, bf16[1280,32]{0,1:T(8,128)(2,1)}, u32[]{:S(2)}) copy-start(bf16[1280,32]{0,1:T(8,128)(2,1)} %param.6) | copy-start | bytes 245764
  117.4 12.1 %all-to-all-start.3 = ((f32[8,1,1280]{2,1,0:T(1,128)}), f32[8,1,1280]{2,1,0:T(1,128)S(1)}, u32[]{:S(2)}, u32[]{:S(2)}) async-start(f32[8,1,1280]{2,1,0:T(1,128)} %broadcast_in_dim.14), calls=%async_computation.3 | async-start | bytes 81920 | tf_op jit(solution)/shard_map/all_to_all | solution.py:96
  130.3 13.4 %all-to-all-start.4 = ((f32[32,1,1280]{2,1,0:T(1,128)}), f32[32,1,1280]{2,1,0:T(1,128)S(1)}, u32[]{:S(2)}, u32[]{:S(2)}) async-start(f32[32,1,1280]{2,1,0:T(1,128)} %broadcast_in_dim.15), calls=%async_computation.4 | async-start | bytes 327680 | tf_op jit(solution)/shard_map/all_to_all | solution.py:89

commit v7 on v4

--- a/solution.py
+++ b/solution.py
@@ -80,10 +80,13 @@
 
 def sum_everywhere(part):
     slots, width = part.shape
-    mine = jnp.sum(swap(part), axis=0, keepdims=True)
-    copies = jnp.broadcast_to(mine, (lax.axis_size("dp"), width))
+    halves = part.astype(jnp.bfloat16).reshape(slots, 2, width // 2)
+    mine = jnp.sum(swap(halves).astype(jnp.float32), axis=0, keepdims=True)
+    copies = jnp.broadcast_to(mine, (lax.axis_size("dp"), 2, width // 2))
     seen = lax.all_to_all(copies, "dp", split_axis=0, concat_axis=0, tiled=True)
-    return swap(jnp.broadcast_to(jnp.sum(seen, axis=0, keepdims=True), (slots, width)))
+    total = jnp.sum(seen, axis=0, keepdims=True).astype(jnp.bfloat16)
+    everywhere = swap(jnp.broadcast_to(total, (slots, 2, width // 2)))
+    return everywhere.reshape(slots, width).astype(jnp.float32)
 
 
 def paired_swap(first, second):

time: 130 us -> 128 us (0.985)
  waiting for transfers between devices: 37.2 us -> 35.8 us
    all_to_all x3, waiting for transfers between devices: 14.7 us -> 13.4 us  [swap(): lax.all_to_all(value, ('tok', 'expert'), split_axis=0, concat_axis=0, til...]
where the time goes in v7:
time: 128 us
  starting transfers between devices  50.4 us (39%)
  waiting for transfers between devices  35.8 us (28%)
  matrix products  16.3 us (13%)
  blocking collectives  16.2 us (13%)
  local copies, waits for them, and re-layouts  4.43 us (3%)
  other arithmetic  3.49 us (3%)
    ppermute x16, starting transfers between devices, shift(): lax.ppermute(value, 'dp', [(i, (i + step) % size) for i in range(size)])  26.8 us
    all_to_all x3, starting transfers between devices, swap(): lax.all_to_all(value, ('tok', 'expert'), split_axis=0, concat_axis=0, til...  18.4 us
    ppermute x16, waiting for transfers between devices, shift(): lax.ppermute(value, 'dp', [(i, (i + step) % size) for i in range(size)])  17 us
    all_to_all x1, blocking collectives, swap(): lax.all_to_all(value, ('tok', 'expert'), split_axis=0, concat_axis=0, til...  16.2 us
    all_to_all x3, waiting for transfers between devices, swap(): lax.all_to_all(value, ('tok', 'expert'), split_axis=0, concat_axis=0, til...  13.4 us
    all_to_all x1, waiting for transfers between devices, sum_everywhere(): seen = lax.all_to_all(copies, 'dp', split_axis=0, concat_axis=0, tiled=True)  5.46 us
    all_to_all x1, starting transfers between devices, sum_everywhere(): seen = lax.all_to_all(copies, 'dp', split_axis=0, concat_axis=0, tiled=True)  5.23 us
    dot_general x1, matrix products, body(): lax.dot_general(hidden_act, all_grad, (((0,), (0,)), ((), ())), preferred...  3.2 us
  transfers between devices with their start and end apart: 20, of which 11 were waited for; matrix products, arithmetic and copies ran while one was open for 8% of the time, Pallas kernels for 0%

profile of v7, /device:TPU:1, one launch (start us, length us, event | category | flops | bytes accessed | tf_op | source)
XLA Modules:
  0.0 127.8 jit_solution(14192269475115274033)
XLA Ops:
  0.7 1.6 %fusion.69 = (f32[256]{0:T(256)S(1)}, f32[256,32]{0,1:T(8,128)S(1)}) fusion(bf16[1280,32]{0,1:T(8,128)(2,1)} %param.6, bf16[1,256,1280]{2,1,0:T(8,128)(2,1)} %param.5), kind=kOutput, calls=%fused_computation.148 | convolution fusion | flops 20979456 | bytes 771072 | tf_op jit(solution)/shard_map/dot_general | solution.py:100
  2.3 0.1 subtract_reduce_fusion.3
  2.4 0.2 exponential_reduce_fusion.6
  2.7 0.1 exponential_reduce_fusion.5
  2.9 0.2 subtract_reduce_fusion.2
  3.1 0.2 exponential_reduce_fusion.4
  3.4 0.1 subtract_reduce_fusion.1
  3.5 0.2 exponential_reduce_fusion.2
  3.9 0.1 exponential_reduce_fusion.1
  4.0 0.2 subtract_reduce_fusion
  4.2 0.2 exponential_reduce_fusion
  4.4 0.3 fusion.5
  4.7 0.2 fusion.6
  4.9 0.2 copy.24
  5.1 16.2 %all_to_all.25 = bf16[32,2,1280]{2,1,0:T(2,128)(2,1)S(1)} all-to-all(bf16[32,2,1280]{2,1,0:T(2,128)(2,1)S(1)} %copy.24), channel_id=1, replica_groups=mesh['dp'=8,'tok'=2,'expert'=16] {'tok','expert'}, dimensions={0} | all-to-all | bytes 327680 | tf_op jit(solution)/shard_map/all_to_all | solution.py:78
  21.3 0.2 fusion.68
  21.6 6.1 %collective-permute-start.3 = (bf16[32,2560]{1,0:T(8,128)(2,1)S(1)}, bf16[32,2560]{1,0:T(8,128)(2,1)S(1)}, u32[]{:S(2)}, u32[]{:S(2)}) collective-permute-start(bf16[32,2560]{1,0:T(8,128)(2,1)S(1)} %get-tuple-element.24), channel_id=1, source_target_pairs={{0,192},{32,224},{64,0},{96,32},{128,64},{160,96},{192,128},{224,1... | collective-permute-start | bytes 491528 | tf_op jit(solution)/shard_map/ppermute | solution.py:47
  27.7 0.7 collective-permute-start
  28.5 2.4 %collective-permute-start.1 = (bf16[32,2560]{1,0:T(8,128)(2,1)S(1)}, bf16[32,2560]{1,0:T(8,128)(2,1)S(1)}, u32[]{:S(2)}, u32[]{:S(2)}) collective-permute-start(bf16[32,2560]{1,0:T(8,128)(2,1)S(1)} %get-tuple-element.24), channel_id=1, source_target_pairs={{0,224},{32,0},{64,32},{96,64},{128,96},{160,128},{192,160},{224,1... | collective-permute-start | bytes 491528 | tf_op jit(solution)/shard_map/ppermute | solution.py:47
  30.9 3.3 %collective-permute-done.3 = bf16[32,2560]{1,0:T(8,128)(2,1)S(1)} collective-permute-done((bf16[32,2560]{1,0:T(8,128)(2,1)S(1)}, bf16[32,2560]{1,0:T(8,128)(2,1)S(1)}, u32[]{:S(2)}, u32[]{:S(2)}) %collective-permute-start.3) | collective-permute-done | bytes 163872 | tf_op jit(solution)/shard_map/ppermute | solution.py:47
  34.1 4.8 %collective-permute-start.7 = (bf16[32,1280]{1,0:T(8,128)(2,1)S(1)}, bf16[32,1280]{1,0:T(8,128)(2,1)S(1)}, u32[]{:S(2)}, u32[]{:S(2)}) collective-permute-start(bf16[32,1280]{1,0:T(8,128)(2,1)S(1)} %slice.108), channel_id=1, source_target_pairs={{0,192},{32,224},{64,0},{96,32},{128,64},{160,96},{192,128},{224,1... | collective-permute-start | bytes 245768 | tf_op jit(solution)/shard_map/ppermute | solution.py:47
  39.1 2.9 %collective-permute-done = bf16[32,2560]{1,0:T(8,128)(2,1)S(1)} collective-permute-done((bf16[32,2560]{1,0:T(8,128)(2,1)S(1)}, bf16[32,2560]{1,0:T(8,128)(2,1)S(1)}, u32[]{:S(2)}, u32[]{:S(2)}) %collective-permute-start) | collective-permute-done | bytes 163872 | tf_op jit(solution)/shard_map/ppermute | solution.py:47
  42.1 4.4 %collective-permute-done.4 = bf16[32,2560]{1,0:T(8,128)(2,1)S(1)} collective-permute-done((bf16[32,2560]{1,0:T(8,128)(2,1)S(1)}, bf16[32,2560]{1,0:T(8,128)(2,1)S(1)}, u32[]{:S(2)}, u32[]{:S(2)}) %collective-permute-start.4) | collective-permute-done | bytes 163872 | tf_op jit(solution)/shard_map/ppermute | solution.py:47
  46.6 0.2 collective-permute-done.5
  46.8 0.7 fusion.13
  47.5 0.8 fusion.9
  48.3 0.8 fusion.18
  49.2 0.7 fusion.11
  49.9 0.1 fusion.2
  50.1 2.5 %collective-permute-start.10 = (bf16[32,2560]{1,0:T(8,128)(2,1)S(1)}, bf16[32,2560]{1,0:T(8,128)(2,1)S(1)}, u32[]{:S(2)}, u32[]{:S(2)}) collective-permute-start(bf16[32,2560]{1,0:T(8,128)(2,1)S(1)} %get-tuple-element.18), channel_id=1, source_target_pairs={{0,224},{32,0},{64,32},{96,64},{128,96},{160,128},{192,160},{224,1... | collective-permute-start | bytes 491528 | tf_op jit(solution)/shard_map/ppermute | solution.py:47
  52.7 3.6 %collective-permute-start.11 = (bf16[32,1280]{1,0:T(8,128)(2,1)S(1)}, bf16[32,1280]{1,0:T(8,128)(2,1)S(1)}, u32[]{:S(2)}, u32[]{:S(2)}) collective-permute-start(bf16[32,1280]{1,0:T(8,128)(2,1)S(1)} %slice.182), channel_id=1, source_target_pairs={{0,192},{32,224},{64,0},{96,32},{128,64},{160,96},{192,128},{224,1... | collective-permute-start | bytes 245768 | tf_op jit(solution)/shard_map/ppermute | solution.py:47
  56.3 0.4 collective-permute-start.9
  56.7 2.3 %collective-permute-start.8 = (bf16[32,2560]{1,0:T(8,128)(2,1)S(1)}, bf16[32,2560]{1,0:T(8,128)(2,1)S(1)}, u32[]{:S(2)}, u32[]{:S(2)}) collective-permute-start(bf16[32,2560]{1,0:T(8,128)(2,1)S(1)} %get-tuple-element.16), channel_id=1, source_target_pairs={{0,224},{32,0},{64,32},{96,64},{128,96},{160,128},{192,160},{224,1... | collective-permute-start | bytes 491528 | tf_op jit(solution)/shard_map/ppermute | solution.py:47
  59.1 0.5 collective-permute-done.14
  59.8 3.6 %collective-permute-start.12 = (bf16[32,2560]{1,0:T(8,128)(2,1)S(1)}, bf16[32,2560]{1,0:T(8,128)(2,1)S(1)}, u32[]{:S(2)}, u32[]{:S(2)}) collective-permute-start(bf16[32,2560]{1,0:T(8,128)(2,1)S(1)} %pad_maximum_fusion.3), channel_id=1, source_target_pairs={{0,192},{32,224},{64,0},{96,32},{128,64},{160,96},{192,128},{224,1... | collective-permute-start | bytes 491528 | tf_op jit(solution)/shard_map/ppermute | solution.py:47
  63.4 1.9 %collective-permute-done.9 = bf16[32,2560]{1,0:T(8,128)(2,1)S(1)} collective-permute-done((bf16[32,2560]{1,0:T(8,128)(2,1)S(1)}, bf16[32,2560]{1,0:T(8,128)(2,1)S(1)}, u32[]{:S(2)}, u32[]{:S(2)}) %collective-permute-start.9) | collective-permute-done | bytes 163872 | tf_op jit(solution)/shard_map/ppermute | solution.py:47
  65.3 3.9 %collective-permute-done.15 = bf16[32,2560]{1,0:T(8,128)(2,1)S(1)} collective-permute-done((bf16[32,2560]{1,0:T(8,128)(2,1)S(1)}, bf16[32,2560]{1,0:T(8,128)(2,1)S(1)}, u32[]{:S(2)}, u32[]{:S(2)}) %collective-permute-start.15) | collective-permute-done | bytes 163872 | tf_op jit(solution)/shard_map/ppermute | solution.py:47
  69.2 0.1 fusion.41
  69.3 0.8 copy.27
  70.2 8.6 %all-to-all-start.1 = ((bf16[32,2,1280]{2,1,0:T(2,128)(2,1)}), bf16[32,2,1280]{2,1,0:T(2,128)(2,1)S(1)}, u32[]{:S(2)}, u32[]{:S(2)}) async-start(bf16[32,2,1280]{2,1,0:T(2,128)(2,1)} %copy.27), calls=%async_computation.1 | async-start | bytes 327680 | tf_op jit(solution)/shard_map/all_to_all | solution.py:78
  78.8 3.2 %fusion.1 = bf16[1,640,1280]{2,1,0:T(8,128)(2,1)} fusion(bf16[256,2560]{1,0:T(8,128)(2,1)} %copy-done.5, f32[256,640]{1,0:T(8,128)} %copy-done.4), kind=kOutput, calls=%fused_computation.10 | convolution fusion | flops 421724160 | bytes 2949120 | tf_op jit(solution)/shard_map/dot_general | solution.py:134
  82.0 4.6 %all-to-all-done.1 = bf16[32,2,1280]{2,1,0:T(2,128)(2,1)S(1)} async-done(((bf16[32,2,1280]{2,1,0:T(2,128)(2,1)}), bf16[32,2,1280]{2,1,0:T(2,128)(2,1)S(1)}, u32[]{:S(2)}, u32[]{:S(2)}) %all-to-all-start.1) | async-done | bytes 163872 | tf_op jit(solution)/shard_map/all_to_all | solution.py:78
  86.6 0.2 fusion.67
  86.8 0.4 fusion.70
  87.2 0.1 fusion.60
  87.4 0.2 fusion.51
  87.6 0.1 fusion.64
  87.7 0.1 fusion.52
  87.9 0.2 fusion.53
  88.1 0.4 multiply_reduce_fusion
  88.5 0.2 convolution_convert_fusion.2
  88.8 0.7 reshape.158
  89.5 4.2 %all-to-all-start.2 = ((bf16[32,2,640]{2,1,0:T(2,128)(2,1)}), bf16[32,2,640]{2,1,0:T(2,128)(2,1)S(1)}, u32[]{:S(2)}, u32[]{:S(2)}) async-start(bf16[32,2,640]{2,1,0:T(2,128)(2,1)} %reshape.158), calls=%async_computation.2 | async-start | bytes 163840 | tf_op jit(solution)/shard_map/all_to_all | solution.py:78
  93.7 3.0 %fusion = bf16[1,1280,640]{2,1,0:T(8,128)(2,1)} fusion(bf16[256,640]{1,0:T(8,128)(2,1)S(1)} %fusion.18, bf16[256,2560]{1,0:T(8,128)(2,1)} %copy-done.5), kind=kOutput, calls=%fused_computation.9 | convolution fusion | flops 420249600 | bytes 2621440 | tf_op jit(solution)/shard_map/dot_general | solution.py:131
  96.7 4.1 %all-to-all-done.2 = bf16[32,2,640]{2,1,0:T(2,128)(2,1)S(1)} async-done(((bf16[32,2,640]{2,1,0:T(2,128)(2,1)}), bf16[32,2,640]{2,1,0:T(2,128)(2,1)S(1)}, u32[]{:S(2)}, u32[]{:S(2)}) %all-to-all-start.2) | async-done | bytes 81952 | tf_op jit(solution)/shard_map/all_to_all | solution.py:78
  100.9 0.6 broadcast_in_dim.11
  101.5 5.2 %all-to-all-start.3 = ((f32[8,2,640]{2,1,0:T(2,128)}), f32[8,2,640]{2,1,0:T(2,128)S(1)}, u32[]{:S(2)}, u32[]{:S(2)}) async-start(f32[8,2,640]{2,1,0:T(2,128)} %broadcast_in_dim.11), calls=%async_computation.3 | async-start | bytes 81920 | tf_op jit(solution)/shard_map/all_to_all | solution.py:86
  106.7 1.5 %fusion.48 = f32[256,1280]{1,0:T(8,128)} fusion(bf16[32,1,1280]{2,1,0:T(2,128)(2,1)S(1)} %copy-done.7, f32[32]{0:T(128)S(1)} %log_add_fusion.4, f32[256]{0:T(256)S(1)} %log_add_fusion, f32[256,32]{0,1:T(8,128)S(1)} %get-tuple-element.13, f32[32]{0:T(128)S(1)} %log_add_fusion.5, f32[256]{0:T(256)S(1)} %log_add_fusion.1), kind=kOutput, calls=%fused_computation.100 | convolution fusion | flops 21012480 | bytes 1427712 | tf_op jit(solution)/shard_map/dot_general | solution.py:156
  108.2 5.5 %all-to-all-done.3 = f32[8,2,640]{2,1,0:T(2,128)S(1)} async-done(((f32[8,2,640]{2,1,0:T(2,128)}), f32[8,2,640]{2,1,0:T(2,128)S(1)}, u32[]{:S(2)}, u32[]{:S(2)}) %all-to-all-start.3) | async-done | bytes 40992 | tf_op jit(solution)/shard_map/all_to_all | solution.py:86
  113.7 0.7 broadcast_in_dim.12
  114.4 5.6 %all-to-all-start.4 = ((bf16[32,2,640]{2,1,0:T(2,128)(2,1)}), bf16[32,2,640]{2,1,0:T(2,128)(2,1)S(1)}, u32[]{:S(2)}, u32[]{:S(2)}) async-start(bf16[32,2,640]{2,1,0:T(2,128)(2,1)} %broadcast_in_dim.12), calls=%async_computation.4 | async-start | bytes 163840 | tf_op jit(solution)/shard_map/all_to_all | solution.py:78
  120.0 2.5 %fusion.4 = bf16[1,256,1280]{2,1,0:T(8,128)(2,1)} fusion(f32[256,1280]{1,0:T(8,128)} %fusion.48, bf16[256,32]{0,1:T(8,128)(2,1)S(1)} %add_convert_fusion, bf16[1280,32]{0,1:T(8,128)(2,1)S(1)} %copy-done.8), kind=kOutput, calls=%fused_computation.14 | convolution fusion | flops 21626880 | bytes 2064384 | tf_op jit(solution)/shard_map/dot_general | solution.py:157
  122.5 4.6 %all-to-all-done.4 = bf16[32,2,640]{2,1,0:T(2,128)(2,1)S(1)} async-done(((bf16[32,2,640]{2,1,0:T(2,128)(2,1)}), bf16[32,2,640]{2,1,0:T(2,128)(2,1)S(1)}, u32[]{:S(2)}, u32[]{:S(2)}) %all-to-all-start.4) | async-done | bytes 81952 | tf_op jit(solution)/shard_map/all_to_all | solution.py:78
  127.2 0.7 copy.36
  (83 shorter events, 1.6 us)
Async XLA Ops:
  0.6 46.9 %copy-start = (bf16[1,640,1280]{2,1,0:T(8,128)(2,1)S(1)}, bf16[1,640,1280]{2,1,0:T(8,128)(2,1)}, u32[]{:S(2)}) copy-start(bf16[1,640,1280]{2,1,0:T(8,128)(2,1)} %param.8) | copy-start | bytes 4915204
  0.6 3.7 %copy-start.1 = (bf16[1,256,1280]{2,1,0:T(8,128)(2,1)S(1)}, bf16[1,256,1280]{2,1,0:T(8,128)(2,1)}, u32[]{:S(2)}) copy-start(bf16[1,256,1280]{2,1,0:T(8,128)(2,1)} %param.5) | copy-start | bytes 1966084
  0.7 4.0 %copy-start.3 = (bf16[1,256,1280]{2,1,0:T(8,128)(2,1)S(1)}, bf16[1,256,1280]{2,1,0:T(8,128)(2,1)}, u32[]{:S(2)}) copy-start(bf16[1,256,1280]{2,1,0:T(8,128)(2,1)} %param.9) | copy-start | bytes 1966084
  21.6 25.2 %copy-start.2 = (bf16[1,1280,640]{2,1,0:T(8,128)(2,1)S(1)}, bf16[1,1280,640]{2,1,0:T(8,128)(2,1)}, u32[]{:S(2)}) copy-start(bf16[1,1280,640]{2,1,0:T(8,128)(2,1)} %param.7) | copy-start | bytes 4915204
  21.6 12.5 %collective-permute-start.3 = (bf16[32,2560]{1,0:T(8,128)(2,1)S(1)}, bf16[32,2560]{1,0:T(8,128)(2,1)S(1)}, u32[]{:S(2)}, u32[]{:S(2)}) collective-permute-start(bf16[32,2560]{1,0:T(8,128)(2,1)S(1)} %get-tuple-element.24), channel_id=1, source_target_pairs={{0,192},{32,224},{64,0},{96,32},{128,64},{160,96},{192,128},{224,1... | collective-permute-start | bytes 491528 | tf_op jit(solution)/shard_map/ppermute | solution.py:47
  27.7 11.2 %collective-permute-start.2 = (bf16[32,2560]{1,0:T(8,128)(2,1)S(1)}, bf16[32,2560]{1,0:T(8,128)(2,1)S(1)}, u32[]{:S(2)}, u32[]{:S(2)}) collective-permute-start(bf16[32,2560]{1,0:T(8,128)(2,1)S(1)} %get-tuple-element.24), channel_id=1, source_target_pairs={{0,64},{32,96},{64,128},{96,160},{128,192},{160,224},{192,0},{224,... | collective-permute-start | bytes 491528 | tf_op jit(solution)/shard_map/ppermute | solution.py:47
  27.7 14.3 %collective-permute-start = (bf16[32,2560]{1,0:T(8,128)(2,1)S(1)}, bf16[32,2560]{1,0:T(8,128)(2,1)S(1)}, u32[]{:S(2)}, u32[]{:S(2)}) collective-permute-start(bf16[32,2560]{1,0:T(8,128)(2,1)S(1)} %get-tuple-element.24), channel_id=1, source_target_pairs={{0,32},{32,64},{64,96},{96,128},{128,160},{160,192},{192,224},{224... | collective-permute-start | bytes 491528 | tf_op jit(solution)/shard_map/ppermute | solution.py:47
  28.5 13.6 %collective-permute-start.1 = (bf16[32,2560]{1,0:T(8,128)(2,1)S(1)}, bf16[32,2560]{1,0:T(8,128)(2,1)S(1)}, u32[]{:S(2)}, u32[]{:S(2)}) collective-permute-start(bf16[32,2560]{1,0:T(8,128)(2,1)S(1)} %get-tuple-element.24), channel_id=1, source_target_pairs={{0,224},{32,0},{64,32},{96,64},{128,96},{160,128},{192,160},{224,1... | collective-permute-start | bytes 491528 | tf_op jit(solution)/shard_map/ppermute | solution.py:47
  34.1 12.6 %collective-permute-start.7 = (bf16[32,1280]{1,0:T(8,128)(2,1)S(1)}, bf16[32,1280]{1,0:T(8,128)(2,1)S(1)}, u32[]{:S(2)}, u32[]{:S(2)}) collective-permute-start(bf16[32,1280]{1,0:T(8,128)(2,1)S(1)} %slice.108), channel_id=1, source_target_pairs={{0,192},{32,224},{64,0},{96,32},{128,64},{160,96},{192,128},{224,1... | collective-permute-start | bytes 245768 | tf_op jit(solution)/shard_map/ppermute | solution.py:47
  38.9 7.8 %collective-permute-start.6 = (bf16[32,1280]{1,0:T(8,128)(2,1)S(1)}, bf16[32,1280]{1,0:T(8,128)(2,1)S(1)}, u32[]{:S(2)}, u32[]{:S(2)}) collective-permute-start(bf16[32,1280]{1,0:T(8,128)(2,1)S(1)} %slice.107), channel_id=1, source_target_pairs={{0,64},{32,96},{64,128},{96,160},{128,192},{160,224},{192,0},{224,... | collective-permute-start | bytes 245768 | tf_op jit(solution)/shard_map/ppermute | solution.py:47
  39.0 7.5 %collective-permute-start.4 = (bf16[32,2560]{1,0:T(8,128)(2,1)S(1)}, bf16[32,2560]{1,0:T(8,128)(2,1)S(1)}, u32[]{:S(2)}, u32[]{:S(2)}) collective-permute-start(bf16[32,2560]{1,0:T(8,128)(2,1)S(1)} %collective-permute-done.2), channel_id=1, source_target_pairs={{0,32},{32,64},{64,96},{96,128},{128,160},{160,192},{192,224},{224... | collective-permute-start | bytes 491528 | tf_op jit(solution)/shard_map/ppermute | solution.py:47
  42.0 4.7 %collective-permute-start.5 = (bf16[32,2560]{1,0:T(8,128)(2,1)S(1)}, bf16[32,2560]{1,0:T(8,128)(2,1)S(1)}, u32[]{:S(2)}, u32[]{:S(2)}) collective-permute-start(bf16[32,2560]{1,0:T(8,128)(2,1)S(1)} %collective-permute-done.3), channel_id=1, source_target_pairs={{0,224},{32,0},{64,32},{96,64},{128,96},{160,128},{192,160},{224,1... | collective-permute-start | bytes 491528 | tf_op jit(solution)/shard_map/ppermute | solution.py:47
  46.8 1.5 %copy-start.5 = (bf16[256,2560]{1,0:T(8,128)(2,1)}, bf16[256,2560]{1,0:T(8,128)(2,1)S(1)}, u32[]{:S(2)}) copy-start(bf16[256,2560]{1,0:T(8,128)(2,1)S(1)} %maximum_dynamic-update-slice_fusion) | copy-start | bytes 3932164
  47.5 0.8 copy-start.4
  50.1 6.6 %collective-permute-start.10 = (bf16[32,2560]{1,0:T(8,128)(2,1)S(1)}, bf16[32,2560]{1,0:T(8,128)(2,1)S(1)}, u32[]{:S(2)}, u32[]{:S(2)}) collective-permute-start(bf16[32,2560]{1,0:T(8,128)(2,1)S(1)} %get-tuple-element.18), channel_id=1, source_target_pairs={{0,224},{32,0},{64,32},{96,64},{128,96},{160,128},{192,160},{224,1... | collective-permute-start | bytes 491528 | tf_op jit(solution)/shard_map/ppermute | solution.py:47
  52.6 6.4 %collective-permute-start.13 = (bf16[32,2560]{1,0:T(8,128)(2,1)S(1)}, bf16[32,2560]{1,0:T(8,128)(2,1)S(1)}, u32[]{:S(2)}, u32[]{:S(2)}) collective-permute-start(bf16[32,2560]{1,0:T(8,128)(2,1)S(1)} %get-tuple-element.17), channel_id=1, source_target_pairs={{0,32},{32,64},{64,96},{96,128},{128,160},{160,192},{192,224},{224... | collective-permute-start | bytes 491528 | tf_op jit(solution)/shard_map/ppermute | solution.py:47
  52.6 6.9 %collective-permute-start.14 = (bf16[32,1280]{1,0:T(8,128)(2,1)S(1)}, bf16[32,1280]{1,0:T(8,128)(2,1)S(1)}, u32[]{:S(2)}, u32[]{:S(2)}) collective-permute-start(bf16[32,1280]{1,0:T(8,128)(2,1)S(1)} %slice.179), channel_id=1, source_target_pairs={{0,64},{32,96},{64,128},{96,160},{128,192},{160,224},{192,0},{224,... | collective-permute-start | bytes 245768 | tf_op jit(solution)/shard_map/ppermute | solution.py:47
  52.7 7.0 %collective-permute-start.11 = (bf16[32,1280]{1,0:T(8,128)(2,1)S(1)}, bf16[32,1280]{1,0:T(8,128)(2,1)S(1)}, u32[]{:S(2)}, u32[]{:S(2)}) collective-permute-start(bf16[32,1280]{1,0:T(8,128)(2,1)S(1)} %slice.182), channel_id=1, source_target_pairs={{0,192},{32,224},{64,0},{96,32},{128,64},{160,96},{192,128},{224,1... | collective-permute-start | bytes 245768 | tf_op jit(solution)/shard_map/ppermute | solution.py:47
  56.3 9.0 %collective-permute-start.9 = (bf16[32,2560]{1,0:T(8,128)(2,1)S(1)}, bf16[32,2560]{1,0:T(8,128)(2,1)S(1)}, u32[]{:S(2)}, u32[]{:S(2)}) collective-permute-start(bf16[32,2560]{1,0:T(8,128)(2,1)S(1)} %get-tuple-element.19), channel_id=1, source_target_pairs={{0,32},{32,64},{64,96},{96,128},{128,160},{160,192},{192,224},{224... | collective-permute-start | bytes 491528 | tf_op jit(solution)/shard_map/ppermute | solution.py:47
  56.7 8.6 %collective-permute-start.8 = (bf16[32,2560]{1,0:T(8,128)(2,1)S(1)}, bf16[32,2560]{1,0:T(8,128)(2,1)S(1)}, u32[]{:S(2)}, u32[]{:S(2)}) collective-permute-start(bf16[32,2560]{1,0:T(8,128)(2,1)S(1)} %get-tuple-element.16), channel_id=1, source_target_pairs={{0,224},{32,0},{64,32},{96,64},{128,96},{160,128},{192,160},{224,1... | collective-permute-start | bytes 491528 | tf_op jit(solution)/shard_map/ppermute | solution.py:47
  59.6 9.6 %collective-permute-start.15 = (bf16[32,2560]{1,0:T(8,128)(2,1)S(1)}, bf16[32,2560]{1,0:T(8,128)(2,1)S(1)}, u32[]{:S(2)}, u32[]{:S(2)}) collective-permute-start(bf16[32,2560]{1,0:T(8,128)(2,1)S(1)} %pad_maximum_fusion.4), channel_id=1, source_target_pairs={{0,64},{32,96},{64,128},{96,160},{128,192},{160,224},{192,0},{224,... | collective-permute-start | bytes 491528 | tf_op jit(solution)/shard_map/ppermute | solution.py:47
  59.8 9.4 %collective-permute-start.12 = (bf16[32,2560]{1,0:T(8,128)(2,1)S(1)}, bf16[32,2560]{1,0:T(8,128)(2,1)S(1)}, u32[]{:S(2)}, u32[]{:S(2)}) collective-permute-start(bf16[32,2560]{1,0:T(8,128)(2,1)S(1)} %pad_maximum_fusion.3), channel_id=1, source_target_pairs={{0,192},{32,224},{64,0},{96,32},{128,64},{160,96},{192,128},{224,1... | collective-permute-start | bytes 491528 | tf_op jit(solution)/shard_map/ppermute | solution.py:47
  70.2 16.4 %all-to-all-start.1 = ((bf16[32,2,1280]{2,1,0:T(2,128)(2,1)}), bf16[32,2,1280]{2,1,0:T(2,128)(2,1)S(1)}, u32[]{:S(2)}, u32[]{:S(2)}) async-start(bf16[32,2,1280]{2,1,0:T(2,128)(2,1)} %copy.27), calls=%async_computation.1 | async-start | bytes 327680 | tf_op jit(solution)/shard_map/all_to_all | solution.py:78
  86.8 1.7 %copy-start.6 = (bf16[32,1,1280]{2,1,0:T(2,128)(2,1)}, bf16[32,1,1280]{2,1,0:T(2,128)(2,1)S(1)}, u32[]{:S(2)}) copy-start(bf16[32,1,1280]{2,1,0:T(2,128)(2,1)S(1)} %get-tuple-element.21) | copy-start | bytes 245764
  89.5 11.3 %all-to-all-start.2 = ((bf16[32,2,640]{2,1,0:T(2,128)(2,1)}), bf16[32,2,640]{2,1,0:T(2,128)(2,1)S(1)}, u32[]{:S(2)}, u32[]{:S(2)}) async-start(bf16[32,2,640]{2,1,0:T(2,128)(2,1)} %reshape.158), calls=%async_computation.2 | async-start | bytes 163840 | tf_op jit(solution)/shard_map/all_to_all | solution.py:78
  93.6 13.1 %copy-start.7 = (bf16[32,1,1280]{2,1,0:T(2,128)(2,1)S(1)}, bf16[32,1,1280]{2,1,0:T(2,128)(2,1)}, u32[]{:S(2)}) copy-start(bf16[32,1,1280]{2,1,0:T(2,128)(2,1)} %copy-done.6) | copy-start | bytes 245764
  96.7 23.3 %copy-start.8 = (bf16[1280,32]{0,1:T(8,128)(2,1)S(1)}, bf16[1280,32]{0,1:T(8,128)(2,1)}, u32[]{:S(2)}) copy-start(bf16[1280,32]{0,1:T(8,128)(2,1)} %param.6) | copy-start | bytes 245764
  101.5 12.2 %all-to-all-start.3 = ((f32[8,2,640]{2,1,0:T(2,128)}), f32[8,2,640]{2,1,0:T(2,128)S(1)}, u32[]{:S(2)}, u32[]{:S(2)}) async-start(f32[8,2,640]{2,1,0:T(2,128)} %broadcast_in_dim.11), calls=%async_computation.3 | async-start | bytes 81920 | tf_op jit(solution)/shard_map/all_to_all | solution.py:86
  114.4 12.7 %all-to-all-start.4 = ((bf16[32,2,640]{2,1,0:T(2,128)(2,1)}), bf16[32,2,640]{2,1,0:T(2,128)(2,1)S(1)}, u32[]{:S(2)}, u32[]{:S(2)}) async-start(bf16[32,2,640]{2,1,0:T(2,128)(2,1)} %broadcast_in_dim.12), calls=%async_computation.4 | async-start | bytes 163840 | tf_op jit(solution)/shard_map/all_to_all | solution.py:78

commit v8 on v7

--- a/solution.py
+++ b/solution.py
@@ -20,14 +20,17 @@
     return (activated, derivative)
 
 
+def log_sum_exp(value, axis):
+    highest = jnp.max(value, axis=axis, keepdims=True)
+    return highest + jnp.log(jnp.sum(jnp.exp(value - highest), axis=axis, keepdims=True))
+
+
 def forward_iterates(router_scores):
     iterate = router_scores
     stored_residuals = []
     for sweep_index in range(ITERS):
-        line_divisor_factor = iterate - jax.nn.logsumexp(iterate, axis=1, keepdims=True)
-        column_divisor = line_divisor_factor - jax.nn.logsumexp(
-            line_divisor_factor, axis=0, keepdims=True
-        )
+        line_divisor_factor = iterate - log_sum_exp(iterate, 1)
+        column_divisor = line_divisor_factor - log_sum_exp(line_divisor_factor, 0)
         stored_residuals.append((line_divisor_factor, column_divisor))
         iterate = column_divisor
     return stored_residuals
@@ -98,9 +101,9 @@
     patches, image_grad = tokens[0], grad_out[0]
     model_width = patches.shape[1]
     router_scores = jnp.dot(patches, router, preferred_element_type=jnp.float32)
-    combine = jax.nn.softmax(router_scores, axis=1)
+    stored_residuals = forward_iterates(router_scores)
+    combine = jnp.exp(stored_residuals[0][0])
     combine_rounded = combine.astype(jnp.bfloat16)
-    stored_residuals = forward_iterates(router_scores)
     assignment_matrix = jnp.exp(stored_residuals[-1][1])
     dispatch_rounded = assignment_matrix.astype(jnp.bfloat16)
     slot_part = jnp.dot(dispatch_rounded.T, patches, preferred_element_type=jnp.float32).astype(

time: 128 us -> 129 us (level)
  no operation moved by 1% of the time
where the time goes in v8:
time: 129 us
  starting transfers between devices  50.4 us (39%)
  waiting for transfers between devices  36 us (28%)
  matrix products  17.2 us (13%)
  blocking collectives  16.2 us (13%)
  local copies, waits for them, and re-layouts  4.38 us (3%)
  other arithmetic  3.47 us (3%)
    ppermute x16, starting transfers between devices, shift(): lax.ppermute(value, 'dp', [(i, (i + step) % size) for i in range(size)])  26.8 us
    all_to_all x3, starting transfers between devices, swap(): lax.all_to_all(value, ('tok', 'expert'), split_axis=0, concat_axis=0, til...  18.4 us
    ppermute x16, waiting for transfers between devices, shift(): lax.ppermute(value, 'dp', [(i, (i + step) % size) for i in range(size)])  17 us
    all_to_all x1, blocking collectives, swap(): lax.all_to_all(value, ('tok', 'expert'), split_axis=0, concat_axis=0, til...  16.2 us
    all_to_all x3, waiting for transfers between devices, swap(): lax.all_to_all(value, ('tok', 'expert'), split_axis=0, concat_axis=0, til...  13.6 us
    all_to_all x1, waiting for transfers between devices, sum_everywhere(): seen = lax.all_to_all(copies, 'dp', split_axis=0, concat_axis=0, tiled=True)  5.46 us
    all_to_all x1, starting transfers between devices, sum_everywhere(): seen = lax.all_to_all(copies, 'dp', split_axis=0, concat_axis=0, tiled=True)  5.21 us
    dot_general x1, matrix products, body(): lax.dot_general(all_in, grad_pre, (((0,), (0,)), ((), ())), preferred_ele...  3 us
  transfers between devices with their start and end apart: 20, of which 11 were waited for; matrix products, arithmetic and copies ran while one was open for 8% of the time, Pallas kernels for 0%

profile of v8, /device:TPU:1, one launch (start us, length us, event | category | flops | bytes accessed | tf_op | source)
XLA Modules:
  0.0 128.8 jit_solution(14724918555640080114)
XLA Ops:
  0.7 1.6 %fusion.66 = (f32[256]{0:T(256)S(1)}, f32[256,32]{0,1:T(8,128)S(1)}) fusion(bf16[1280,32]{0,1:T(8,128)(2,1)} %param.6, bf16[1,256,1280]{2,1,0:T(8,128)(2,1)} %param.5), kind=kOutput, calls=%fused_computation.138 | convolution fusion | flops 20979456 | bytes 771072 | tf_op jit(solution)/shard_map/dot_general | solution.py:103
  2.3 0.1 subtract_reduce_fusion.3
  2.4 1.3 %fusion.6 = bf16[32,1,1280]{2,0,1:T(8,128)(2,1)S(1)} fusion(bf16[1,256,1280]{2,1,0:T(8,128)(2,1)} %param.9, f32[256,32]{0,1:T(8,128)S(1)} %get-tuple-element.27, f32[256]{0:T(256)S(1)} %log_add_fusion.3), kind=kOutput, calls=%fused_computation.19 | convolution fusion | flops 21028864 | bytes 771072 | tf_op jit(solution)/shard_map/dot_general | solution.py:112
  3.7 0.2 exponential_reduce_fusion.6
  4.0 0.1 exponential_reduce_fusion.5
  4.1 0.2 subtract_reduce_fusion.2
  4.3 0.2 exponential_reduce_fusion.4
  4.7 0.1 subtract_reduce_fusion.1
  4.8 0.2 exponential_reduce_fusion.2
  5.1 0.1 exponential_reduce_fusion.1
  5.2 0.2 subtract_reduce_fusion
  5.4 0.2 exponential_reduce_fusion
  5.6 0.3 fusion.5
  5.9 0.2 copy.24
  6.1 16.2 %all_to_all.25 = bf16[32,2,1280]{2,1,0:T(2,128)(2,1)S(1)} all-to-all(bf16[32,2,1280]{2,1,0:T(2,128)(2,1)S(1)} %copy.24), channel_id=1, replica_groups=mesh['dp'=8,'tok'=2,'expert'=16] {'tok','expert'}, dimensions={0} | all-to-all | bytes 327680 | tf_op jit(solution)/shard_map/all_to_all | solution.py:81
  22.3 0.2 fusion.65
  22.6 6.1 %collective-permute-start.3 = (bf16[32,2560]{1,0:T(8,128)(2,1)S(1)}, bf16[32,2560]{1,0:T(8,128)(2,1)S(1)}, u32[]{:S(2)}, u32[]{:S(2)}) collective-permute-start(bf16[32,2560]{1,0:T(8,128)(2,1)S(1)} %get-tuple-element.22), channel_id=1, source_target_pairs={{0,192},{32,224},{64,0},{96,32},{128,64},{160,96},{192,128},{224,1... | collective-permute-start | bytes 491528 | tf_op jit(solution)/shard_map/ppermute | solution.py:50
  28.7 0.7 collective-permute-start
  29.5 2.4 %collective-permute-start.1 = (bf16[32,2560]{1,0:T(8,128)(2,1)S(1)}, bf16[32,2560]{1,0:T(8,128)(2,1)S(1)}, u32[]{:S(2)}, u32[]{:S(2)}) collective-permute-start(bf16[32,2560]{1,0:T(8,128)(2,1)S(1)} %get-tuple-element.22), channel_id=1, source_target_pairs={{0,224},{32,0},{64,32},{96,64},{128,96},{160,128},{192,160},{224,1... | collective-permute-start | bytes 491528 | tf_op jit(solution)/shard_map/ppermute | solution.py:50
  31.9 3.3 %collective-permute-done.3 = bf16[32,2560]{1,0:T(8,128)(2,1)S(1)} collective-permute-done((bf16[32,2560]{1,0:T(8,128)(2,1)S(1)}, bf16[32,2560]{1,0:T(8,128)(2,1)S(1)}, u32[]{:S(2)}, u32[]{:S(2)}) %collective-permute-start.3) | collective-permute-done | bytes 163872 | tf_op jit(solution)/shard_map/ppermute | solution.py:50
  35.1 4.8 %collective-permute-start.7 = (bf16[32,1280]{1,0:T(8,128)(2,1)S(1)}, bf16[32,1280]{1,0:T(8,128)(2,1)S(1)}, u32[]{:S(2)}, u32[]{:S(2)}) collective-permute-start(bf16[32,1280]{1,0:T(8,128)(2,1)S(1)} %slice.108), channel_id=1, source_target_pairs={{0,192},{32,224},{64,0},{96,32},{128,64},{160,96},{192,128},{224,1... | collective-permute-start | bytes 245768 | tf_op jit(solution)/shard_map/ppermute | solution.py:50
  40.1 2.9 %collective-permute-done = bf16[32,2560]{1,0:T(8,128)(2,1)S(1)} collective-permute-done((bf16[32,2560]{1,0:T(8,128)(2,1)S(1)}, bf16[32,2560]{1,0:T(8,128)(2,1)S(1)}, u32[]{:S(2)}, u32[]{:S(2)}) %collective-permute-start) | collective-permute-done | bytes 163872 | tf_op jit(solution)/shard_map/ppermute | solution.py:50
  43.1 4.4 %collective-permute-done.4 = bf16[32,2560]{1,0:T(8,128)(2,1)S(1)} collective-permute-done((bf16[32,2560]{1,0:T(8,128)(2,1)S(1)}, bf16[32,2560]{1,0:T(8,128)(2,1)S(1)}, u32[]{:S(2)}, u32[]{:S(2)}) %collective-permute-start.4) | collective-permute-done | bytes 163872 | tf_op jit(solution)/shard_map/ppermute | solution.py:50
  47.6 0.2 collective-permute-done.5
  47.8 0.7 fusion.13
  48.5 0.8 fusion.9
  49.3 0.8 fusion.18
  50.1 0.7 fusion.11
  50.8 0.1 fusion.2
  51.0 2.5 %collective-permute-start.10 = (bf16[32,2560]{1,0:T(8,128)(2,1)S(1)}, bf16[32,2560]{1,0:T(8,128)(2,1)S(1)}, u32[]{:S(2)}, u32[]{:S(2)}) collective-permute-start(bf16[32,2560]{1,0:T(8,128)(2,1)S(1)} %get-tuple-element.16), channel_id=1, source_target_pairs={{0,224},{32,0},{64,32},{96,64},{128,96},{160,128},{192,160},{224,1... | collective-permute-start | bytes 491528 | tf_op jit(solution)/shard_map/ppermute | solution.py:50
  53.7 3.6 %collective-permute-start.11 = (bf16[32,1280]{1,0:T(8,128)(2,1)S(1)}, bf16[32,1280]{1,0:T(8,128)(2,1)S(1)}, u32[]{:S(2)}, u32[]{:S(2)}) collective-permute-start(bf16[32,1280]{1,0:T(8,128)(2,1)S(1)} %slice.182), channel_id=1, source_target_pairs={{0,192},{32,224},{64,0},{96,32},{128,64},{160,96},{192,128},{224,1... | collective-permute-start | bytes 245768 | tf_op jit(solution)/shard_map/ppermute | solution.py:50
  57.3 0.4 collective-permute-start.9
  57.6 2.3 %collective-permute-start.8 = (bf16[32,2560]{1,0:T(8,128)(2,1)S(1)}, bf16[32,2560]{1,0:T(8,128)(2,1)S(1)}, u32[]{:S(2)}, u32[]{:S(2)}) collective-permute-start(bf16[32,2560]{1,0:T(8,128)(2,1)S(1)} %get-tuple-element.14), channel_id=1, source_target_pairs={{0,224},{32,0},{64,32},{96,64},{128,96},{160,128},{192,160},{224,1... | collective-permute-start | bytes 491528 | tf_op jit(solution)/shard_map/ppermute | solution.py:50
  60.0 0.5 collective-permute-done.14
  60.8 3.6 %collective-permute-start.12 = (bf16[32,2560]{1,0:T(8,128)(2,1)S(1)}, bf16[32,2560]{1,0:T(8,128)(2,1)S(1)}, u32[]{:S(2)}, u32[]{:S(2)}) collective-permute-start(bf16[32,2560]{1,0:T(8,128)(2,1)S(1)} %pad_maximum_fusion.3), channel_id=1, source_target_pairs={{0,192},{32,224},{64,0},{96,32},{128,64},{160,96},{192,128},{224,1... | collective-permute-start | bytes 491528 | tf_op jit(solution)/shard_map/ppermute | solution.py:50
  64.4 1.9 %collective-permute-done.9 = bf16[32,2560]{1,0:T(8,128)(2,1)S(1)} collective-permute-done((bf16[32,2560]{1,0:T(8,128)(2,1)S(1)}, bf16[32,2560]{1,0:T(8,128)(2,1)S(1)}, u32[]{:S(2)}, u32[]{:S(2)}) %collective-permute-start.9) | collective-permute-done | bytes 163872 | tf_op jit(solution)/shard_map/ppermute | solution.py:50
  66.2 3.9 %collective-permute-done.15 = bf16[32,2560]{1,0:T(8,128)(2,1)S(1)} collective-permute-done((bf16[32,2560]{1,0:T(8,128)(2,1)S(1)}, bf16[32,2560]{1,0:T(8,128)(2,1)S(1)}, u32[]{:S(2)}, u32[]{:S(2)}) %collective-permute-start.15) | collective-permute-done | bytes 163872 | tf_op jit(solution)/shard_map/ppermute | solution.py:50
  70.1 0.1 fusion.41
  70.3 0.8 copy.27
  71.1 8.6 %all-to-all-start.1 = ((bf16[32,2,1280]{2,1,0:T(2,128)(2,1)}), bf16[32,2,1280]{2,1,0:T(2,128)(2,1)S(1)}, u32[]{:S(2)}, u32[]{:S(2)}) async-start(bf16[32,2,1280]{2,1,0:T(2,128)(2,1)} %copy.27), calls=%async_computation.1 | async-start | bytes 327680 | tf_op jit(solution)/shard_map/all_to_all | solution.py:81
  79.7 3.0 %fusion.1 = bf16[1,640,1280]{2,1,0:T(8,128)(2,1)} fusion(bf16[256,2560]{1,0:T(8,128)(2,1)} %copy-done.4, f32[256,640]{1,0:T(8,128)S(1)} %fusion.13), kind=kOutput, calls=%fused_computation.10 | convolution fusion | flops 421724160 | bytes 2949120 | tf_op jit(solution)/shard_map/dot_general | solution.py:137
  82.7 4.8 %all-to-all-done.1 = bf16[32,2,1280]{2,1,0:T(2,128)(2,1)S(1)} async-done(((bf16[32,2,1280]{2,1,0:T(2,128)(2,1)}), bf16[32,2,1280]{2,1,0:T(2,128)(2,1)S(1)}, u32[]{:S(2)}, u32[]{:S(2)}) %all-to-all-start.1) | async-done | bytes 163872 | tf_op jit(solution)/shard_map/all_to_all | solution.py:81
  87.5 0.2 fusion.64
  87.8 0.4 fusion.67
  88.2 0.1 fusion.57
  88.3 0.2 fusion.49
  88.5 0.1 fusion.61
  88.6 0.1 fusion.50
  88.9 0.2 fusion.51
  89.1 0.3 multiply_reduce_fusion
  89.5 0.2 convolution_convert_fusion.2
  89.8 0.7 reshape.100
  90.4 4.2 %all-to-all-start.2 = ((bf16[32,2,640]{2,1,0:T(2,128)(2,1)}), bf16[32,2,640]{2,1,0:T(2,128)(2,1)S(1)}, u32[]{:S(2)}, u32[]{:S(2)}) async-start(bf16[32,2,640]{2,1,0:T(2,128)(2,1)} %reshape.100), calls=%async_computation.2 | async-start | bytes 163840 | tf_op jit(solution)/shard_map/all_to_all | solution.py:81
  94.6 3.0 %fusion = bf16[1,1280,640]{2,1,0:T(8,128)(2,1)} fusion(bf16[256,640]{1,0:T(8,128)(2,1)S(1)} %fusion.18, bf16[256,2560]{1,0:T(8,128)(2,1)} %copy-done.4), kind=kOutput, calls=%fused_computation.9 | convolution fusion | flops 420249600 | bytes 2621440 | tf_op jit(solution)/shard_map/dot_general | solution.py:134
  97.6 4.1 %all-to-all-done.2 = bf16[32,2,640]{2,1,0:T(2,128)(2,1)S(1)} async-done(((bf16[32,2,640]{2,1,0:T(2,128)(2,1)}), bf16[32,2,640]{2,1,0:T(2,128)(2,1)S(1)}, u32[]{:S(2)}, u32[]{:S(2)}) %all-to-all-start.2) | async-done | bytes 81952 | tf_op jit(solution)/shard_map/all_to_all | solution.py:81
  101.9 0.6 broadcast_in_dim.11
  102.5 5.2 %all-to-all-start.3 = ((f32[8,2,640]{2,1,0:T(2,128)}), f32[8,2,640]{2,1,0:T(2,128)S(1)}, u32[]{:S(2)}, u32[]{:S(2)}) async-start(f32[8,2,640]{2,1,0:T(2,128)} %broadcast_in_dim.11), calls=%async_computation.3 | async-start | bytes 81920 | tf_op jit(solution)/shard_map/all_to_all | solution.py:89
  107.7 1.5 %fusion.48 = f32[256,1280]{1,0:T(8,128)} fusion(bf16[32,1,1280]{2,1,0:T(2,128)(2,1)S(1)} %copy-done.6, f32[32]{0:T(128)S(1)} %log_add_fusion.4, f32[256]{0:T(256)S(1)} %log_add_fusion, f32[256,32]{0,1:T(8,128)S(1)} %get-tuple-element.11, f32[32]{0:T(128)S(1)} %log_add_fusion.5, f32[256]{0:T(256)S(1)} %log_add_fusion.1), kind=kOutput, calls=%fused_computation.99 | convolution fusion | flops 21012480 | bytes 1427712 | tf_op jit(solution)/shard_map/dot_general | solution.py:159
  109.2 5.5 %all-to-all-done.3 = f32[8,2,640]{2,1,0:T(2,128)S(1)} async-done(((f32[8,2,640]{2,1,0:T(2,128)}), f32[8,2,640]{2,1,0:T(2,128)S(1)}, u32[]{:S(2)}, u32[]{:S(2)}) %all-to-all-start.3) | async-done | bytes 40992 | tf_op jit(solution)/shard_map/all_to_all | solution.py:89
  114.7 0.7 broadcast_in_dim.12
  115.4 5.6 %all-to-all-start.4 = ((bf16[32,2,640]{2,1,0:T(2,128)(2,1)}), bf16[32,2,640]{2,1,0:T(2,128)(2,1)S(1)}, u32[]{:S(2)}, u32[]{:S(2)}) async-start(bf16[32,2,640]{2,1,0:T(2,128)(2,1)} %broadcast_in_dim.12), calls=%async_computation.4 | async-start | bytes 163840 | tf_op jit(solution)/shard_map/all_to_all | solution.py:81
  121.0 2.5 %fusion.4 = bf16[1,256,1280]{2,1,0:T(8,128)(2,1)} fusion(f32[256,1280]{1,0:T(8,128)} %fusion.48, bf16[256,32]{0,1:T(8,128)(2,1)S(1)} %add_convert_fusion, bf16[1280,32]{0,1:T(8,128)(2,1)S(1)} %copy-done.7), kind=kOutput, calls=%fused_computation.14 | convolution fusion | flops 21626880 | bytes 2064384 | tf_op jit(solution)/shard_map/dot_general | solution.py:160
  123.5 4.6 %all-to-all-done.4 = bf16[32,2,640]{2,1,0:T(2,128)(2,1)S(1)} async-done(((bf16[32,2,640]{2,1,0:T(2,128)(2,1)}), bf16[32,2,640]{2,1,0:T(2,128)(2,1)S(1)}, u32[]{:S(2)}, u32[]{:S(2)}) %all-to-all-start.4) | async-done | bytes 81952 | tf_op jit(solution)/shard_map/all_to_all | solution.py:81
  128.1 0.7 copy.36
  (73 shorter events, 1.6 us)
Async XLA Ops:
  0.6 47.9 %copy-start = (bf16[1,640,1280]{2,1,0:T(8,128)(2,1)S(1)}, bf16[1,640,1280]{2,1,0:T(8,128)(2,1)}, u32[]{:S(2)}) copy-start(bf16[1,640,1280]{2,1,0:T(8,128)(2,1)} %param.8) | copy-start | bytes 4915204
  0.6 5.0 %copy-start.1 = (bf16[1,256,1280]{2,1,0:T(8,128)(2,1)S(1)}, bf16[1,256,1280]{2,1,0:T(8,128)(2,1)}, u32[]{:S(2)}) copy-start(bf16[1,256,1280]{2,1,0:T(8,128)(2,1)} %param.5) | copy-start | bytes 1966084
  22.6 25.2 %copy-start.2 = (bf16[1,1280,640]{2,1,0:T(8,128)(2,1)S(1)}, bf16[1,1280,640]{2,1,0:T(8,128)(2,1)}, u32[]{:S(2)}) copy-start(bf16[1,1280,640]{2,1,0:T(8,128)(2,1)} %param.7) | copy-start | bytes 4915204
  22.6 12.5 %collective-permute-start.3 = (bf16[32,2560]{1,0:T(8,128)(2,1)S(1)}, bf16[32,2560]{1,0:T(8,128)(2,1)S(1)}, u32[]{:S(2)}, u32[]{:S(2)}) collective-permute-start(bf16[32,2560]{1,0:T(8,128)(2,1)S(1)} %get-tuple-element.22), channel_id=1, source_target_pairs={{0,192},{32,224},{64,0},{96,32},{128,64},{160,96},{192,128},{224,1... | collective-permute-start | bytes 491528 | tf_op jit(solution)/shard_map/ppermute | solution.py:50
  28.7 11.2 %collective-permute-start.2 = (bf16[32,2560]{1,0:T(8,128)(2,1)S(1)}, bf16[32,2560]{1,0:T(8,128)(2,1)S(1)}, u32[]{:S(2)}, u32[]{:S(2)}) collective-permute-start(bf16[32,2560]{1,0:T(8,128)(2,1)S(1)} %get-tuple-element.22), channel_id=1, source_target_pairs={{0,64},{32,96},{64,128},{96,160},{128,192},{160,224},{192,0},{224,... | collective-permute-start | bytes 491528 | tf_op jit(solution)/shard_map/ppermute | solution.py:50
  28.7 14.3 %collective-permute-start = (bf16[32,2560]{1,0:T(8,128)(2,1)S(1)}, bf16[32,2560]{1,0:T(8,128)(2,1)S(1)}, u32[]{:S(2)}, u32[]{:S(2)}) collective-permute-start(bf16[32,2560]{1,0:T(8,128)(2,1)S(1)} %get-tuple-element.22), channel_id=1, source_target_pairs={{0,32},{32,64},{64,96},{96,128},{128,160},{160,192},{192,224},{224... | collective-permute-start | bytes 491528 | tf_op jit(solution)/shard_map/ppermute | solution.py:50
  29.5 13.6 %collective-permute-start.1 = (bf16[32,2560]{1,0:T(8,128)(2,1)S(1)}, bf16[32,2560]{1,0:T(8,128)(2,1)S(1)}, u32[]{:S(2)}, u32[]{:S(2)}) collective-permute-start(bf16[32,2560]{1,0:T(8,128)(2,1)S(1)} %get-tuple-element.22), channel_id=1, source_target_pairs={{0,224},{32,0},{64,32},{96,64},{128,96},{160,128},{192,160},{224,1... | collective-permute-start | bytes 491528 | tf_op jit(solution)/shard_map/ppermute | solution.py:50
  35.1 12.6 %collective-permute-start.7 = (bf16[32,1280]{1,0:T(8,128)(2,1)S(1)}, bf16[32,1280]{1,0:T(8,128)(2,1)S(1)}, u32[]{:S(2)}, u32[]{:S(2)}) collective-permute-start(bf16[32,1280]{1,0:T(8,128)(2,1)S(1)} %slice.108), channel_id=1, source_target_pairs={{0,192},{32,224},{64,0},{96,32},{128,64},{160,96},{192,128},{224,1... | collective-permute-start | bytes 245768 | tf_op jit(solution)/shard_map/ppermute | solution.py:50
  40.0 7.8 %collective-permute-start.6 = (bf16[32,1280]{1,0:T(8,128)(2,1)S(1)}, bf16[32,1280]{1,0:T(8,128)(2,1)S(1)}, u32[]{:S(2)}, u32[]{:S(2)}) collective-permute-start(bf16[32,1280]{1,0:T(8,128)(2,1)S(1)} %slice.107), channel_id=1, source_target_pairs={{0,64},{32,96},{64,128},{96,160},{128,192},{160,224},{192,0},{224,... | collective-permute-start | bytes 245768 | tf_op jit(solution)/shard_map/ppermute | solution.py:50
  40.0 7.5 %collective-permute-start.4 = (bf16[32,2560]{1,0:T(8,128)(2,1)S(1)}, bf16[32,2560]{1,0:T(8,128)(2,1)S(1)}, u32[]{:S(2)}, u32[]{:S(2)}) collective-permute-start(bf16[32,2560]{1,0:T(8,128)(2,1)S(1)} %collective-permute-done.2), channel_id=1, source_target_pairs={{0,32},{32,64},{64,96},{96,128},{128,160},{160,192},{192,224},{224... | collective-permute-start | bytes 491528 | tf_op jit(solution)/shard_map/ppermute | solution.py:50
  43.0 4.7 %collective-permute-start.5 = (bf16[32,2560]{1,0:T(8,128)(2,1)S(1)}, bf16[32,2560]{1,0:T(8,128)(2,1)S(1)}, u32[]{:S(2)}, u32[]{:S(2)}) collective-permute-start(bf16[32,2560]{1,0:T(8,128)(2,1)S(1)} %collective-permute-done.3), channel_id=1, source_target_pairs={{0,224},{32,0},{64,32},{96,64},{128,96},{160,128},{192,160},{224,1... | collective-permute-start | bytes 491528 | tf_op jit(solution)/shard_map/ppermute | solution.py:50
  47.8 1.5 %copy-start.4 = (bf16[256,2560]{1,0:T(8,128)(2,1)}, bf16[256,2560]{1,0:T(8,128)(2,1)S(1)}, u32[]{:S(2)}) copy-start(bf16[256,2560]{1,0:T(8,128)(2,1)S(1)} %maximum_dynamic-update-slice_fusion) | copy-start | bytes 3932164
  51.0 6.6 %collective-permute-start.10 = (bf16[32,2560]{1,0:T(8,128)(2,1)S(1)}, bf16[32,2560]{1,0:T(8,128)(2,1)S(1)}, u32[]{:S(2)}, u32[]{:S(2)}) collective-permute-start(bf16[32,2560]{1,0:T(8,128)(2,1)S(1)} %get-tuple-element.16), channel_id=1, source_target_pairs={{0,224},{32,0},{64,32},{96,64},{128,96},{160,128},{192,160},{224,1... | collective-permute-start | bytes 491528 | tf_op jit(solution)/shard_map/ppermute | solution.py:50
  53.6 6.4 %collective-permute-start.13 = (bf16[32,2560]{1,0:T(8,128)(2,1)S(1)}, bf16[32,2560]{1,0:T(8,128)(2,1)S(1)}, u32[]{:S(2)}, u32[]{:S(2)}) collective-permute-start(bf16[32,2560]{1,0:T(8,128)(2,1)S(1)} %get-tuple-element.15), channel_id=1, source_target_pairs={{0,32},{32,64},{64,96},{96,128},{128,160},{160,192},{192,224},{224... | collective-permute-start | bytes 491528 | tf_op jit(solution)/shard_map/ppermute | solution.py:50
  53.6 6.9 %collective-permute-start.14 = (bf16[32,1280]{1,0:T(8,128)(2,1)S(1)}, bf16[32,1280]{1,0:T(8,128)(2,1)S(1)}, u32[]{:S(2)}, u32[]{:S(2)}) collective-permute-start(bf16[32,1280]{1,0:T(8,128)(2,1)S(1)} %slice.179), channel_id=1, source_target_pairs={{0,64},{32,96},{64,128},{96,160},{128,192},{160,224},{192,0},{224,... | collective-permute-start | bytes 245768 | tf_op jit(solution)/shard_map/ppermute | solution.py:50
  53.7 7.0 %collective-permute-start.11 = (bf16[32,1280]{1,0:T(8,128)(2,1)S(1)}, bf16[32,1280]{1,0:T(8,128)(2,1)S(1)}, u32[]{:S(2)}, u32[]{:S(2)}) collective-permute-start(bf16[32,1280]{1,0:T(8,128)(2,1)S(1)} %slice.182), channel_id=1, source_target_pairs={{0,192},{32,224},{64,0},{96,32},{128,64},{160,96},{192,128},{224,1... | collective-permute-start | bytes 245768 | tf_op jit(solution)/shard_map/ppermute | solution.py:50
  57.3 9.0 %collective-permute-start.9 = (bf16[32,2560]{1,0:T(8,128)(2,1)S(1)}, bf16[32,2560]{1,0:T(8,128)(2,1)S(1)}, u32[]{:S(2)}, u32[]{:S(2)}) collective-permute-start(bf16[32,2560]{1,0:T(8,128)(2,1)S(1)} %get-tuple-element.17), channel_id=1, source_target_pairs={{0,32},{32,64},{64,96},{96,128},{128,160},{160,192},{192,224},{224... | collective-permute-start | bytes 491528 | tf_op jit(solution)/shard_map/ppermute | solution.py:50
  57.6 8.6 %collective-permute-start.8 = (bf16[32,2560]{1,0:T(8,128)(2,1)S(1)}, bf16[32,2560]{1,0:T(8,128)(2,1)S(1)}, u32[]{:S(2)}, u32[]{:S(2)}) collective-permute-start(bf16[32,2560]{1,0:T(8,128)(2,1)S(1)} %get-tuple-element.14), channel_id=1, source_target_pairs={{0,224},{32,0},{64,32},{96,64},{128,96},{160,128},{192,160},{224,1... | collective-permute-start | bytes 491528 | tf_op jit(solution)/shard_map/ppermute | solution.py:50
  60.6 9.6 %collective-permute-start.15 = (bf16[32,2560]{1,0:T(8,128)(2,1)S(1)}, bf16[32,2560]{1,0:T(8,128)(2,1)S(1)}, u32[]{:S(2)}, u32[]{:S(2)}) collective-permute-start(bf16[32,2560]{1,0:T(8,128)(2,1)S(1)} %pad_maximum_fusion.4), channel_id=1, source_target_pairs={{0,64},{32,96},{64,128},{96,160},{128,192},{160,224},{192,0},{224,... | collective-permute-start | bytes 491528 | tf_op jit(solution)/shard_map/ppermute | solution.py:50
  60.8 9.4 %collective-permute-start.12 = (bf16[32,2560]{1,0:T(8,128)(2,1)S(1)}, bf16[32,2560]{1,0:T(8,128)(2,1)S(1)}, u32[]{:S(2)}, u32[]{:S(2)}) collective-permute-start(bf16[32,2560]{1,0:T(8,128)(2,1)S(1)} %pad_maximum_fusion.3), channel_id=1, source_target_pairs={{0,192},{32,224},{64,0},{96,32},{128,64},{160,96},{192,128},{224,1... | collective-permute-start | bytes 491528 | tf_op jit(solution)/shard_map/ppermute | solution.py:50
  71.1 16.4 %all-to-all-start.1 = ((bf16[32,2,1280]{2,1,0:T(2,128)(2,1)}), bf16[32,2,1280]{2,1,0:T(2,128)(2,1)S(1)}, u32[]{:S(2)}, u32[]{:S(2)}) async-start(bf16[32,2,1280]{2,1,0:T(2,128)(2,1)} %copy.27), calls=%async_computation.1 | async-start | bytes 327680 | tf_op jit(solution)/shard_map/all_to_all | solution.py:81
  82.7 6.3 %copy-start.3 = (bf16[1,256,1280]{2,1,0:T(8,128)(2,1)S(1)}, bf16[1,256,1280]{2,1,0:T(8,128)(2,1)}, u32[]{:S(2)}) copy-start(bf16[1,256,1280]{2,1,0:T(8,128)(2,1)} %param.9) | copy-start | bytes 1966084
  87.8 1.7 %copy-start.5 = (bf16[32,1,1280]{2,1,0:T(2,128)(2,1)}, bf16[32,1,1280]{2,1,0:T(2,128)(2,1)S(1)}, u32[]{:S(2)}) copy-start(bf16[32,1,1280]{2,1,0:T(2,128)(2,1)S(1)} %get-tuple-element.19) | copy-start | bytes 245764
  90.4 11.3 %all-to-all-start.2 = ((bf16[32,2,640]{2,1,0:T(2,128)(2,1)}), bf16[32,2,640]{2,1,0:T(2,128)(2,1)S(1)}, u32[]{:S(2)}, u32[]{:S(2)}) async-start(bf16[32,2,640]{2,1,0:T(2,128)(2,1)} %reshape.100), calls=%async_computation.2 | async-start | bytes 163840 | tf_op jit(solution)/shard_map/all_to_all | solution.py:81
  94.6 13.1 %copy-start.6 = (bf16[32,1,1280]{2,1,0:T(2,128)(2,1)S(1)}, bf16[32,1,1280]{2,1,0:T(2,128)(2,1)}, u32[]{:S(2)}) copy-start(bf16[32,1,1280]{2,1,0:T(2,128)(2,1)} %copy-done.5) | copy-start | bytes 245764
  97.6 23.3 %copy-start.7 = (bf16[1280,32]{0,1:T(8,128)(2,1)S(1)}, bf16[1280,32]{0,1:T(8,128)(2,1)}, u32[]{:S(2)}) copy-start(bf16[1280,32]{0,1:T(8,128)(2,1)} %param.6) | copy-start | bytes 245764
  102.5 12.2 %all-to-all-start.3 = ((f32[8,2,640]{2,1,0:T(2,128)}), f32[8,2,640]{2,1,0:T(2,128)S(1)}, u32[]{:S(2)}, u32[]{:S(2)}) async-start(f32[8,2,640]{2,1,0:T(2,128)} %broadcast_in_dim.11), calls=%async_computation.3 | async-start | bytes 81920 | tf_op jit(solution)/shard_map/all_to_all | solution.py:89
  115.4 12.7 %all-to-all-start.4 = ((bf16[32,2,640]{2,1,0:T(2,128)(2,1)}), bf16[32,2,640]{2,1,0:T(2,128)(2,1)S(1)}, u32[]{:S(2)}, u32[]{:S(2)}) async-start(bf16[32,2,640]{2,1,0:T(2,128)(2,1)} %broadcast_in_dim.12), calls=%async_computation.4 | async-start | bytes 163840 | tf_op jit(solution)/shard_map/all_to_all | solution.py:81
